TPU v7x, 32 devices: a whole 2x2x4 slice. The times are simulated.
32 devices in a mesh: leaf: 2 (over x), rows: 16 (over z, y, core).
Axes of the slice: x: 2, y: 2, z: 4, core: 2. Of those that a mesh axis runs over, the one named last changes fastest.
Arguments:
- features: bfloat16 [262144, 256], P(('leaf', 'rows')), parts along dimension 0, may hold values from -80 to 80
- node_ids: int32 [262144], P(('leaf', 'rows')), parts along dimension 0, may hold values from -1 to 15, as said below
- labels: int32 [262144], P(('leaf', 'rows')), parts along dimension 0, may hold values from 0 to 15
- owners: int32 [32], P('leaf'), parts along dimension 0, may hold values from 0 to 15, each once
Outputs:
- hyperplanes: float32 [32, 16, 256], P(('leaf', 'rows')), parts along dimension 0
- scores: float32 [16, 262144], P(None, ('leaf', 'rows')), parts along dimension 1
There are 2 independent parts, one for each index of `leaf`. A program takes and returns all parts, laid end to end along the dimension named above; each array names one. Nothing has to cross between parts.
Inputs may be any that keep to these rules, and one draw needn't show every extreme that they name: `node_ids`: on rows device d, row p of node n's segment (local row n * 512 + p) holds n or -1; the live rows of a segment come first and there is at least one; some segment of every device is full. Each node number appears once in owners; node n is owned by the device of rows with index owners[n].
All inputs are finite; a program needn't handle non-finite values.
Results may differ from a plain program's by a relative error of at most 0.0035.
Values may be sent and summed in bfloat16 or wider, within the bound.
No kernel may reach another device: no remote copies, remote signals or barrier semaphores. Data moves between devices by JAX's collectives and lax.ppermute only.
A program may use at most 128 MiB of HBM per device.

v0:
```python
import jax
import jax.numpy as jnp
from jax import lax
from jax.sharding import PartitionSpec as P

CLASSES = 16


ridge_term = 0.1


def solve_nodes(scatter, sums, counts):
    totals = jnp.sum(counts, axis=1)
    centers = jnp.sum(sums, axis=1) / totals[:, None]
    scaled = sums / jnp.maximum(counts, 1.0)[:, :, None]
    within = scatter - jnp.einsum("ncf,ncg->nfg", scaled, sums, precision=lax.Precision.HIGHEST)
    identity = jnp.eye(scatter.shape[-1], dtype=jnp.float32)
    system = within / totals[:, None, None] + ridge_term * identity
    shifts = (sums - counts[:, :, None] * centers[:, None, :]) / totals[:, None, None]
    factor = jnp.linalg.cholesky(system)
    planes = jax.vmap(lambda lower, right: jax.scipy.linalg.cho_solve((lower, True), right.T).T)(
        factor, shifts
    )
    offsets = -jnp.einsum("ncf,nf->nc", planes, centers, precision=lax.Precision.HIGHEST)
    return (planes, offsets)


def on_device(features, node_ids, labels, owners):
    row_count, feature_count = features.shape
    node_count = owners.shape[0]
    segment = row_count // node_count
    inverse = (
        jnp.zeros((node_count,), jnp.int32).at[owners].set(jnp.arange(node_count, dtype=jnp.int32))
    )
    blocks = jnp.take(features.reshape(node_count, segment, feature_count), inverse, axis=0)
    slot_ids = jnp.take(node_ids.reshape(node_count, segment), inverse, axis=0)
    marks = jnp.take(labels.reshape(node_count, segment), inverse, axis=0)
    live_rows = slot_ids == inverse[:, None]
    masked = jnp.where(live_rows[:, :, None], blocks, jnp.zeros((), jnp.bfloat16))
    classes = jnp.arange(CLASSES, dtype=jnp.int32)
    tagged = jnp.where(live_rows, marks, -1).astype(jnp.bfloat16)
    arrived, arrived_tags = (
        lax.all_to_all(masked, "rows", split_axis=0, concat_axis=1, tiled=True),
        lax.all_to_all(tagged, "rows", split_axis=0, concat_axis=1, tiled=True),
    )
    owner_tags = arrived_tags.astype(jnp.int32)
    owner_hot = (owner_tags[:, None, :] == classes[None, :, None]).astype(jnp.bfloat16)
    mine_sums = jnp.einsum("ncs,nsf->ncf", owner_hot, arrived, preferred_element_type=jnp.float32)
    mine_counts = jnp.sum(owner_hot.astype(jnp.float32), axis=2)
    scatter = jnp.einsum("nsf,nsg->nfg", arrived, arrived, preferred_element_type=jnp.float32)
    planes, offsets = solve_nodes(scatter, mine_sums, mine_counts)
    every_planes, every_offsets = (
        lax.all_gather(planes, "rows", axis=0, tiled=True),
        lax.all_gather(offsets, "rows", axis=0, tiled=True),
    )
    rounded = every_planes.astype(jnp.bfloat16)
    result = jnp.einsum("ncf,nsf->cns", rounded, blocks, preferred_element_type=jnp.float32)
    result = result + every_offsets.T[:, :, None]
    result = jnp.where(live_rows[None], result, 0.0)
    result = jnp.take(result, owners, axis=1).reshape(CLASSES, row_count)
    return (planes, result)


def solution(mesh):
    in_specs = (P(("leaf", "rows"), None), P(("leaf", "rows")), P(("leaf", "rows")), P("leaf"))
    out_specs = (P(("leaf", "rows"), None, None), P(None, ("leaf", "rows")))
    return jax.shard_map(
        on_device, mesh=mesh, in_specs=in_specs, out_specs=out_specs, check_vma=False
    )
```

profile of v0, /device:TPU:0, one launch (start us, length us, event | category | flops | bytes accessed | tf_op | source)
XLA Modules:
  0.0 252.3 jit_solution(4196847479306877663)
XLA Ops:
  0.6 0.7 compare_select_fusion.1
  1.3 0.6 scatter_custom_fusion
  1.9 0.7 compare_and_fusion
  2.6 0.8 reshape.307
  3.4 0.8 reshape.309
  4.1 0.6 gather_fusion.2
  4.7 0.6 gather_fusion.3
  5.3 0.1 fusion.22
  5.4 0.5 broadcast.305
  5.9 0.7 reduce.23
  6.6 0.6 reshape.402
  7.2 7.4 %all-to-all-start.1 = ((bf16[16,2,256]{2,1,0:T(2,128)(2,1)}), bf16[16,2,256]{2,1,0:T(2,128)(2,1)S(1)}, u32[]{:S(2)}, u32[]{:S(2)}) async-start(bf16[16,2,256]{2,1,0:T(2,128)(2,1)} %reshape.402), calls=%async_computation.1 | async-start | bytes 32768 | tf_op jit(solution)/shard_map/all_to_all | solution.py:44
  14.6 4.9 %gather_fusion = bf16[16,512,256]{2,1,0:T(8,128)(2,1)} fusion(bf16[16,512,256]{2,1,0:T(8,128)(2,1)} %bitcast.110, s32[1024]{0:T(1024)S(1)} %pad_clamp_fusion.1), kind=kCustom, calls=%fused_computation.2 | custom fusion | bytes 8388672 | tf_op jit(solution)/shard_map/jit(_take)/gather | solution.py:35
  19.5 5.3 %broadcast_select_fusion.1 = bf16[16,512,256]{2,1,0:T(8,128)(2,1)} fusion(pred[16,512]{1,0:T(8,128)(4,1)S(1)} %get-tuple-element.24, bf16[16,512,256]{2,1,0:T(8,128)(2,1)} %gather_fusion, pred[16]{0:T(512)(128)(4,1)S(1)} %get-tuple-element.35), kind=kLoop, calls=%fused_computation.8 | loop fusion | flops 4194304 | bytes 8396816 | tf_op jit(solution)/shard_map/jit(_where)/select_n | solution.py:39
  24.8 0.0 copy-start
  24.8 0.0 all-to-all-done.1
  24.8 6.2 %all-to-all-start = ((bf16[16,512,256]{2,1,0:T(8,128)(2,1)}), bf16[16,512,256]{2,1,0:T(8,128)(2,1)}, u32[]{:S(2)}, u32[]{:S(2)}) async-start(bf16[16,512,256]{2,1,0:T(8,128)(2,1)} %broadcast_select_fusion.1), calls=%async_computation | async-start | bytes 8388608 | tf_op jit(solution)/shard_map/all_to_all | solution.py:43
  31.0 0.1 broadcast_bitcast_fusion
  31.1 0.0 copy-done
  31.1 0.6 dynamic-slice.4
  32.4 0.8 convert_reduce_fusion.1
  33.2 75.4 %all-to-all-done = bf16[16,512,256]{2,1,0:T(8,128)(2,1)} async-done(((bf16[16,512,256]{2,1,0:T(8,128)(2,1)}), bf16[16,512,256]{2,1,0:T(8,128)(2,1)}, u32[]{:S(2)}, u32[]{:S(2)}) %all-to-all-start) | async-done | bytes 4194336 | tf_op jit(solution)/shard_map/all_to_all | solution.py:43
  108.6 2.9 %fusion.33 = (f32[256]{0:T(256)S(1)}, f32[16,256]{1,0:T(8,128)S(1)}) fusion(bf16[8192,256]{1,0:T(8,128)(2,1)} %bitcast.4, s32[8192]{0:T(1024)S(1)} %bitcast.115), kind=kOutput, calls=%fused_computation.85 | convolution fusion | flops 67243776 | bytes 4244480 | tf_op jit(solution)/shard_map/ncs,nsf->ncf/dot_general | solution.py:48
  111.5 0.7 broadcast_divide_fusion
  112.2 0.7 divide_bitcast_fusion
  112.9 5.2 %convolution_bitcast_fusion = f32[256,256]{0,1:T(8,128)S(1)} fusion(bf16[16,512,256]{2,1,0:T(8,128)(2,1)} %all-to-all-done), kind=kOutput, calls=%fused_computation.16 | convolution fusion | flops 1073741824 | bytes 4456448 | tf_op jit(solution)/shard_map/nsf,nsg->nfg/dot_general | solution.py:50
  118.1 1.1 fusion.5
  119.2 0.1 copy.25
  119.4 11.7 %custom-call.20 = f32[1,128,128]{2,1,0:T(8,128)S(1)} custom-call(f32[1,128,128]{2,1,0:T(8,128)S(1)} %cholesky.117), custom_call_target="Cholesky" | custom-call | tf_op jit(solution)/shard_map/jit(cholesky)/cholesky | solution.py:20
  131.1 9.8 %custom-call.21 = f32[1,1,128,128]{2,3,1,0:T(8,128)S(1)} custom-call(f32[1,1,128,128]{3,2,1,0:T(8,128)S(1)} %get-tuple-element.30), custom_call_target="InvertDiagBlocksLowerTriangular" | custom-call | tf_op jit(solution)/shard_map/jit(cholesky)/cholesky | solution.py:20
  141.0 0.2 bitcast_dynamic-update-slice_fusion.1
  141.2 0.3 fusion.6
  141.4 11.9 %custom-call.22 = f32[1,128,128]{2,1,0:T(8,128)S(1)} custom-call(f32[1,128,128]{2,1,0:T(8,128)S(1)} %fusion.6), custom_call_target="Cholesky" | custom-call | tf_op jit(solution)/shard_map/jit(cholesky)/cholesky | solution.py:20
  153.4 0.6 compare_reduce_fusion
  154.0 0.6 compare_reduce_fusion.1
  156.0 0.1 triangular_solve.71
  156.0 3.9 %while.1 = (s32[]{:T(128)}, f32[1,256,256]{2,1,0:T(8,128)S(1)}, s32[2,2]{1,0:T(2,128)S(1)}, f32[2,1,128,128]{3,2,1,0:T(8,128)S(1)}, s32[]{:T(128)}) while((s32[]{:T(128)}, f32[1,256,256]{2,1,0:T(8,128)S(1)}, s32[2,2]{1,0:T(2,128)S(1)}, f32[2,1,128,128]{3,2,1,0:T(8,128)S(1)}, s32[]{:T(128)}) %tuple.32), condition=%wide.while_cond, body=%wide.while_body.sunk | while | flops 2 | bytes 131181 | solution.py:21
  156.0 0.6 fusion.48
  156.6 1.4 bitcast_dynamic-update-slice_fusion.3
  158.0 0.6 fusion.48
  158.6 1.4 bitcast_dynamic-update-slice_fusion.3
  160.0 19.7 %custom-call.23 = f32[1,2,128,128]{2,3,1,0:T(8,128)S(1)} custom-call(f32[1,2,128,128]{3,2,1,0:T(8,128)S(1)} %bitcast.121), custom_call_target="InvertDiagBlocksLowerTriangular" | custom-call | tf_op jit(solution)/shard_map/vmap(jit(_cho_solve))/triangular_solve | solution.py:21
  179.6 0.2 fusion.17
  179.8 0.2 fusion.8
  180.0 0.2 fusion.19
  180.2 0.2 fusion.18
  180.4 0.2 convolution_subtract_fusion.1
  180.6 0.2 convolution_bitcast_fusion.2
  180.8 0.7 fusion.30
  181.4 35.7 %all_gather.6 = bf16[16,16,256]{2,1,0:T(8,128)(2,1)S(1)} all-gather(bf16[1,16,256]{2,1,0:T(8,128)(2,1)S(1)} %get-tuple-element.21), channel_id=1, replica_groups=mesh['leaf'=2,'rows'=16] {'rows'}, dimensions={0}, use_global_device_ids=true | all-gather | bytes 139264 | tf_op jit(solution)/shard_map/all_gather | solution.py:53
  217.1 0.1 fusion.9
  217.3 0.2 dynamic-update-slice.11
  217.5 29.8 %all-reduce.1 = f32[256]{0:T(256)S(1)} all-reduce(f32[256]{0:T(256)S(1)} %dynamic-update-slice.11), channel_id=2, replica_groups=mesh['leaf'=2,'rows'=16] {'rows'}, use_global_device_ids=true, to_apply=%add.1 | all-reduce | flops 256 | bytes 2048
  247.3 0.1 reshape.382
  247.4 3.4 %fusion.3 = f32[16,16,512]{2,0,1:T(8,128)S(1)} fusion(bf16[16,512,256]{2,1,0:T(8,128)(2,1)} %gather_fusion, pred[16]{0:T(512)(128)(4,1)S(1)} %get-tuple-element.35, f32[16,16]{0,1:T(8,128)S(1)} %bitcast.120, pred[16,512]{1,0:T(8,128)(4,1)S(1)} %get-tuple-element.24, bf16[16,16,256]{2,1,0:T(8,128)(2,1)S(1)} %all_gather.6), kind=kOutput, calls=%fused_computation.12 | convolution fusion | flops 69468160 | bytes 4858896 | tf_op jit(solution)/shard_map/ncf,nsf->cns/dot_general | solution.py:57
  250.8 0.6 gather_fusion.1
  251.5 0.8 broadcast_select_fusion.9
  (20 shorter events, 0.3 us)
Async XLA Ops:
  7.2 17.6 %all-to-all-start.1 = ((bf16[16,2,256]{2,1,0:T(2,128)(2,1)}), bf16[16,2,256]{2,1,0:T(2,128)(2,1)S(1)}, u32[]{:S(2)}, u32[]{:S(2)}) async-start(bf16[16,2,256]{2,1,0:T(2,128)(2,1)} %reshape.402), calls=%async_computation.1 | async-start | bytes 32768 | tf_op jit(solution)/shard_map/all_to_all | solution.py:44
  24.8 6.3 %copy-start = (u32[32]{0:T(128)S(1)}, u32[32]{0:T(128)}, u32[]{:S(2)}) copy-start(u32[32]{0:T(128)} %constant.166) | copy-start | bytes 388
  24.8 83.9 %all-to-all-start = ((bf16[16,512,256]{2,1,0:T(8,128)(2,1)}), bf16[16,512,256]{2,1,0:T(8,128)(2,1)}, u32[]{:S(2)}, u32[]{:S(2)}) async-start(bf16[16,512,256]{2,1,0:T(8,128)(2,1)} %broadcast_select_fusion.1), calls=%async_computation | async-start | bytes 8388608 | tf_op jit(solution)/shard_map/all_to_all | solution.py:43
where the time goes:
time: 253 us; the launch traced here: 252 us
  waiting for transfers between devices  75.4 us (30%)
  other arithmetic  65.5 us (26%)
  blocking collectives  65.5 us (26%)
  local copies, waits for them, and re-layouts  15.1 us (6%)
  matrix products  14.3 us (6%)
  starting transfers between devices  13.6 us (5%)
  between operations  2.8 us (1%)
    all_to_all x1, waiting for transfers between devices, on_device(): lax.all_to_all(masked, 'rows', split_axis=0, concat_axis=1, tiled=True)  75.4 us
    all_gather x1, blocking collectives, on_device(): lax.all_gather(planes, 'rows', axis=0, tiled=True)  35.7 us
    another operation x7, other arithmetic, solve_nodes(): factor = jnp.linalg.cholesky(system)  34.8 us
    unnamed x1, blocking collectives  29.8 us
    another operation x3, other arithmetic, solve_nodes(): jax.scipy.linalg.cho_solve((lower, True), right.T)  19.7 us
    all_to_all x1, starting transfers between devices, on_device(): lax.all_to_all(tagged, 'rows', split_axis=0, concat_axis=1, tiled=True)  7.39 us
    all_to_all x1, starting transfers between devices, on_device(): lax.all_to_all(masked, 'rows', split_axis=0, concat_axis=1, tiled=True)  6.19 us
    select_n x1, other arithmetic, on_device(): jnp.where(live_rows[:, :, None], blocks, jnp.zeros((), jnp.bfloat16))  5.27 us
  transfers between devices with their start and end apart: 2, of which 1 were waited for; matrix products, arithmetic and copies ran while one was open for 5% of the time, Pallas kernels for 0%

commit v1 on v0

v1 whole, which is shorter than its diff:
```python
import functools

import jax
import jax.numpy as jnp
from jax import lax
from jax.experimental import pallas as pl
from jax.experimental.pallas import tpu as pltpu
from jax.sharding import PartitionSpec as P

CLASSES = 16
RIDGE = 0.1
PANEL = 16
LANES = 128
HIGH = lax.Precision.HIGHEST


def split(x):
    hi = x.astype(jnp.bfloat16)
    rest = x - hi.astype(jnp.float32)
    mid = rest.astype(jnp.bfloat16)
    low = (rest - mid.astype(jnp.float32)).astype(jnp.bfloat16)
    return hi, mid, low


def over_rows(a, b):
    return lax.dot_general(a, b, (((0,), (0,)), ((), ())), preferred_element_type=jnp.float32)


def wide_over_rows(a, b):
    a1, a2, a3 = split(a)
    b1, b2, b3 = split(b)
    return over_rows(
        jnp.concatenate([a1, a1, a2, a2, a1, a3], axis=0), jnp.concatenate([b1, b2, b1, b2, b3, b1], axis=0)
    )


def reverse(number, bits):
    return sum((((number >> b) & 1) << (bits - 1 - b)) for b in range(bits))


def sums_kernel(bits, owners, features, node_ids, labels, kept, sent):
    node = pl.program_id(0)
    segment, size = features.shape
    half = size // 2
    here = pl.ds(pl.multiple_of(node * segment, segment), segment)
    alive = node_ids[here].reshape(1, segment) == node
    marks = labels[here].reshape(1, segment)
    classes = lax.broadcasted_iota(jnp.int32, (CLASSES, segment), 0)
    hot = jnp.where((marks == classes) & alive, 1.0, 0.0)
    length = jnp.sum(jnp.where(alive, 1.0, 0.0), axis=1, keepdims=True).astype(jnp.int32)
    rows = lax.broadcasted_iota(jnp.int32, (segment, size), 0)
    masked = jnp.where(rows < length, features[...], jnp.zeros((), jnp.bfloat16))
    moment = over_rows(masked, masked)
    sums = jnp.dot(hot.astype(jnp.bfloat16), masked, preferred_element_type=jnp.float32)
    counts = jnp.sum(hot, axis=1, keepdims=True)
    ci = lax.broadcasted_iota(jnp.int32, (CLASSES, half), 0)
    cj = lax.broadcasted_iota(jnp.int32, (CLASSES, half), 1)
    count_row = jnp.sum(jnp.where(ci == cj, counts, 0.0), axis=0, keepdims=True)
    i = lax.broadcasted_iota(jnp.int32, (half, half), 0)
    j = lax.broadcasted_iota(jnp.int32, (half, half), 1)
    last = moment[half:, half:]
    mixed = jnp.where(i <= j, moment[:half, :half], last)
    diagonal = jnp.sum(jnp.where(i == j, last, 0.0), axis=0, keepdims=True)
    ti = lax.broadcasted_iota(jnp.int32, (8, half), 0)
    tail = jnp.where(ti == 0, diagonal, jnp.where(ti == 1, count_row, 0.0))

    apart = owners[node] ^ lax.axis_index("rows")
    place = reverse(apart & -2, bits)

    def store(out):
        out[place, 0:half] = moment[:half, half:]
        out[place, half : 2 * half] = mixed
        out[place, 2 * half : 2 * half + CLASSES] = sums[:, :half]
        out[place, 2 * half + CLASSES : 2 * half + 2 * CLASSES] = sums[:, half:]
        out[place, 2 * half + 2 * CLASSES :] = tail

    @pl.when((apart & 1) == 0)
    def _():
        store(kept)

    @pl.when((apart & 1) == 1)
    def _():
        store(sent)


def local_sums(features, node_ids, labels, owners, bits):
    row_count, size = features.shape
    nodes = owners.shape[0]
    segment = row_count // nodes
    block = (nodes // 2, size + 2 * CLASSES + 8, size // 2)
    out = jax.ShapeDtypeStruct(block, jnp.float32)
    whole = pl.BlockSpec(block, lambda n, o: (0, 0, 0))
    return pl.pallas_call(
        functools.partial(sums_kernel, bits),
        out_shape=(out, out),
        grid_spec=pltpu.PrefetchScalarGridSpec(
            num_scalar_prefetch=1,
            grid=(nodes,),
            in_specs=[
                pl.BlockSpec((segment, size), lambda n, o: (n, 0)),
                pl.BlockSpec((row_count,), lambda n, o: (0,)),
                pl.BlockSpec((row_count,), lambda n, o: (0,)),
            ],
            out_specs=(whole, whole),
        ),
        compiler_params=pltpu.CompilerParams(vmem_limit_bytes=48 << 20),
        name="local_sums",
    )(owners, features, node_ids, labels)


def sweep(matrix, size):
    lanes=lax.broadcasted_iota(jnp.int32,(1,size),1)
    rows=lax.broadcasted_iota(jnp.int32,(PANEL,1),0)
    lane_id=lax.broadcasted_iota(jnp.int32,(PANEL,size),1)
    row_id=lax.broadcasted_iota(jnp.int32,(PANEL,size),0)
    panel=matrix[0:PANEL,:]
    for first in range(0,size,PANEL):
        last=first+PANEL
        inside=(lanes>=first)&(lanes<last)
        p1,p2,p3=split(panel)
        left=jnp.concatenate([p1,p1,p2,p2,p1,p3],axis=0)
        column=[jnp.broadcast_to(panel[:,first+c:first+c+1],(PANEL,128)) for c in range(PANEL)]
        work=jnp.where(inside,jnp.where(lane_id==row_id+first,-1.0,0.0),panel)
        scale=jnp.zeros((PANEL,128),jnp.float32)
        for k in range(PANEL):
            here=rows==k
            inverse=1.0/jnp.broadcast_to(column[k][k:k+1,:],(PANEL,128))
            factor=jnp.where(here,0.0,column[k]*inverse)
            scale=jnp.where(here,inverse,scale)
            for c in range(k+1,PANEL):
                column[c]=column[c]-factor*column[c][k:k+1,:]
            work=work-jnp.concatenate([factor]*(size//128),axis=1)*work[k:k+1,:]
        work=work*jnp.concatenate([scale]*(size//128),axis=1)
        w1,w2,w3=split(work)
        right=jnp.concatenate([w1,w2,w1,w2,w3,w1],axis=0)
        if last<size:
            base=last//128*128
            edge=over_rows(left[:,base:base+128],right)
            panel=jnp.where(inside,0.0,matrix[last:last+PANEL,:])-edge[last-base:last-base+PANEL,:]
        update=over_rows(left,right)
        matrix[...]=jnp.where(inside,0.0,matrix[...])-update
        matrix[first:last,:]=work
def solve_kernel(size, kept, came, planes, message, matrix):
    half=size//2
    total_block=kept[0]+came[0]
    cross=total_block[0:half]
    mixed=total_block[half:2*half]
    sums=jnp.concatenate([total_block[2*half:2*half+CLASSES],total_block[2*half+CLASSES:2*half+2*CLASSES]],axis=1)
    at=2*half+2*CLASSES
    diagonal=total_block[at:at+1]
    count_row=total_block[at+1:at+2]
    i=lax.broadcasted_iota(jnp.int32,(half,half),0); j=lax.broadcasted_iota(jnp.int32,(half,half),1)
    ci=lax.broadcasted_iota(jnp.int32,(CLASSES,half),0); cj=lax.broadcasted_iota(jnp.int32,(CLASSES,half),1)
    counts=jnp.sum(jnp.where(ci==cj,count_row,0.0),axis=1,keepdims=True)
    total=jnp.sum(counts,axis=0,keepdims=True)
    centers=jnp.sum(sums,axis=0,keepdims=True)/total
    scaled=sums/jnp.maximum(counts,1.0)
    shifts=(sums-counts*centers)/total
    between=wide_over_rows(sums,scaled)
    upper=jnp.where(i<j,mixed,0.0)
    lower=jnp.where(i>j,mixed,0.0)
    ridge=jnp.where(i==j,RIDGE,0.0)
    a11=upper+upper.T+jnp.where(i==j,mixed,0.0)
    a22=lower+lower.T+jnp.where(i==j,diagonal,0.0)
    matrix[0:half,0:half]=(a11-between[0:half,0:half])/total+ridge
    matrix[0:half,half:]=(cross-between[0:half,half:])/total
    matrix[half:,0:half]=(cross.T-between[half:,0:half])/total
    matrix[half:,half:]=(a22-between[half:,half:])/total+ridge
    sweep(matrix,size)
    result=-jnp.dot(shifts,matrix[...],precision=HIGH,preferred_element_type=jnp.float32)
    planes[0]=result
    offsets=-jnp.sum(result*centers,axis=1,keepdims=True)
    o1,o2,o3=split(offsets)
    message[0,:,0:size]=result.astype(jnp.bfloat16)
    lane=lax.broadcasted_iota(jnp.int32,(CLASSES,128),1)
    message[0,:,size:]=jnp.where(lane==0,o1.astype(jnp.float32),jnp.where(lane==1,o2.astype(jnp.float32),jnp.where(lane==2,o3.astype(jnp.float32),0.0))).astype(jnp.bfloat16)
def solve(kept,came,size):
    return pl.pallas_call(functools.partial(solve_kernel,size),
        out_shape=(jax.ShapeDtypeStruct((1,CLASSES,size),jnp.float32),jax.ShapeDtypeStruct((1,CLASSES,size+128),jnp.bfloat16)),
        scratch_shapes=[pltpu.VMEM((size,size),jnp.float32)],
        compiler_params=pltpu.CompilerParams(vmem_limit_bytes=32<<20),
        name="solve")(kept,came)


def scores_kernel(bits, owners, features, node_ids, messages, scores):
    node = pl.program_id(0)
    segment, size = features.shape
    here = pl.ds(pl.multiple_of(node * segment, segment), segment)
    alive = node_ids[here].reshape(1, segment) == node
    message = messages[reverse(owners[node] ^ lax.axis_index("rows"), bits)]
    offsets = jnp.sum(message[:, size:].astype(jnp.float32), axis=1, keepdims=True)
    result = lax.dot_general(
        message[:, :size], features[...], (((1,), (1,)), ((), ())), preferred_element_type=jnp.float32
    )
    scores[...] = jnp.where(alive, result + offsets, 0.0)


def all_scores(features, node_ids, owners, messages, bits):
    row_count, size = features.shape
    nodes = owners.shape[0]
    segment = row_count // nodes
    return pl.pallas_call(
        functools.partial(scores_kernel, bits),
        out_shape=jax.ShapeDtypeStruct((CLASSES, row_count), jnp.float32),
        grid_spec=pltpu.PrefetchScalarGridSpec(
            num_scalar_prefetch=1,
            grid=(nodes,),
            in_specs=[
                pl.BlockSpec((segment, size), lambda n, o: (n, 0)),
                pl.BlockSpec((row_count,), lambda n, o: (0,)),
                pl.BlockSpec(messages.shape, lambda n, o: (0, 0, 0)),
            ],
            out_specs=pl.BlockSpec((CLASSES, segment), lambda n, o: (0, n)),
        ),
        compiler_params=pltpu.CompilerParams(vmem_limit_bytes=32 << 20),
        name="all_scores",
    )(owners, features, node_ids, messages)


def on_device(ranks, features, node_ids, labels, owners):
    size = features.shape[1]
    bits = ranks.bit_length() - 1

    def swap(x, distance):
        return lax.ppermute(x, "rows", [(r, r ^ distance) for r in range(ranks)])

    kept, sent = local_sums(features, node_ids, labels, owners, bits)
    came = swap(sent, 1)
    for b in range(1, bits):
        middle = kept.shape[0] // 2
        sent = kept[middle:] + came[middle:]
        next_came = swap(sent, 1 << b)
        kept = kept[:middle] + came[:middle]
        came = next_came
    planes, held = solve(kept, came, size)
    for b in reversed(range(bits)):
        held = jnp.concatenate([held, swap(held, 1 << b)], axis=0)
    return planes, all_scores(features, node_ids, owners, held, bits)


def solution(mesh):
    ranks = mesh.shape["rows"]
    in_specs = (P(("leaf", "rows"), None), P(("leaf", "rows")), P(("leaf", "rows")), P("leaf"))
    out_specs = (P(("leaf", "rows"), None, None), P(None, ("leaf", "rows")))
    return jax.shard_map(
        functools.partial(on_device, ranks), mesh=mesh, in_specs=in_specs, out_specs=out_specs, check_vma=False
    )
```

time: 253 us -> 82.6 us (0.33)
  blocking collectives: 65.5 us -> 0 us
  other arithmetic: 65.5 us -> 0.25 us
  waiting for transfers between devices: 75.4 us -> 41.6 us
  Pallas kernels: 0 us -> 27.5 us
  matrix products: 14.3 us -> 0 us
  local copies, waits for them, and re-layouts: 15.1 us -> 2.22 us
  starting transfers between devices: 13.6 us -> 9.8 us
    all_to_all x2 -> x0, waiting for transfers between devices: 75.4 us -> none  [the longest x1 75.4 us: on_device(): lax.all_to_all(masked, 'rows', split_axis=0, concat_axis=1, tiled=True)]
    another operation x10 -> x0, other arithmetic: 54.5 us -> none  [the longest x7 34.8 us: solve_nodes(): factor = jnp.linalg.cholesky(system)]
    ppermute x0 -> x8, waiting for transfers between devices: none -> 41.6 us  [swap(): return lax.ppermute(x, 'rows', [(r, r ^ distance) for r in range(ranks)])]
    all_gather x1 -> x0, blocking collectives: 35.7 us -> none  [on_device(): lax.all_gather(planes, 'rows', axis=0, tiled=True)]
    unnamed x1 -> x0, blocking collectives: 29.8 us -> none
    pallas_call x0 -> x3, Pallas kernels: none -> 27.5 us  [the longest x1 12.2 us: local_sums(): pl.pallas_call(functools.partial(sums_kernel, bits), out_shape=(out, out)...]
    all_to_all x2 -> x0, starting transfers between devices: 13.6 us -> none  [the longest x1 7.39 us: on_device(): lax.all_to_all(tagged, 'rows', split_axis=0, concat_axis=1, tiled=True)]
    dot_general x5 -> x0, matrix products: 12.7 us -> none  [the longest x1 5.2 us: on_device(): jnp.einsum('nsf,nsg->nfg', arrived, arrived, preferred_element_type=jnp.f...]
  transfers between devices with their start and end apart: 2 -> 8, of which waited for: 1 -> 8; matrix products, arithmetic and copies ran while one was open for 5% -> 0% of each run, Pallas kernels for 0% -> 0%
where the time goes in v1:
time: 82.6 us; the launch traced here: 82.1 us
  waiting for transfers between devices  41.6 us (50%)
  Pallas kernels  27.5 us (33%)
  starting transfers between devices  9.8 us (12%)
  local copies, waits for them, and re-layouts  2.22 us (3%)
    ppermute x8, waiting for transfers between devices, swap(): return lax.ppermute(x, 'rows', [(r, r ^ distance) for r in range(ranks)])  41.6 us
    pallas_call x1, Pallas kernels, local_sums(): pl.pallas_call(functools.partial(sums_kernel, bits), out_shape=(out, out)...  12.2 us
    ppermute x8, starting transfers between devices, swap(): return lax.ppermute(x, 'rows', [(r, r ^ distance) for r in range(ranks)])  9.8 us
    pallas_call x1, Pallas kernels, solve(): pl.pallas_call(functools.partial(solve_kernel, size), out_shape=(jax.Shap...  8.16 us
    pallas_call x1, Pallas kernels, all_scores(): pl.pallas_call(functools.partial(scores_kernel, bits), out_shape=jax.Shap...  7.14 us
    unnamed x12, local copies, waits for them, and re-layouts  2.2 us
  transfers between devices with their start and end apart: 8, of which 8 were waited for; matrix products, arithmetic and copies ran while one was open for 0% of the time, Pallas kernels for 0%

profile of v1, /device:TPU:0, one launch (start us, length us, event | category | flops | bytes accessed | tf_op | source)
XLA Modules:
  0.0 82.1 jit_solution(5014928401436100804)
XLA Ops:
  0.6 0.0 copy-start.1
  0.6 0.7 copy-done.1
  1.4 0.0 copy-start.2
  1.4 0.8 copy-done.2
  2.1 0.0 copy-start.3
  2.1 0.7 copy-done.3
  2.8 12.2 %local_sums.1 = (f32[8,296,128]{2,1,0:T(8,128)S(1)}, f32[8,296,128]{2,1,0:T(8,128)S(1)}) custom-call(s32[16]{0:T(128)S(1)} %copy-done.3, bf16[8192,256]{1,0:T(8,128)(2,1)} %features.3, s32[8192]{0:T(1024)S(1)} %copy-done.1, s32[8192]{0:T(1024)S(1)} %copy-done.2), custom_call_target="tpu_custom_call" | custom-call | tf_op jit(solution)/shard_map/local_sums/pallas_call | solution.py:93
  15.0 0.5 collective-permute-start
  15.5 2.5 %collective-permute-done = f32[8,296,128]{2,1,0:T(8,128)S(1)} collective-permute-done((f32[8,296,128]{2,1,0:T(8,128)S(1)}, f32[8,296,128]{2,1,0:T(8,128)S(1)}, u32[]{:S(2)}, u32[]{:S(2)}) %collective-permute-start) | collective-permute-done | bytes 1212448 | tf_op jit(solution)/shard_map/ppermute | solution.py:225
  18.1 0.0 copy-start
  18.1 0.1 slice_add_fusion.1
  18.2 2.9 %collective-permute-start.1 = (f32[4,296,128]{2,1,0:T(8,128)S(1)}, f32[4,296,128]{2,1,0:T(8,128)S(1)}, u32[]{:S(2)}, u32[]{:S(2)}) collective-permute-start(f32[4,296,128]{2,1,0:T(8,128)S(1)} %get-tuple-element.11), channel_id=1, source_target_pairs={{0,2},{1,3},{2,0},{3,1},{4,6},{5,7},{6,4},{7,5},{8,10},{9,11},{10,... | collective-permute-start | bytes 1818632 | tf_op jit(solution)/shard_map/ppermute | solution.py:225
  21.1 14.0 %collective-permute-done.1 = f32[4,296,128]{2,1,0:T(8,128)S(1)} collective-permute-done((f32[4,296,128]{2,1,0:T(8,128)S(1)}, f32[4,296,128]{2,1,0:T(8,128)S(1)}, u32[]{:S(2)}, u32[]{:S(2)}) %collective-permute-start.1) | collective-permute-done | bytes 606240 | tf_op jit(solution)/shard_map/ppermute | solution.py:225
  35.1 0.1 slice_add_fusion.3
  35.2 1.9 %collective-permute-start.2 = (f32[2,296,128]{2,1,0:T(8,128)S(1)}, f32[2,296,128]{2,1,0:T(8,128)S(1)}, u32[]{:S(2)}, u32[]{:S(2)}) collective-permute-start(f32[2,296,128]{2,1,0:T(8,128)S(1)} %get-tuple-element.13), channel_id=1, source_target_pairs={{0,4},{1,5},{2,6},{3,7},{4,0},{5,1},{6,2},{7,3},{8,12},{9,13},{10,... | collective-permute-start | bytes 909320 | tf_op jit(solution)/shard_map/ppermute | solution.py:225
  37.0 6.9 %collective-permute-done.2 = f32[2,296,128]{2,1,0:T(8,128)S(1)} collective-permute-done((f32[2,296,128]{2,1,0:T(8,128)S(1)}, f32[2,296,128]{2,1,0:T(8,128)S(1)}, u32[]{:S(2)}, u32[]{:S(2)}) %collective-permute-start.2) | collective-permute-done | bytes 303136 | tf_op jit(solution)/shard_map/ppermute | solution.py:225
  44.0 2.6 %collective-permute-start.3 = (f32[1,296,128]{2,1,0:T(8,128)S(1)}, f32[1,296,128]{2,1,0:T(8,128)S(1)}, u32[]{:S(2)}, u32[]{:S(2)}) collective-permute-start(f32[1,296,128]{2,1,0:T(8,128)S(1)} %get-tuple-element.14), channel_id=1, source_target_pairs={{0,8},{1,9},{2,10},{3,11},{4,12},{5,13},{6,14},{7,15},{8,0},{9,1},... | collective-permute-start | bytes 454664 | tf_op jit(solution)/shard_map/ppermute | solution.py:225
  46.6 6.2 %collective-permute-done.3.came = f32[1,296,128]{2,1,0:T(8,128)S(1)} collective-permute-done((f32[1,296,128]{2,1,0:T(8,128)S(1)}, f32[1,296,128]{2,1,0:T(8,128)S(1)}, u32[]{:S(2)}, u32[]{:S(2)}) %collective-permute-start.3) | collective-permute-done | bytes 151584 | tf_op jit(solution)/shard_map/ppermute | solution.py:225
  52.8 8.2 %solve.1 = (f32[1,16,256]{2,1,0:T(8,128)}, bf16[1,16,384]{2,1,0:T(8,128)(2,1)S(1)}) custom-call(f32[1,296,128]{2,1,0:T(8,128)S(1)} %get-tuple-element.15.kept, f32[1,296,128]{2,1,0:T(8,128)S(1)} %collective-permute-done.3.came), custom_call_target="tpu_custom_call" | custom-call | tf_op jit(solution)/shard_map/solve/pallas_call | solution.py:178
  60.9 0.0 collective-permute-start.4
  60.9 4.6 %collective-permute-done.4 = bf16[1,16,384]{2,1,0:T(8,128)(2,1)S(1)} collective-permute-done((bf16[1,16,384]{2,1,0:T(8,128)(2,1)S(1)}, bf16[1,16,384]{2,1,0:T(8,128)(2,1)S(1)}, u32[]{:S(2)}, u32[]{:S(2)}) %collective-permute-start.4) | collective-permute-done | bytes 12320 | tf_op jit(solution)/shard_map/ppermute | solution.py:225
  65.5 0.7 collective-permute-start.5
  66.2 3.1 %collective-permute-done.5 = bf16[2,16,384]{2,1,0:T(8,128)(2,1)S(1)} collective-permute-done((bf16[2,16,384]{2,1,0:T(8,128)(2,1)S(1)}, bf16[2,16,384]{2,1,0:T(8,128)(2,1)S(1)}, u32[]{:S(2)}, u32[]{:S(2)}) %collective-permute-start.5) | collective-permute-done | bytes 24608 | tf_op jit(solution)/shard_map/ppermute | solution.py:225
  69.4 1.1 %collective-permute-start.6 = (bf16[4,16,384]{2,1,0:T(8,128)(2,1)S(1)}, bf16[4,16,384]{2,1,0:T(8,128)(2,1)S(1)}, u32[]{:S(2)}, u32[]{:S(2)}) collective-permute-start(bf16[4,16,384]{2,1,0:T(8,128)(2,1)S(1)} %pad_maximum_fusion.1), channel_id=1, source_target_pairs={{0,2},{1,3},{2,0},{3,1},{4,6},{5,7},{6,4},{7,5},{8,10},{9,11},{10,... | collective-permute-start | bytes 147464 | tf_op jit(solution)/shard_map/ppermute | solution.py:225
  70.5 3.0 %collective-permute-done.6 = bf16[4,16,384]{2,1,0:T(8,128)(2,1)S(1)} collective-permute-done((bf16[4,16,384]{2,1,0:T(8,128)(2,1)S(1)}, bf16[4,16,384]{2,1,0:T(8,128)(2,1)S(1)}, u32[]{:S(2)}, u32[]{:S(2)}) %collective-permute-start.6) | collective-permute-done | bytes 49184 | tf_op jit(solution)/shard_map/ppermute | solution.py:225
  73.6 0.1 collective-permute-start.7
  73.7 1.3 %collective-permute-done.7 = bf16[8,16,384]{2,1,0:T(8,128)(2,1)S(1)} collective-permute-done((bf16[8,16,384]{2,1,0:T(8,128)(2,1)S(1)}, bf16[8,16,384]{2,1,0:T(8,128)(2,1)S(1)}, u32[]{:S(2)}, u32[]{:S(2)}) %collective-permute-start.7) | collective-permute-done | bytes 98336 | tf_op jit(solution)/shard_map/ppermute | solution.py:225
  74.9 0.0 copy-done
  75.0 7.1 %all_scores.1 = f32[16,8192]{1,0:T(8,128)} custom-call(s32[16]{0:T(128)S(1)} %copy-done.3, bf16[8192,256]{1,0:T(8,128)(2,1)S(1)} %copy-done, s32[8192]{0:T(1024)S(1)} %copy-done.1, bf16[16,16,384]{2,1,0:T(8,128)(2,1)S(1)} %constant_dynamic-update-slice_fusion.messages), custom_call_target="tpu_custom_call" | custom-call | tf_op jit(solution)/shard_map/all_scores/pallas_call | solution.py:202
  (9 shorter events, 0.1 us)
Async XLA Ops:
  0.6 0.8 copy-start.1
  1.4 0.8 copy-start.2
  2.1 0.7 copy-start.3
  15.0 3.0 %collective-permute-start = (f32[8,296,128]{2,1,0:T(8,128)S(1)}, f32[8,296,128]{2,1,0:T(8,128)S(1)}, u32[]{:S(2)}, u32[]{:S(2)}) collective-permute-start(f32[8,296,128]{2,1,0:T(8,128)S(1)} %get-tuple-element.7), channel_id=1, source_target_pairs={{0,1},{1,0},{2,3},{3,2},{4,5},{5,4},{6,7},{7,6},{8,9},{9,8},{10,11... | collective-permute-start | bytes 3637256 | tf_op jit(solution)/shard_map/ppermute | solution.py:225
  18.1 56.9 %copy-start = (bf16[8192,256]{1,0:T(8,128)(2,1)S(1)}, bf16[8192,256]{1,0:T(8,128)(2,1)}, u32[]{:S(2)}) copy-start(bf16[8192,256]{1,0:T(8,128)(2,1)} %features.3) | copy-start | bytes 12582916
  18.2 16.9 %collective-permute-start.1 = (f32[4,296,128]{2,1,0:T(8,128)S(1)}, f32[4,296,128]{2,1,0:T(8,128)S(1)}, u32[]{:S(2)}, u32[]{:S(2)}) collective-permute-start(f32[4,296,128]{2,1,0:T(8,128)S(1)} %get-tuple-element.11), channel_id=1, source_target_pairs={{0,2},{1,3},{2,0},{3,1},{4,6},{5,7},{6,4},{7,5},{8,10},{9,11},{10,... | collective-permute-start | bytes 1818632 | tf_op jit(solution)/shard_map/ppermute | solution.py:225
  35.2 8.8 %collective-permute-start.2 = (f32[2,296,128]{2,1,0:T(8,128)S(1)}, f32[2,296,128]{2,1,0:T(8,128)S(1)}, u32[]{:S(2)}, u32[]{:S(2)}) collective-permute-start(f32[2,296,128]{2,1,0:T(8,128)S(1)} %get-tuple-element.13), channel_id=1, source_target_pairs={{0,4},{1,5},{2,6},{3,7},{4,0},{5,1},{6,2},{7,3},{8,12},{9,13},{10,... | collective-permute-start | bytes 909320 | tf_op jit(solution)/shard_map/ppermute | solution.py:225
  44.0 8.8 %collective-permute-start.3 = (f32[1,296,128]{2,1,0:T(8,128)S(1)}, f32[1,296,128]{2,1,0:T(8,128)S(1)}, u32[]{:S(2)}, u32[]{:S(2)}) collective-permute-start(f32[1,296,128]{2,1,0:T(8,128)S(1)} %get-tuple-element.14), channel_id=1, source_target_pairs={{0,8},{1,9},{2,10},{3,11},{4,12},{5,13},{6,14},{7,15},{8,0},{9,1},... | collective-permute-start | bytes 454664 | tf_op jit(solution)/shard_map/ppermute | solution.py:225
  60.9 4.6 %collective-permute-start.4 = (bf16[1,16,384]{2,1,0:T(8,128)(2,1)S(1)}, bf16[1,16,384]{2,1,0:T(8,128)(2,1)S(1)}, u32[]{:S(2)}, u32[]{:S(2)}) collective-permute-start(bf16[1,16,384]{2,1,0:T(8,128)(2,1)S(1)} %get-tuple-element.9), channel_id=1, source_target_pairs={{0,8},{1,9},{2,10},{3,11},{4,12},{5,13},{6,14},{7,15},{8,0},{9,1},... | collective-permute-start | bytes 36872 | tf_op jit(solution)/shard_map/ppermute | solution.py:225
  65.5 3.8 %collective-permute-start.5 = (bf16[2,16,384]{2,1,0:T(8,128)(2,1)S(1)}, bf16[2,16,384]{2,1,0:T(8,128)(2,1)S(1)}, u32[]{:S(2)}, u32[]{:S(2)}) collective-permute-start(bf16[2,16,384]{2,1,0:T(8,128)(2,1)S(1)} %pad_maximum_fusion.2), channel_id=1, source_target_pairs={{0,4},{1,5},{2,6},{3,7},{4,0},{5,1},{6,2},{7,3},{8,12},{9,13},{10,... | collective-permute-start | bytes 73736 | tf_op jit(solution)/shard_map/ppermute | solution.py:225
  69.4 4.2 %collective-permute-start.6 = (bf16[4,16,384]{2,1,0:T(8,128)(2,1)S(1)}, bf16[4,16,384]{2,1,0:T(8,128)(2,1)S(1)}, u32[]{:S(2)}, u32[]{:S(2)}) collective-permute-start(bf16[4,16,384]{2,1,0:T(8,128)(2,1)S(1)} %pad_maximum_fusion.1), channel_id=1, source_target_pairs={{0,2},{1,3},{2,0},{3,1},{4,6},{5,7},{6,4},{7,5},{8,10},{9,11},{10,... | collective-permute-start | bytes 147464 | tf_op jit(solution)/shard_map/ppermute | solution.py:225
  73.6 1.4 %collective-permute-start.7 = (bf16[8,16,384]{2,1,0:T(8,128)(2,1)S(1)}, bf16[8,16,384]{2,1,0:T(8,128)(2,1)S(1)}, u32[]{:S(2)}, u32[]{:S(2)}) collective-permute-start(bf16[8,16,384]{2,1,0:T(8,128)(2,1)S(1)} %pad_maximum_fusion), channel_id=1, source_target_pairs={{0,1},{1,0},{2,3},{3,2},{4,5},{5,4},{6,7},{7,6},{8,9},{9,8},{10,11... | collective-permute-start | bytes 294920 | tf_op jit(solution)/shard_map/ppermute | solution.py:225

commit v2 on v1

--- a/solution.py
+++ b/solution.py
@@ -38,21 +38,21 @@
     return sum((((number >> b) & 1) << (bits - 1 - b)) for b in range(bits))
 
 
-def sums_kernel(bits, owners, features, node_ids, labels, kept, sent):
-    node = pl.program_id(0)
-    segment, size = features.shape
+def exchange_orders(bits):
+    plain = list(range(1, bits))
+    return plain, plain if bits < 3 else [2, 1] + plain[2:]
+
+
+def packed_sums(x, alive, marks):
+    segment, size = x.shape
     half = size // 2
-    here = pl.ds(pl.multiple_of(node * segment, segment), segment)
-    alive = node_ids[here].reshape(1, segment) == node
-    marks = labels[here].reshape(1, segment)
     classes = lax.broadcasted_iota(jnp.int32, (CLASSES, segment), 0)
     hot = jnp.where((marks == classes) & alive, 1.0, 0.0)
-    length = jnp.sum(jnp.where(alive, 1.0, 0.0), axis=1, keepdims=True).astype(jnp.int32)
-    rows = lax.broadcasted_iota(jnp.int32, (segment, size), 0)
-    masked = jnp.where(rows < length, features[...], jnp.zeros((), jnp.bfloat16))
-    moment = over_rows(masked, masked)
-    sums = jnp.dot(hot.astype(jnp.bfloat16), masked, preferred_element_type=jnp.float32)
     counts = jnp.sum(hot, axis=1, keepdims=True)
+    live = jnp.where(alive, 1.0, 0.0).astype(jnp.bfloat16)
+    left = jnp.concatenate([x.T * live, hot.astype(jnp.bfloat16)], axis=0)
+    both = jnp.dot(left, x, preferred_element_type=jnp.float32)
+    moment, sums = both[:size], both[size:]
     ci = lax.broadcasted_iota(jnp.int32, (CLASSES, half), 0)
     cj = lax.broadcasted_iota(jnp.int32, (CLASSES, half), 1)
     count_row = jnp.sum(jnp.where(ci == cj, counts, 0.0), axis=0, keepdims=True)
@@ -63,47 +63,92 @@
     diagonal = jnp.sum(jnp.where(i == j, last, 0.0), axis=0, keepdims=True)
     ti = lax.broadcasted_iota(jnp.int32, (8, half), 0)
     tail = jnp.where(ti == 0, diagonal, jnp.where(ti == 1, count_row, 0.0))
-
-    apart = owners[node] ^ lax.axis_index("rows")
-    place = reverse(apart & -2, bits)
-
-    def store(out):
-        out[place, 0:half] = moment[:half, half:]
-        out[place, half : 2 * half] = mixed
-        out[place, 2 * half : 2 * half + CLASSES] = sums[:, :half]
-        out[place, 2 * half + CLASSES : 2 * half + 2 * CLASSES] = sums[:, half:]
-        out[place, 2 * half + 2 * CLASSES :] = tail
-
-    @pl.when((apart & 1) == 0)
-    def _():
-        store(kept)
-
-    @pl.when((apart & 1) == 1)
-    def _():
-        store(sent)
-
-
-def local_sums(features, node_ids, labels, owners, bits):
+    return moment[:half, half:], mixed, sums, tail
+
+
+def sums_kernel(
+    bits, group, owners, features, node_ids, labels, kept, sent, listed, rows, ids, marks, row_sems, id_sem, mark_sem
+):
+    me = lax.axis_index("rows")
+    nodes = owners.shape[0]
+    count, segment, size = rows.shape
+    half = size // 2
+    copy_ids = pltpu.make_async_copy(node_ids, ids, id_sem)
+    copy_marks = pltpu.make_async_copy(labels, marks, mark_sem)
+    copy_ids.start()
+    copy_marks.start()
+
+    def segment_of(node):
+        return pl.ds(pl.multiple_of(node * segment, segment), segment)
+
+    def fetch(q, node):
+        return pltpu.make_async_copy(features.at[segment_of(node)], rows.at[q], row_sems.at[q])
+
+    even_order, odd_order = exchange_orders(bits)
+    for node in range(nodes):
+        owner = owners[node]
+        apart = owner ^ me
+
+        def position(order, apart=apart):
+            return sum(((apart >> b) & 1) << (bits - 2 - t) for t, b in enumerate(order))
+
+        place = jnp.where((owner & 1) == 1, position(odd_order), position(even_order))
+        slot = (place & (count // 2 - 1)) + (apart & 1) * (count // 2)
+
+        @pl.when((place >> (bits - 2)) == group)
+        def _(slot=slot, node=node):
+            listed[slot] = node
+            fetch(slot, node).start()
+
+    copy_ids.wait()
+    copy_marks.wait()
+
+    def fill(out, base):
+        def step(q, carry):
+            node = listed[base + q]
+            fetch(base + q, node).wait()
+            here = segment_of(node)
+            alive = ids[here].reshape(1, segment) == node
+            cross, mixed, sums, tail = packed_sums(rows[base + q], alive, marks[here].reshape(1, segment))
+            out[q, 0:half] = cross
+            out[q, half : 2 * half] = mixed
+            out[q, 2 * half : 2 * half + CLASSES] = sums[:, :half]
+            out[q, 2 * half + CLASSES : 2 * half + 2 * CLASSES] = sums[:, half:]
+            out[q, 2 * half + 2 * CLASSES :] = tail
+            return carry
+
+        lax.fori_loop(0, count // 2, step, 0)
+
+    fill(sent, count // 2)
+    fill(kept, 0)
+
+
+def local_sums(features, node_ids, labels, owners, bits, group):
     row_count, size = features.shape
     nodes = owners.shape[0]
     segment = row_count // nodes
-    block = (nodes // 2, size + 2 * CLASSES + 8, size // 2)
-    out = jax.ShapeDtypeStruct(block, jnp.float32)
-    whole = pl.BlockSpec(block, lambda n, o: (0, 0, 0))
+    count = nodes // 2
+    out = jax.ShapeDtypeStruct((count // 2, size + 2 * CLASSES + 8, size // 2), jnp.float32)
+    far = pl.BlockSpec(memory_space=pltpu.HBM)
+    near = pl.BlockSpec(memory_space=pltpu.VMEM)
     return pl.pallas_call(
-        functools.partial(sums_kernel, bits),
+        functools.partial(sums_kernel, bits, group),
         out_shape=(out, out),
-        grid_spec=pltpu.PrefetchScalarGridSpec(
-            num_scalar_prefetch=1,
-            grid=(nodes,),
-            in_specs=[
-                pl.BlockSpec((segment, size), lambda n, o: (n, 0)),
-                pl.BlockSpec((row_count,), lambda n, o: (0,)),
-                pl.BlockSpec((row_count,), lambda n, o: (0,)),
-            ],
-            out_specs=(whole, whole),
+        in_specs=[pl.BlockSpec(memory_space=pltpu.SMEM), far, far, far],
+        out_specs=(near, near),
+        scratch_shapes=[
+            pltpu.SMEM((count,), jnp.int32),
+            pltpu.VMEM((count, segment, size), jnp.bfloat16),
+            pltpu.VMEM((row_count,), jnp.int32),
+            pltpu.VMEM((row_count,), jnp.int32),
+            pltpu.SemaphoreType.DMA((count,)),
+            pltpu.SemaphoreType.DMA,
+            pltpu.SemaphoreType.DMA,
+        ],
+        compiler_params=pltpu.CompilerParams(vmem_limit_bytes=58 << 20),
+        cost_estimate=pl.CostEstimate(
+            flops=row_count * size * size, bytes_accessed=row_count * size, transcendentals=0
         ),
-        compiler_params=pltpu.CompilerParams(vmem_limit_bytes=48 << 20),
         name="local_sums",
     )(owners, features, node_ids, labels)
 
@@ -182,36 +227,33 @@
         name="solve")(kept,came)
 
 
-def scores_kernel(bits, owners, features, node_ids, messages, scores):
-    node = pl.program_id(0)
-    segment, size = features.shape
-    here = pl.ds(pl.multiple_of(node * segment, segment), segment)
-    alive = node_ids[here].reshape(1, segment) == node
-    message = messages[reverse(owners[node] ^ lax.axis_index("rows"), bits)]
-    offsets = jnp.sum(message[:, size:].astype(jnp.float32), axis=1, keepdims=True)
-    result = lax.dot_general(
-        message[:, :size], features[...], (((1,), (1,)), ((), ())), preferred_element_type=jnp.float32
-    )
-    scores[...] = jnp.where(alive, result + offsets, 0.0)
+def scores_kernel(bits, group, owners, features, node_ids, messages, scores):
+    size = features.shape[1]
+    segment = scores.shape[1] // group
+    for g in range(group):
+        node = pl.program_id(0) * group + g
+        here = pl.ds(pl.multiple_of(node * segment, segment), segment)
+        alive = node_ids[here].reshape(1, segment) == node
+        message = messages[reverse(owners[node] ^ lax.axis_index("rows"), bits)]
+        offsets = jnp.sum(message[:, size:].astype(jnp.float32), axis=1, keepdims=True)
+        result = lax.dot_general(
+            message[:, :size], features[here, :], (((1,), (1,)), ((), ())), preferred_element_type=jnp.float32
+        )
+        scores[:, g * segment : (g + 1) * segment] = jnp.where(alive, result + offsets, 0.0)
 
 
 def all_scores(features, node_ids, owners, messages, bits):
     row_count, size = features.shape
     nodes = owners.shape[0]
     segment = row_count // nodes
+    group = nodes // 2
+    near = pl.BlockSpec(memory_space=pltpu.VMEM)
     return pl.pallas_call(
-        functools.partial(scores_kernel, bits),
+        functools.partial(scores_kernel, bits, group),
         out_shape=jax.ShapeDtypeStruct((CLASSES, row_count), jnp.float32),
-        grid_spec=pltpu.PrefetchScalarGridSpec(
-            num_scalar_prefetch=1,
-            grid=(nodes,),
-            in_specs=[
-                pl.BlockSpec((segment, size), lambda n, o: (n, 0)),
-                pl.BlockSpec((row_count,), lambda n, o: (0,)),
-                pl.BlockSpec(messages.shape, lambda n, o: (0, 0, 0)),
-            ],
-            out_specs=pl.BlockSpec((CLASSES, segment), lambda n, o: (0, n)),
-        ),
+        grid=(nodes // group,),
+        in_specs=[pl.BlockSpec(memory_space=pltpu.SMEM), near, near, near],
+        out_specs=pl.BlockSpec((CLASSES, segment * group), lambda n: (0, n)),
         compiler_params=pltpu.CompilerParams(vmem_limit_bytes=32 << 20),
         name="all_scores",
     )(owners, features, node_ids, messages)
@@ -220,21 +262,29 @@
 def on_device(ranks, features, node_ids, labels, owners):
     size = features.shape[1]
     bits = ranks.bit_length() - 1
-
-    def swap(x, distance):
-        return lax.ppermute(x, "rows", [(r, r ^ distance) for r in range(ranks)])
-
-    kept, sent = local_sums(features, node_ids, labels, owners, bits)
-    came = swap(sent, 1)
-    for b in range(1, bits):
-        middle = kept.shape[0] // 2
-        sent = kept[middle:] + came[middle:]
-        next_came = swap(sent, 1 << b)
-        kept = kept[:middle] + came[:middle]
+    orders = exchange_orders(bits)
+
+    def swap(x, distances):
+        return lax.ppermute(x, "rows", [(r, r ^ distances[r & 1]) for r in range(ranks)])
+
+    def halving(x, step):
+        return swap(x, [1 << order[step] for order in orders])
+
+    kept, sent = local_sums(features, node_ids, labels, owners, bits, 1)
+    sent = kept + swap(sent, (1, 1))
+    sent, later_owners = lax.optimization_barrier((sent, owners))
+    came = halving(sent, 0)
+    kept, sent = local_sums(features, node_ids, labels, later_owners, bits, 0)
+    kept = (kept, swap(sent, (1, 1)))
+    for step in range(1, bits - 1):
+        middle = came.shape[0] // 2
+        sent = sum(k[middle:] for k in kept) + came[middle:]
+        next_came = halving(sent, step)
+        kept = (sum(k[:middle] for k in kept) + came[:middle],)
         came = next_came
-    planes, held = solve(kept, came, size)
+    planes, held = solve(kept[0], came, size)
     for b in reversed(range(bits)):
-        held = jnp.concatenate([held, swap(held, 1 << b)], axis=0)
+        held = jnp.concatenate([held, swap(held, (1 << b, 1 << b))], axis=0)
     return planes, all_scores(features, node_ids, owners, held, bits)
 
 

time: 82.6 us -> 62.6 us (0.76)
  waiting for transfers between devices: 41.6 us -> 25.8 us
  Pallas kernels: 27.5 us -> 21.5 us
  local copies, waits for them, and re-layouts: 2.22 us -> 0.07 us
  other arithmetic: 0.25 us -> 2.37 us
  starting transfers between devices: 9.8 us -> 11.8 us
    ppermute x8 -> x9, waiting for transfers between devices: 41.6 us -> 25.8 us  [swap(): lax.ppermute(x, 'rows', [(r, r ^ distances[r & 1]) for r in range(ranks)])]
    pallas_call x2 -> x3, Pallas kernels: 19.3 us -> 13.4 us  [the longest x2 10.8 us: local_sums(): pl.pallas_call(functools.partial(sums_kernel, bits, group), out_shape=(ou...]
    unnamed x12 -> x10, local copies, waits for them, and re-layouts: 2.2 us -> 0.05 us
    add x3, other arithmetic: 0.22 us -> 2.34 us  [the longest x1 1.16 us: on_device(): kept = (sum((k[:middle] for k in kept)) + came[:middle],)]
    ppermute x8 -> x9, starting transfers between devices: 9.8 us -> 11.8 us  [swap(): lax.ppermute(x, 'rows', [(r, r ^ distances[r & 1]) for r in range(ranks)])]
  transfers between devices with their start and end apart: 8 -> 9, of which waited for: 8 -> 8; matrix products, arithmetic and copies ran while one was open for 0% -> 0% of each run, Pallas kernels for 0% -> 9%
where the time goes in v2:
time: 62.6 us; the launch traced here: 62.3 us
  waiting for transfers between devices  25.8 us (41%)
  Pallas kernels  21.5 us (34%)
  starting transfers between devices  11.8 us (19%)
  other arithmetic  2.37 us (4%)
  between operations  0.74 us (1%)
    ppermute x9, waiting for transfers between devices, swap(): lax.ppermute(x, 'rows', [(r, r ^ distances[r & 1]) for r in range(ranks)])  25.8 us
    ppermute x9, starting transfers between devices, swap(): lax.ppermute(x, 'rows', [(r, r ^ distances[r & 1]) for r in range(ranks)])  11.8 us
    pallas_call x2, Pallas kernels, local_sums(): pl.pallas_call(functools.partial(sums_kernel, bits, group), out_shape=(ou...  10.8 us
    pallas_call x1, Pallas kernels, solve(): pl.pallas_call(functools.partial(solve_kernel, size), out_shape=(jax.Shap...  8.16 us
    pallas_call x1, Pallas kernels, all_scores(): pl.pallas_call(functools.partial(scores_kernel, bits, group), out_shape=j...  2.61 us
  transfers between devices with their start and end apart: 9, of which 8 were waited for; matrix products, arithmetic and copies ran while one was open for 0% of the time, Pallas kernels for 9%

profile of v2, /device:TPU:0, one launch (start us, length us, event | category | flops | bytes accessed | tf_op | source)
XLA Modules:
  0.0 62.3 jit_solution(14979278890788730841)
XLA Ops:
  0.6 5.4 %local_sums.2 = (f32[4,296,128]{2,1,0:T(8,128)}, f32[4,296,128]{2,1,0:T(8,128)}) custom-call(s32[16]{0:T(128)} %owners.4, bf16[8192,256]{1,0:T(8,128)(2,1)} %features.5, s32[8192]{0:T(1024)} %node_ids.5, s32[8192]{0:T(1024)} %labels.3), custom_call_target="tpu_custom_call" | custom-call | flops 536870912 | bytes 2097152 | tf_op jit(solution)/shard_map/local_sums/pallas_call | solution.py:134
  6.0 0.4 collective-permute-start
  6.4 1.9 %collective-permute-done = f32[4,296,128]{2,1,0:T(8,128)S(1)} collective-permute-done((f32[4,296,128]{2,1,0:T(8,128)}, f32[4,296,128]{2,1,0:T(8,128)S(1)}, u32[]{:S(2)}, u32[]{:S(2)}) %collective-permute-start) | collective-permute-done | bytes 606240 | tf_op jit(solution)/shard_map/ppermute | solution.py:268
  8.3 1.1 %add.21 = f32[4,296,128]{2,1,0:T(8,128)S(1)} add(f32[4,296,128]{2,1,0:T(8,128)} %get-tuple-element.10, f32[4,296,128]{2,1,0:T(8,128)S(1)} %collective-permute-done) | non-fusion elementwise | flops 151552 | bytes 1818624 | tf_op jit(solution)/shard_map/add | solution.py:274
  9.5 0.0 copy-start
  9.5 0.0 copy-start.1
  9.5 0.0 copy-start.2
  9.5 2.9 %collective-permute-start.2 = (f32[4,296,128]{2,1,0:T(8,128)S(1)}, f32[4,296,128]{2,1,0:T(8,128)S(1)}, u32[]{:S(2)}, u32[]{:S(2)}) collective-permute-start(f32[4,296,128]{2,1,0:T(8,128)S(1)} %add.21), channel_id=1, source_target_pairs={{0,2},{1,5},{2,0},{3,7},{4,6},{5,1},{6,4},{7,3},{8,10},{9,13},{10,... | collective-permute-start | bytes 1818632 | tf_op jit(solution)/shard_map/ppermute | solution.py:268
  12.4 5.4 %local_sums.3 = (f32[4,296,128]{2,1,0:T(8,128)}, f32[4,296,128]{2,1,0:T(8,128)}) custom-call(s32[16]{0:T(128)} %owners.4, bf16[8192,256]{1,0:T(8,128)(2,1)} %features.5, s32[8192]{0:T(1024)} %node_ids.5, s32[8192]{0:T(1024)} %labels.3), custom_call_target="tpu_custom_call" | custom-call | flops 536870912 | bytes 2097152 | tf_op jit(solution)/shard_map/local_sums/pallas_call | solution.py:134
  17.8 0.1 collective-permute-start.1
  17.8 2.6 %collective-permute-done.2 = f32[4,296,128]{2,1,0:T(8,128)S(1)} collective-permute-done((f32[4,296,128]{2,1,0:T(8,128)S(1)}, f32[4,296,128]{2,1,0:T(8,128)S(1)}, u32[]{:S(2)}, u32[]{:S(2)}) %collective-permute-start.2) | collective-permute-done | bytes 606240 | tf_op jit(solution)/shard_map/ppermute | solution.py:268
  20.4 0.0 collective-permute-done.1
  20.4 1.2 %slice_add_fusion.2 = (f32[2,296,128]{2,1,0:T(8,128)S(1)}, f32[2,296,128]{2,1,0:T(8,128)S(1)}) fusion(f32[4,296,128]{2,1,0:T(8,128)S(1)} %collective-permute-done.2, f32[4,296,128]{2,1,0:T(8,128)S(1)} %collective-permute-done.1, f32[4,296,128]{2,1,0:T(8,128)} %get-tuple-element.13), kind=kLoop, calls=%fused_computation.2 | loop fusion | flops 303104 | bytes 2424832 | tf_op jit(solution)/shard_map/add | solution.py:283
  21.6 2.3 %collective-permute-start.3 = (f32[2,296,128]{2,1,0:T(8,128)S(1)}, f32[2,296,128]{2,1,0:T(8,128)S(1)}, u32[]{:S(2)}, u32[]{:S(2)}) collective-permute-start(f32[2,296,128]{2,1,0:T(8,128)S(1)} %get-tuple-element.19), channel_id=1, source_target_pairs={{0,4},{1,3},{2,6},{3,1},{4,0},{5,7},{6,2},{7,5},{8,12},{9,11},{10,... | collective-permute-start | bytes 909320 | tf_op jit(solution)/shard_map/ppermute | solution.py:268
  23.9 4.8 %collective-permute-done.3 = f32[2,296,128]{2,1,0:T(8,128)S(1)} collective-permute-done((f32[2,296,128]{2,1,0:T(8,128)S(1)}, f32[2,296,128]{2,1,0:T(8,128)S(1)}, u32[]{:S(2)}, u32[]{:S(2)}) %collective-permute-start.3) | collective-permute-done | bytes 303136 | tf_op jit(solution)/shard_map/ppermute | solution.py:268
  28.7 3.0 %collective-permute-start.4 = (f32[1,296,128]{2,1,0:T(8,128)S(1)}, f32[1,296,128]{2,1,0:T(8,128)S(1)}, u32[]{:S(2)}, u32[]{:S(2)}) collective-permute-start(f32[1,296,128]{2,1,0:T(8,128)S(1)} %get-tuple-element.20), channel_id=1, source_target_pairs={{0,8},{1,9},{2,10},{3,11},{4,12},{5,13},{6,14},{7,15},{8,0},{9,1},... | collective-permute-start | bytes 454664 | tf_op jit(solution)/shard_map/ppermute | solution.py:268
  31.7 5.8 %collective-permute-done.4.came = f32[1,296,128]{2,1,0:T(8,128)S(1)} collective-permute-done((f32[1,296,128]{2,1,0:T(8,128)S(1)}, f32[1,296,128]{2,1,0:T(8,128)S(1)}, u32[]{:S(2)}, u32[]{:S(2)}) %collective-permute-start.4) | collective-permute-done | bytes 151584 | tf_op jit(solution)/shard_map/ppermute | solution.py:268
  37.5 8.2 %solve.1 = (f32[1,16,256]{2,1,0:T(8,128)}, bf16[1,16,384]{2,1,0:T(8,128)(2,1)S(1)}) custom-call(f32[1,296,128]{2,1,0:T(8,128)S(1)} %get-tuple-element.21.kept, f32[1,296,128]{2,1,0:T(8,128)S(1)} %collective-permute-done.4.came), custom_call_target="tpu_custom_call" | custom-call | tf_op jit(solution)/shard_map/solve/pallas_call | solution.py:223
  45.7 0.4 collective-permute-start.5
  46.1 4.2 %collective-permute-done.5 = bf16[1,16,384]{2,1,0:T(8,128)(2,1)S(1)} collective-permute-done((bf16[1,16,384]{2,1,0:T(8,128)(2,1)S(1)}, bf16[1,16,384]{2,1,0:T(8,128)(2,1)S(1)}, u32[]{:S(2)}, u32[]{:S(2)}) %collective-permute-start.5) | collective-permute-done | bytes 12320 | tf_op jit(solution)/shard_map/ppermute | solution.py:268
  50.3 1.2 %collective-permute-start.6 = (bf16[2,16,384]{2,1,0:T(8,128)(2,1)S(1)}, bf16[2,16,384]{2,1,0:T(8,128)(2,1)S(1)}, u32[]{:S(2)}, u32[]{:S(2)}) collective-permute-start(bf16[2,16,384]{2,1,0:T(8,128)(2,1)S(1)} %pad_maximum_fusion.2), channel_id=1, source_target_pairs={{0,4},{1,5},{2,6},{3,7},{4,0},{5,1},{6,2},{7,3},{8,12},{9,13},{10,... | collective-permute-start | bytes 73736 | tf_op jit(solution)/shard_map/ppermute | solution.py:268
  51.4 2.7 %collective-permute-done.6 = bf16[2,16,384]{2,1,0:T(8,128)(2,1)S(1)} collective-permute-done((bf16[2,16,384]{2,1,0:T(8,128)(2,1)S(1)}, bf16[2,16,384]{2,1,0:T(8,128)(2,1)S(1)}, u32[]{:S(2)}, u32[]{:S(2)}) %collective-permute-start.6) | collective-permute-done | bytes 24608 | tf_op jit(solution)/shard_map/ppermute | solution.py:268
  54.1 1.6 %collective-permute-start.7 = (bf16[4,16,384]{2,1,0:T(8,128)(2,1)S(1)}, bf16[4,16,384]{2,1,0:T(8,128)(2,1)S(1)}, u32[]{:S(2)}, u32[]{:S(2)}) collective-permute-start(bf16[4,16,384]{2,1,0:T(8,128)(2,1)S(1)} %pad_maximum_fusion.1), channel_id=1, source_target_pairs={{0,2},{1,3},{2,0},{3,1},{4,6},{5,7},{6,4},{7,5},{8,10},{9,11},{10,... | collective-permute-start | bytes 147464 | tf_op jit(solution)/shard_map/ppermute | solution.py:268
  55.7 2.6 %collective-permute-done.7 = bf16[4,16,384]{2,1,0:T(8,128)(2,1)S(1)} collective-permute-done((bf16[4,16,384]{2,1,0:T(8,128)(2,1)S(1)}, bf16[4,16,384]{2,1,0:T(8,128)(2,1)S(1)}, u32[]{:S(2)}, u32[]{:S(2)}) %collective-permute-start.7) | collective-permute-done | bytes 49184 | tf_op jit(solution)/shard_map/ppermute | solution.py:268
  58.3 0.1 collective-permute-start.8
  58.4 1.3 %collective-permute-done.8 = bf16[8,16,384]{2,1,0:T(8,128)(2,1)S(1)} collective-permute-done((bf16[8,16,384]{2,1,0:T(8,128)(2,1)S(1)}, bf16[8,16,384]{2,1,0:T(8,128)(2,1)S(1)}, u32[]{:S(2)}, u32[]{:S(2)}) %collective-permute-start.8) | collective-permute-done | bytes 98336 | tf_op jit(solution)/shard_map/ppermute | solution.py:268
  59.7 0.0 copy-done
  59.7 0.0 copy-done.1
  59.7 0.0 copy-done.2
  59.7 2.6 %all_scores.1 = f32[16,8192]{1,0:T(8,128)} custom-call(s32[16]{0:T(128)S(1)} %copy-done.2, bf16[8192,256]{1,0:T(8,128)(2,1)S(1)} %copy-done, s32[8192]{0:T(1024)S(1)} %copy-done.1, bf16[16,16,384]{2,1,0:T(8,128)(2,1)S(1)} %constant_dynamic-update-slice_fusion.messages), custom_call_target="tpu_custom_call" | custom-call | tf_op jit(solution)/shard_map/all_scores/pallas_call | solution.py:251
  (9 shorter events, 0.1 us)
Async XLA Ops:
  6.0 2.3 %collective-permute-start = (f32[4,296,128]{2,1,0:T(8,128)}, f32[4,296,128]{2,1,0:T(8,128)S(1)}, u32[]{:S(2)}, u32[]{:S(2)}) collective-permute-start(f32[4,296,128]{2,1,0:T(8,128)} %get-tuple-element.11), channel_id=1, source_target_pairs={{0,1},{1,0},{2,3},{3,2},{4,5},{5,4},{6,7},{7,6},{8,9},{9,8},{10,11... | collective-permute-start | bytes 1818632 | tf_op jit(solution)/shard_map/ppermute | solution.py:268
  9.5 50.2 %copy-start = (bf16[8192,256]{1,0:T(8,128)(2,1)S(1)}, bf16[8192,256]{1,0:T(8,128)(2,1)}, u32[]{:S(2)}) copy-start(bf16[8192,256]{1,0:T(8,128)(2,1)} %features.5) | copy-start | bytes 12582916
  9.5 50.2 %copy-start.1 = (s32[8192]{0:T(1024)S(1)}, s32[8192]{0:T(1024)}, u32[]{:S(2)}) copy-start(s32[8192]{0:T(1024)} %node_ids.5) | copy-start | bytes 98308
  9.5 50.2 %copy-start.2 = (s32[16]{0:T(128)S(1)}, s32[16]{0:T(128)}, u32[]{:S(2)}) copy-start(s32[16]{0:T(128)} %owners.4) | copy-start | bytes 196
  9.5 10.9 %collective-permute-start.2 = (f32[4,296,128]{2,1,0:T(8,128)S(1)}, f32[4,296,128]{2,1,0:T(8,128)S(1)}, u32[]{:S(2)}, u32[]{:S(2)}) collective-permute-start(f32[4,296,128]{2,1,0:T(8,128)S(1)} %add.21), channel_id=1, source_target_pairs={{0,2},{1,5},{2,0},{3,7},{4,6},{5,1},{6,4},{7,3},{8,10},{9,13},{10,... | collective-permute-start | bytes 1818632 | tf_op jit(solution)/shard_map/ppermute | solution.py:268
  17.8 2.7 %collective-permute-start.1 = (f32[4,296,128]{2,1,0:T(8,128)}, f32[4,296,128]{2,1,0:T(8,128)S(1)}, u32[]{:S(2)}, u32[]{:S(2)}) collective-permute-start(f32[4,296,128]{2,1,0:T(8,128)} %get-tuple-element.14), channel_id=1, source_target_pairs={{0,1},{1,0},{2,3},{3,2},{4,5},{5,4},{6,7},{7,6},{8,9},{9,8},{10,11... | collective-permute-start | bytes 1818632 | tf_op jit(solution)/shard_map/ppermute | solution.py:268
  21.6 7.1 %collective-permute-start.3 = (f32[2,296,128]{2,1,0:T(8,128)S(1)}, f32[2,296,128]{2,1,0:T(8,128)S(1)}, u32[]{:S(2)}, u32[]{:S(2)}) collective-permute-start(f32[2,296,128]{2,1,0:T(8,128)S(1)} %get-tuple-element.19), channel_id=1, source_target_pairs={{0,4},{1,3},{2,6},{3,1},{4,0},{5,7},{6,2},{7,5},{8,12},{9,11},{10,... | collective-permute-start | bytes 909320 | tf_op jit(solution)/shard_map/ppermute | solution.py:268
  28.7 8.8 %collective-permute-start.4 = (f32[1,296,128]{2,1,0:T(8,128)S(1)}, f32[1,296,128]{2,1,0:T(8,128)S(1)}, u32[]{:S(2)}, u32[]{:S(2)}) collective-permute-start(f32[1,296,128]{2,1,0:T(8,128)S(1)} %get-tuple-element.20), channel_id=1, source_target_pairs={{0,8},{1,9},{2,10},{3,11},{4,12},{5,13},{6,14},{7,15},{8,0},{9,1},... | collective-permute-start | bytes 454664 | tf_op jit(solution)/shard_map/ppermute | solution.py:268
  45.7 4.6 %collective-permute-start.5 = (bf16[1,16,384]{2,1,0:T(8,128)(2,1)S(1)}, bf16[1,16,384]{2,1,0:T(8,128)(2,1)S(1)}, u32[]{:S(2)}, u32[]{:S(2)}) collective-permute-start(bf16[1,16,384]{2,1,0:T(8,128)(2,1)S(1)} %get-tuple-element.17), channel_id=1, source_target_pairs={{0,8},{1,9},{2,10},{3,11},{4,12},{5,13},{6,14},{7,15},{8,0},{9,1},... | collective-permute-start | bytes 36872 | tf_op jit(solution)/shard_map/ppermute | solution.py:268
  50.3 3.8 %collective-permute-start.6 = (bf16[2,16,384]{2,1,0:T(8,128)(2,1)S(1)}, bf16[2,16,384]{2,1,0:T(8,128)(2,1)S(1)}, u32[]{:S(2)}, u32[]{:S(2)}) collective-permute-start(bf16[2,16,384]{2,1,0:T(8,128)(2,1)S(1)} %pad_maximum_fusion.2), channel_id=1, source_target_pairs={{0,4},{1,5},{2,6},{3,7},{4,0},{5,1},{6,2},{7,3},{8,12},{9,13},{10,... | collective-permute-start | bytes 73736 | tf_op jit(solution)/shard_map/ppermute | solution.py:268
  54.1 4.2 %collective-permute-start.7 = (bf16[4,16,384]{2,1,0:T(8,128)(2,1)S(1)}, bf16[4,16,384]{2,1,0:T(8,128)(2,1)S(1)}, u32[]{:S(2)}, u32[]{:S(2)}) collective-permute-start(bf16[4,16,384]{2,1,0:T(8,128)(2,1)S(1)} %pad_maximum_fusion.1), channel_id=1, source_target_pairs={{0,2},{1,3},{2,0},{3,1},{4,6},{5,7},{6,4},{7,5},{8,10},{9,11},{10,... | collective-permute-start | bytes 147464 | tf_op jit(solution)/shard_map/ppermute | solution.py:268
  58.3 1.4 %collective-permute-start.8 = (bf16[8,16,384]{2,1,0:T(8,128)(2,1)S(1)}, bf16[8,16,384]{2,1,0:T(8,128)(2,1)S(1)}, u32[]{:S(2)}, u32[]{:S(2)}) collective-permute-start(bf16[8,16,384]{2,1,0:T(8,128)(2,1)S(1)} %pad_maximum_fusion), channel_id=1, source_target_pairs={{0,1},{1,0},{2,3},{3,2},{4,5},{5,4},{6,7},{7,6},{8,9},{9,8},{10,11... | collective-permute-start | bytes 294920 | tf_op jit(solution)/shard_map/ppermute | solution.py:268

commit v3 on v2

--- a/solution.py
+++ b/solution.py
@@ -34,13 +34,16 @@
     )
 
 
-def reverse(number, bits):
-    return sum((((number >> b) & 1) << (bits - 1 - b)) for b in range(bits))
-
-
 def exchange_orders(bits):
     plain = list(range(1, bits))
     return plain, plain if bits < 3 else [2, 1] + plain[2:]
+
+
+def place_of(apart, owner, bits):
+    even, odd = (
+        sum(((apart >> b) & 1) << (bits - 2 - t) for t, b in enumerate(order)) for order in exchange_orders(bits)
+    )
+    return jnp.where((owner & 1) == 1, odd, even)
 
 
 def packed_sums(x, alive, marks):
@@ -84,15 +87,9 @@
     def fetch(q, node):
         return pltpu.make_async_copy(features.at[segment_of(node)], rows.at[q], row_sems.at[q])
 
-    even_order, odd_order = exchange_orders(bits)
     for node in range(nodes):
-        owner = owners[node]
-        apart = owner ^ me
-
-        def position(order, apart=apart):
-            return sum(((apart >> b) & 1) << (bits - 2 - t) for t, b in enumerate(order))
-
-        place = jnp.where((owner & 1) == 1, position(odd_order), position(even_order))
+        apart = owners[node] ^ me
+        place = place_of(apart, owners[node], bits)
         slot = (place & (count // 2 - 1)) + (apart & 1) * (count // 2)
 
         @pl.when((place >> (bits - 2)) == group)
@@ -128,7 +125,7 @@
     nodes = owners.shape[0]
     segment = row_count // nodes
     count = nodes // 2
-    out = jax.ShapeDtypeStruct((count // 2, size + 2 * CLASSES + 8, size // 2), jnp.float32)
+    out = pltpu.VMEM((count // 2, size + 2 * CLASSES + 8, size // 2), jnp.float32)
     far = pl.BlockSpec(memory_space=pltpu.HBM)
     near = pl.BlockSpec(memory_space=pltpu.VMEM)
     return pl.pallas_call(
@@ -145,86 +142,123 @@
             pltpu.SemaphoreType.DMA,
             pltpu.SemaphoreType.DMA,
         ],
-        compiler_params=pltpu.CompilerParams(vmem_limit_bytes=58 << 20),
+        compiler_params=pltpu.CompilerParams(vmem_limit_bytes=32 << 20),
         cost_estimate=pl.CostEstimate(
             flops=row_count * size * size, bytes_accessed=row_count * size, transcendentals=0
         ),
         name="local_sums",
-    )(owners, features, node_ids, labels)
+    )(*(pltpu.with_memory_space_constraint(a, pltpu.HBM) for a in (owners, features, node_ids, labels)))
 
 
 def sweep(matrix, size):
-    lanes=lax.broadcasted_iota(jnp.int32,(1,size),1)
-    rows=lax.broadcasted_iota(jnp.int32,(PANEL,1),0)
-    lane_id=lax.broadcasted_iota(jnp.int32,(PANEL,size),1)
-    row_id=lax.broadcasted_iota(jnp.int32,(PANEL,size),0)
-    panel=matrix[0:PANEL,:]
-    for first in range(0,size,PANEL):
-        last=first+PANEL
-        inside=(lanes>=first)&(lanes<last)
-        p1,p2,p3=split(panel)
-        left=jnp.concatenate([p1,p1,p2,p2,p1,p3],axis=0)
-        column=[jnp.broadcast_to(panel[:,first+c:first+c+1],(PANEL,128)) for c in range(PANEL)]
-        work=jnp.where(inside,jnp.where(lane_id==row_id+first,-1.0,0.0),panel)
-        scale=jnp.zeros((PANEL,128),jnp.float32)
-        for k in range(PANEL):
-            here=rows==k
-            inverse=1.0/jnp.broadcast_to(column[k][k:k+1,:],(PANEL,128))
-            factor=jnp.where(here,0.0,column[k]*inverse)
-            scale=jnp.where(here,inverse,scale)
-            for c in range(k+1,PANEL):
-                column[c]=column[c]-factor*column[c][k:k+1,:]
-            work=work-jnp.concatenate([factor]*(size//128),axis=1)*work[k:k+1,:]
-        work=work*jnp.concatenate([scale]*(size//128),axis=1)
-        w1,w2,w3=split(work)
-        right=jnp.concatenate([w1,w2,w1,w2,w3,w1],axis=0)
-        if last<size:
-            base=last//128*128
-            edge=over_rows(left[:,base:base+128],right)
-            panel=jnp.where(inside,0.0,matrix[last:last+PANEL,:])-edge[last-base:last-base+PANEL,:]
-        update=over_rows(left,right)
-        matrix[...]=jnp.where(inside,0.0,matrix[...])-update
-        matrix[first:last,:]=work
-def solve_kernel(size, kept, came, planes, message, matrix):
-    half=size//2
-    total_block=kept[0]+came[0]
-    cross=total_block[0:half]
-    mixed=total_block[half:2*half]
-    sums=jnp.concatenate([total_block[2*half:2*half+CLASSES],total_block[2*half+CLASSES:2*half+2*CLASSES]],axis=1)
-    at=2*half+2*CLASSES
-    diagonal=total_block[at:at+1]
-    count_row=total_block[at+1:at+2]
-    i=lax.broadcasted_iota(jnp.int32,(half,half),0); j=lax.broadcasted_iota(jnp.int32,(half,half),1)
-    ci=lax.broadcasted_iota(jnp.int32,(CLASSES,half),0); cj=lax.broadcasted_iota(jnp.int32,(CLASSES,half),1)
-    counts=jnp.sum(jnp.where(ci==cj,count_row,0.0),axis=1,keepdims=True)
-    total=jnp.sum(counts,axis=0,keepdims=True)
-    centers=jnp.sum(sums,axis=0,keepdims=True)/total
-    scaled=sums/jnp.maximum(counts,1.0)
-    shifts=(sums-counts*centers)/total
-    between=wide_over_rows(sums,scaled)
-    upper=jnp.where(i<j,mixed,0.0)
-    lower=jnp.where(i>j,mixed,0.0)
-    ridge=jnp.where(i==j,RIDGE,0.0)
-    a11=upper+upper.T+jnp.where(i==j,mixed,0.0)
-    a22=lower+lower.T+jnp.where(i==j,diagonal,0.0)
-    matrix[0:half,0:half]=(a11-between[0:half,0:half])/total+ridge
-    matrix[0:half,half:]=(cross-between[0:half,half:])/total
-    matrix[half:,0:half]=(cross.T-between[half:,0:half])/total
-    matrix[half:,half:]=(a22-between[half:,half:])/total+ridge
-    sweep(matrix,size)
-    result=-jnp.dot(shifts,matrix[...],precision=HIGH,preferred_element_type=jnp.float32)
-    planes[0]=result
-    offsets=-jnp.sum(result*centers,axis=1,keepdims=True)
-    o1,o2,o3=split(offsets)
-    message[0,:,0:size]=result.astype(jnp.bfloat16)
-    lane=lax.broadcasted_iota(jnp.int32,(CLASSES,128),1)
-    message[0,:,size:]=jnp.where(lane==0,o1.astype(jnp.float32),jnp.where(lane==1,o2.astype(jnp.float32),jnp.where(lane==2,o3.astype(jnp.float32),0.0))).astype(jnp.bfloat16)
-def solve(kept,came,size):
-    return pl.pallas_call(functools.partial(solve_kernel,size),
-        out_shape=(jax.ShapeDtypeStruct((1,CLASSES,size),jnp.float32),jax.ShapeDtypeStruct((1,CLASSES,size+128),jnp.bfloat16)),
-        scratch_shapes=[pltpu.VMEM((size,size),jnp.float32)],
-        compiler_params=pltpu.CompilerParams(vmem_limit_bytes=32<<20),
-        name="solve")(kept,came)
+    across = size // LANES
+    lanes = lax.broadcasted_iota(jnp.int32, (1, size), 1)
+    rows = lax.broadcasted_iota(jnp.int32, (PANEL, 1), 0)
+    lane_id = lax.broadcasted_iota(jnp.int32, (PANEL, size), 1)
+    row_id = lax.broadcasted_iota(jnp.int32, (PANEL, size), 0)
+    odd = (lax.broadcasted_iota(jnp.int32, (PANEL, size), 0) & 1) == 1
+
+    def spread(x, at):
+        return jnp.broadcast_to(x[:, at : at + 1], (PANEL, LANES))
+
+    def wide(x):
+        return jnp.concatenate([x] * across, axis=1)
+
+    panel = matrix[0:PANEL, :]
+    for first in range(0, size, PANEL):
+        last = first + PANEL
+        inside = (lanes >= first) & (lanes < last)
+        p1, p2, p3 = split(panel)
+        left = jnp.concatenate([p1, p1, p2, p2, p1, p3], axis=0)
+        column = [spread(panel, first + c) for c in range(PANEL)]
+        if last < size:
+            following = matrix[last : last + PANEL, :]
+            ahead = [spread(following, first + c) for c in range(PANEL)]
+        work = jnp.where(inside, jnp.where(lane_id == row_id + first, -1.0, 0.0), panel)
+        own = jnp.zeros((PANEL, LANES), jnp.float32)
+        cross = own
+        for k in range(0, PANEL, 2):
+            c0, c1 = column[k], column[k + 1]
+            b00 = jnp.broadcast_to(c0[k : k + 1, :], (PANEL, LANES))
+            b10 = jnp.broadcast_to(c0[k + 1 : k + 2, :], (PANEL, LANES))
+            b11 = jnp.broadcast_to(c1[k + 1 : k + 2, :], (PANEL, LANES))
+            inverse = 1.0 / (b00 * b11 - b10 * b10)
+            n00, n10, n11 = b11 * inverse, -b10 * inverse, b00 * inverse
+            pair = (rows == k) | (rows == k + 1)
+            c0, c1 = jnp.where(pair, 0.0, c0), jnp.where(pair, 0.0, c1)
+            f0, f1 = c0 * n00 + c1 * n10, c0 * n10 + c1 * n11
+            own = jnp.where(rows == k, n00, jnp.where(rows == k + 1, n11, own))
+            cross = jnp.where(pair, n10, cross)
+            for c in range(k + 2, PANEL):
+                column[c] = column[c] - f0 * column[c][k : k + 1, :] - f1 * column[c][k + 1 : k + 2, :]
+            work = work - wide(f0) * work[k : k + 1, :] - wide(f1) * work[k + 1 : k + 2, :]
+        other = jnp.where(odd, pltpu.roll(work, 1, 0), pltpu.roll(work, PANEL - 1, 0))
+        work = work * wide(own) + other * wide(cross)
+        if last < size:
+            terms = [wide(ahead[c]) * work[c : c + 1, :] for c in range(PANEL)]
+            while len(terms) > 1:
+                terms = [terms[t] + terms[t + 1] for t in range(0, len(terms), 2)]
+            panel = jnp.where(inside, 0.0, following) - terms[0]
+        w1, w2, w3 = split(work)
+        right = jnp.concatenate([w1, w2, w1, w2, w3, w1], axis=0)
+        starts = list(range(0, size, LANES))
+        needed = last + PANEL if last + PANEL < size else 0
+        for base in sorted(starts, key=lambda t: not t <= needed < t + LANES):
+            part = over_rows(left[:, base : base + LANES], right)
+            matrix[base : base + LANES, :] = jnp.where(inside, 0.0, matrix[base : base + LANES, :]) - part
+        matrix[first:last, :] = work
+
+
+def solve_kernel(kept, came, planes, message, matrix):
+    size = matrix.shape[0]
+    half = size // 2
+    packed = kept[0] + came[0]
+    cross, mixed = packed[:half], packed[half:size]
+    sums = jnp.concatenate([packed[size : size + CLASSES], packed[size + CLASSES : size + 2 * CLASSES]], axis=1)
+    at = size + 2 * CLASSES
+    diagonal, count_row = packed[at : at + 1], packed[at + 1 : at + 2]
+    i = lax.broadcasted_iota(jnp.int32, (half, half), 0)
+    j = lax.broadcasted_iota(jnp.int32, (half, half), 1)
+    ci = lax.broadcasted_iota(jnp.int32, (CLASSES, half), 0)
+    cj = lax.broadcasted_iota(jnp.int32, (CLASSES, half), 1)
+    counts = jnp.sum(jnp.where(ci == cj, count_row, 0.0), axis=1, keepdims=True)
+    total = jnp.sum(counts, axis=0, keepdims=True)
+    centers = jnp.sum(sums, axis=0, keepdims=True) / total
+    scaled = sums / jnp.maximum(counts, 1.0)
+    shifts = (sums - counts * centers) / total
+    between = wide_over_rows(sums, scaled)
+    upper = jnp.where(i < j, mixed, 0.0)
+    lower = jnp.where(i > j, mixed, 0.0)
+    ridge = jnp.where(i == j, RIDGE, 0.0)
+    start = upper + upper.T + jnp.where(i == j, mixed, 0.0)
+    end = lower + lower.T + jnp.where(i == j, diagonal, 0.0)
+    matrix[:half, :half] = (start - between[:half, :half]) / total + ridge
+    matrix[:half, half:] = (cross - between[:half, half:]) / total
+    matrix[half:, :half] = (cross.T - between[half:, :half]) / total
+    matrix[half:, half:] = (end - between[half:, half:]) / total + ridge
+    sweep(matrix, size)
+    result = -jnp.dot(shifts, matrix[...], precision=HIGH, preferred_element_type=jnp.float32)
+    planes[0] = result
+    offsets = -jnp.sum(result * centers, axis=1, keepdims=True)
+    lane = lax.broadcasted_iota(jnp.int32, (CLASSES, LANES), 1)
+    parts = jnp.zeros((CLASSES, LANES), jnp.float32)
+    for t, term in enumerate(split(offsets)):
+        parts = jnp.where(lane == t, term.astype(jnp.float32), parts)
+    message[0, :, :size] = result.astype(jnp.bfloat16)
+    message[0, :, size:] = parts.astype(jnp.bfloat16)
+
+
+def solve(kept, came, size):
+    return pl.pallas_call(
+        solve_kernel,
+        out_shape=(
+            jax.ShapeDtypeStruct((1, CLASSES, size), jnp.float32),
+            jax.ShapeDtypeStruct((1, CLASSES, size + LANES), jnp.bfloat16),
+        ),
+        scratch_shapes=[pltpu.VMEM((size, size), jnp.float32)],
+        compiler_params=pltpu.CompilerParams(vmem_limit_bytes=32 << 20),
+        name="solve",
+    )(kept, came)
 
 
 def scores_kernel(bits, group, owners, features, node_ids, messages, scores):
@@ -234,7 +268,9 @@
         node = pl.program_id(0) * group + g
         here = pl.ds(pl.multiple_of(node * segment, segment), segment)
         alive = node_ids[here].reshape(1, segment) == node
-        message = messages[reverse(owners[node] ^ lax.axis_index("rows"), bits)]
+        owner = owners[node]
+        apart = owner ^ lax.axis_index("rows")
+        message = messages[place_of(apart, owner, bits) + ((apart & 1) << (bits - 1))]
         offsets = jnp.sum(message[:, size:].astype(jnp.float32), axis=1, keepdims=True)
         result = lax.dot_general(
             message[:, :size], features[here, :], (((1,), (1,)), ((), ())), preferred_element_type=jnp.float32
@@ -283,8 +319,9 @@
         kept = (sum(k[:middle] for k in kept) + came[:middle],)
         came = next_came
     planes, held = solve(kept[0], came, size)
-    for b in reversed(range(bits)):
-        held = jnp.concatenate([held, swap(held, (1 << b, 1 << b))], axis=0)
+    for step in reversed(range(bits - 1)):
+        held = jnp.concatenate([held, halving(held, step)], axis=0)
+    held = jnp.concatenate([held, swap(held, (1, 1))], axis=0)
     return planes, all_scores(features, node_ids, owners, held, bits)
 
 

time: 62.6 us -> 58.5 us (0.935)
  Pallas kernels: 21.5 us -> 18.6 us
  other arithmetic: 2.37 us -> 0.27 us
    pallas_call x2, Pallas kernels: 10.8 us -> 8.83 us  [local_sums(): pl.pallas_call(functools.partial(sums_kernel, bits, group), out_shape=(ou...]
    add x1, other arithmetic: 1.13 us -> 0.06 us  [on_device(): sent = kept + swap(sent, (1, 1))]
    add x1, other arithmetic: 1.16 us -> 0.13 us  [on_device(): kept = (sum((k[:middle] for k in kept)) + came[:middle],)]
    pallas_call x1, Pallas kernels: 8.16 us -> 7.14 us  [solve(): pl.pallas_call(solve_kernel, out_shape=(jax.ShapeDtypeStruct((1, CLASSES,...]
  transfers between devices with their start and end apart: 9 -> 9, of which waited for: 8 -> 8; matrix products, arithmetic and copies ran while one was open for 0% -> 0% of each run, Pallas kernels for 9% -> 8%
where the time goes in v3:
time: 58.5 us; the launch traced here: 58.2 us
  waiting for transfers between devices  26.3 us (45%)
  Pallas kernels  18.6 us (32%)
  starting transfers between devices  12.2 us (21%)
  between operations  0.74 us (1%)
    ppermute x9, waiting for transfers between devices, swap(): lax.ppermute(x, 'rows', [(r, r ^ distances[r & 1]) for r in range(ranks)])  26.3 us
    ppermute x9, starting transfers between devices, swap(): lax.ppermute(x, 'rows', [(r, r ^ distances[r & 1]) for r in range(ranks)])  12.2 us
    pallas_call x2, Pallas kernels, local_sums(): pl.pallas_call(functools.partial(sums_kernel, bits, group), out_shape=(ou...  8.83 us
    pallas_call x1, Pallas kernels, solve(): pl.pallas_call(solve_kernel, out_shape=(jax.ShapeDtypeStruct((1, CLASSES,...  7.14 us
    pallas_call x1, Pallas kernels, all_scores(): pl.pallas_call(functools.partial(scores_kernel, bits, group), out_shape=j...  2.61 us
  transfers between devices with their start and end apart: 9, of which 8 were waited for; matrix products, arithmetic and copies ran while one was open for 0% of the time, Pallas kernels for 8%

profile of v3, /device:TPU:0, one launch (start us, length us, event | category | flops | bytes accessed | tf_op | source)
XLA Modules:
  0.0 58.2 jit_solution(16647011315209351518)
XLA Ops:
  0.6 4.5 %local_sums.2 = (f32[4,296,128]{2,1,0:T(8,128)S(1)}, f32[4,296,128]{2,1,0:T(8,128)S(1)}) custom-call(s32[16]{0:T(128)} %owners.4, bf16[8192,256]{1,0:T(8,128)(2,1)} %features.5, s32[8192]{0:T(1024)} %node_ids.5, s32[8192]{0:T(1024)} %labels.3), custom_call_target="tpu_custom_call" | custom-call | flops 536870912 | bytes 2097152 | tf_op jit(solution)/shard_map/local_sums/pallas_call | solution.py:131
  5.1 0.5 collective-permute-start
  5.6 1.7 %collective-permute-done = f32[4,296,128]{2,1,0:T(8,128)S(1)} collective-permute-done((f32[4,296,128]{2,1,0:T(8,128)S(1)}, f32[4,296,128]{2,1,0:T(8,128)S(1)}, u32[]{:S(2)}, u32[]{:S(2)}) %collective-permute-start) | collective-permute-done | bytes 606240 | tf_op jit(solution)/shard_map/ppermute | solution.py:304
  7.3 0.1 add.21
  7.3 0.0 copy-start
  7.3 0.0 copy-start.1
  7.4 0.0 copy-start.2
  7.4 3.0 %collective-permute-start.2 = (f32[4,296,128]{2,1,0:T(8,128)S(1)}, f32[4,296,128]{2,1,0:T(8,128)S(1)}, u32[]{:S(2)}, u32[]{:S(2)}) collective-permute-start(f32[4,296,128]{2,1,0:T(8,128)S(1)} %add.21), channel_id=1, source_target_pairs={{0,2},{1,5},{2,0},{3,7},{4,6},{5,1},{6,4},{7,3},{8,10},{9,13},{10,... | collective-permute-start | bytes 1818632 | tf_op jit(solution)/shard_map/ppermute | solution.py:304
  10.3 4.4 %local_sums.3 = (f32[4,296,128]{2,1,0:T(8,128)S(1)}, f32[4,296,128]{2,1,0:T(8,128)S(1)}) custom-call(s32[16]{0:T(128)} %owners.4, bf16[8192,256]{1,0:T(8,128)(2,1)} %features.5, s32[8192]{0:T(1024)} %node_ids.5, s32[8192]{0:T(1024)} %labels.3), custom_call_target="tpu_custom_call" | custom-call | flops 536870912 | bytes 2097152 | tf_op jit(solution)/shard_map/local_sums/pallas_call | solution.py:131
  14.7 0.1 collective-permute-start.1
  14.8 3.6 %collective-permute-done.2 = f32[4,296,128]{2,1,0:T(8,128)S(1)} collective-permute-done((f32[4,296,128]{2,1,0:T(8,128)S(1)}, f32[4,296,128]{2,1,0:T(8,128)S(1)}, u32[]{:S(2)}, u32[]{:S(2)}) %collective-permute-start.2) | collective-permute-done | bytes 606240 | tf_op jit(solution)/shard_map/ppermute | solution.py:304
  18.4 0.0 collective-permute-done.1
  18.4 0.1 slice_add_fusion.2
  18.5 2.0 %collective-permute-start.3 = (f32[2,296,128]{2,1,0:T(8,128)S(1)}, f32[2,296,128]{2,1,0:T(8,128)S(1)}, u32[]{:S(2)}, u32[]{:S(2)}) collective-permute-start(f32[2,296,128]{2,1,0:T(8,128)S(1)} %get-tuple-element.19), channel_id=1, source_target_pairs={{0,4},{1,3},{2,6},{3,1},{4,0},{5,7},{6,2},{7,5},{8,12},{9,11},{10,... | collective-permute-start | bytes 909320 | tf_op jit(solution)/shard_map/ppermute | solution.py:304
  20.6 4.8 %collective-permute-done.3 = f32[2,296,128]{2,1,0:T(8,128)S(1)} collective-permute-done((f32[2,296,128]{2,1,0:T(8,128)S(1)}, f32[2,296,128]{2,1,0:T(8,128)S(1)}, u32[]{:S(2)}, u32[]{:S(2)}) %collective-permute-start.3) | collective-permute-done | bytes 303136 | tf_op jit(solution)/shard_map/ppermute | solution.py:304
  25.4 3.1 %collective-permute-start.4 = (f32[1,296,128]{2,1,0:T(8,128)S(1)}, f32[1,296,128]{2,1,0:T(8,128)S(1)}, u32[]{:S(2)}, u32[]{:S(2)}) collective-permute-start(f32[1,296,128]{2,1,0:T(8,128)S(1)} %get-tuple-element.20), channel_id=1, source_target_pairs={{0,8},{1,9},{2,10},{3,11},{4,12},{5,13},{6,14},{7,15},{8,0},{9,1},... | collective-permute-start | bytes 454664 | tf_op jit(solution)/shard_map/ppermute | solution.py:304
  28.6 5.8 %collective-permute-done.4.came = f32[1,296,128]{2,1,0:T(8,128)S(1)} collective-permute-done((f32[1,296,128]{2,1,0:T(8,128)S(1)}, f32[1,296,128]{2,1,0:T(8,128)S(1)}, u32[]{:S(2)}, u32[]{:S(2)}) %collective-permute-start.4) | collective-permute-done | bytes 151584 | tf_op jit(solution)/shard_map/ppermute | solution.py:304
  34.3 7.1 %solve.1 = (f32[1,16,256]{2,1,0:T(8,128)}, bf16[1,16,384]{2,1,0:T(8,128)(2,1)S(1)}) custom-call(f32[1,296,128]{2,1,0:T(8,128)S(1)} %get-tuple-element.21.kept, f32[1,296,128]{2,1,0:T(8,128)S(1)} %collective-permute-done.4.came), custom_call_target="tpu_custom_call" | custom-call | tf_op jit(solution)/shard_map/solve/pallas_call | solution.py:252
  41.5 0.4 collective-permute-start.5
  41.9 4.2 %collective-permute-done.5 = bf16[1,16,384]{2,1,0:T(8,128)(2,1)S(1)} collective-permute-done((bf16[1,16,384]{2,1,0:T(8,128)(2,1)S(1)}, bf16[1,16,384]{2,1,0:T(8,128)(2,1)S(1)}, u32[]{:S(2)}, u32[]{:S(2)}) %collective-permute-start.5) | collective-permute-done | bytes 12320 | tf_op jit(solution)/shard_map/ppermute | solution.py:304
  46.1 1.2 %collective-permute-start.6 = (bf16[2,16,384]{2,1,0:T(8,128)(2,1)S(1)}, bf16[2,16,384]{2,1,0:T(8,128)(2,1)S(1)}, u32[]{:S(2)}, u32[]{:S(2)}) collective-permute-start(bf16[2,16,384]{2,1,0:T(8,128)(2,1)S(1)} %pad_maximum_fusion.2), channel_id=1, source_target_pairs={{0,4},{1,3},{2,6},{3,1},{4,0},{5,7},{6,2},{7,5},{8,12},{9,11},{10,... | collective-permute-start | bytes 73736 | tf_op jit(solution)/shard_map/ppermute | solution.py:304
  47.3 2.7 %collective-permute-done.6 = bf16[2,16,384]{2,1,0:T(8,128)(2,1)S(1)} collective-permute-done((bf16[2,16,384]{2,1,0:T(8,128)(2,1)S(1)}, bf16[2,16,384]{2,1,0:T(8,128)(2,1)S(1)}, u32[]{:S(2)}, u32[]{:S(2)}) %collective-permute-start.6) | collective-permute-done | bytes 24608 | tf_op jit(solution)/shard_map/ppermute | solution.py:304
  50.0 1.8 %collective-permute-start.7 = (bf16[4,16,384]{2,1,0:T(8,128)(2,1)S(1)}, bf16[4,16,384]{2,1,0:T(8,128)(2,1)S(1)}, u32[]{:S(2)}, u32[]{:S(2)}) collective-permute-start(bf16[4,16,384]{2,1,0:T(8,128)(2,1)S(1)} %pad_maximum_fusion.1), channel_id=1, source_target_pairs={{0,2},{1,5},{2,0},{3,7},{4,6},{5,1},{6,4},{7,3},{8,10},{9,13},{10,... | collective-permute-start | bytes 147464 | tf_op jit(solution)/shard_map/ppermute | solution.py:304
  51.8 2.3 %collective-permute-done.7 = bf16[4,16,384]{2,1,0:T(8,128)(2,1)S(1)} collective-permute-done((bf16[4,16,384]{2,1,0:T(8,128)(2,1)S(1)}, bf16[4,16,384]{2,1,0:T(8,128)(2,1)S(1)}, u32[]{:S(2)}, u32[]{:S(2)}) %collective-permute-start.7) | collective-permute-done | bytes 49184 | tf_op jit(solution)/shard_map/ppermute | solution.py:304
  54.1 0.1 collective-permute-start.8
  54.2 1.3 %collective-permute-done.8 = bf16[8,16,384]{2,1,0:T(8,128)(2,1)S(1)} collective-permute-done((bf16[8,16,384]{2,1,0:T(8,128)(2,1)S(1)}, bf16[8,16,384]{2,1,0:T(8,128)(2,1)S(1)}, u32[]{:S(2)}, u32[]{:S(2)}) %collective-permute-start.8) | collective-permute-done | bytes 98336 | tf_op jit(solution)/shard_map/ppermute | solution.py:304
  55.5 0.0 copy-done
  55.5 0.0 copy-done.1
  55.5 0.0 copy-done.2
  55.5 2.6 %all_scores.1 = f32[16,8192]{1,0:T(8,128)} custom-call(s32[16]{0:T(128)S(1)} %copy-done.2, bf16[8192,256]{1,0:T(8,128)(2,1)S(1)} %copy-done, s32[8192]{0:T(1024)S(1)} %copy-done.1, bf16[16,16,384]{2,1,0:T(8,128)(2,1)S(1)} %constant_dynamic-update-slice_fusion.messages), custom_call_target="tpu_custom_call" | custom-call | tf_op jit(solution)/shard_map/all_scores/pallas_call | solution.py:287
  (9 shorter events, 0.1 us)
Async XLA Ops:
  5.1 2.2 %collective-permute-start = (f32[4,296,128]{2,1,0:T(8,128)S(1)}, f32[4,296,128]{2,1,0:T(8,128)S(1)}, u32[]{:S(2)}, u32[]{:S(2)}) collective-permute-start(f32[4,296,128]{2,1,0:T(8,128)S(1)} %get-tuple-element.11), channel_id=1, source_target_pairs={{0,1},{1,0},{2,3},{3,2},{4,5},{5,4},{6,7},{7,6},{8,9},{9,8},{10,11... | collective-permute-start | bytes 1818632 | tf_op jit(solution)/shard_map/ppermute | solution.py:304
  7.3 48.2 %copy-start = (bf16[8192,256]{1,0:T(8,128)(2,1)S(1)}, bf16[8192,256]{1,0:T(8,128)(2,1)}, u32[]{:S(2)}) copy-start(bf16[8192,256]{1,0:T(8,128)(2,1)} %features.5) | copy-start | bytes 12582916
  7.3 48.2 %copy-start.1 = (s32[8192]{0:T(1024)S(1)}, s32[8192]{0:T(1024)}, u32[]{:S(2)}) copy-start(s32[8192]{0:T(1024)} %node_ids.5) | copy-start | bytes 98308
  7.4 48.2 %copy-start.2 = (s32[16]{0:T(128)S(1)}, s32[16]{0:T(128)}, u32[]{:S(2)}) copy-start(s32[16]{0:T(128)} %owners.4) | copy-start | bytes 196
  7.4 11.0 %collective-permute-start.2 = (f32[4,296,128]{2,1,0:T(8,128)S(1)}, f32[4,296,128]{2,1,0:T(8,128)S(1)}, u32[]{:S(2)}, u32[]{:S(2)}) collective-permute-start(f32[4,296,128]{2,1,0:T(8,128)S(1)} %add.21), channel_id=1, source_target_pairs={{0,2},{1,5},{2,0},{3,7},{4,6},{5,1},{6,4},{7,3},{8,10},{9,13},{10,... | collective-permute-start | bytes 1818632 | tf_op jit(solution)/shard_map/ppermute | solution.py:304
  14.7 3.7 %collective-permute-start.1 = (f32[4,296,128]{2,1,0:T(8,128)S(1)}, f32[4,296,128]{2,1,0:T(8,128)S(1)}, u32[]{:S(2)}, u32[]{:S(2)}) collective-permute-start(f32[4,296,128]{2,1,0:T(8,128)S(1)} %get-tuple-element.14), channel_id=1, source_target_pairs={{0,1},{1,0},{2,3},{3,2},{4,5},{5,4},{6,7},{7,6},{8,9},{9,8},{10,11... | collective-permute-start | bytes 1818632 | tf_op jit(solution)/shard_map/ppermute | solution.py:304
  18.5 6.9 %collective-permute-start.3 = (f32[2,296,128]{2,1,0:T(8,128)S(1)}, f32[2,296,128]{2,1,0:T(8,128)S(1)}, u32[]{:S(2)}, u32[]{:S(2)}) collective-permute-start(f32[2,296,128]{2,1,0:T(8,128)S(1)} %get-tuple-element.19), channel_id=1, source_target_pairs={{0,4},{1,3},{2,6},{3,1},{4,0},{5,7},{6,2},{7,5},{8,12},{9,11},{10,... | collective-permute-start | bytes 909320 | tf_op jit(solution)/shard_map/ppermute | solution.py:304
  25.4 8.9 %collective-permute-start.4 = (f32[1,296,128]{2,1,0:T(8,128)S(1)}, f32[1,296,128]{2,1,0:T(8,128)S(1)}, u32[]{:S(2)}, u32[]{:S(2)}) collective-permute-start(f32[1,296,128]{2,1,0:T(8,128)S(1)} %get-tuple-element.20), channel_id=1, source_target_pairs={{0,8},{1,9},{2,10},{3,11},{4,12},{5,13},{6,14},{7,15},{8,0},{9,1},... | collective-permute-start | bytes 454664 | tf_op jit(solution)/shard_map/ppermute | solution.py:304
  41.5 4.6 %collective-permute-start.5 = (bf16[1,16,384]{2,1,0:T(8,128)(2,1)S(1)}, bf16[1,16,384]{2,1,0:T(8,128)(2,1)S(1)}, u32[]{:S(2)}, u32[]{:S(2)}) collective-permute-start(bf16[1,16,384]{2,1,0:T(8,128)(2,1)S(1)} %get-tuple-element.17), channel_id=1, source_target_pairs={{0,8},{1,9},{2,10},{3,11},{4,12},{5,13},{6,14},{7,15},{8,0},{9,1},... | collective-permute-start | bytes 36872 | tf_op jit(solution)/shard_map/ppermute | solution.py:304
  46.1 3.9 %collective-permute-start.6 = (bf16[2,16,384]{2,1,0:T(8,128)(2,1)S(1)}, bf16[2,16,384]{2,1,0:T(8,128)(2,1)S(1)}, u32[]{:S(2)}, u32[]{:S(2)}) collective-permute-start(bf16[2,16,384]{2,1,0:T(8,128)(2,1)S(1)} %pad_maximum_fusion.2), channel_id=1, source_target_pairs={{0,4},{1,3},{2,6},{3,1},{4,0},{5,7},{6,2},{7,5},{8,12},{9,11},{10,... | collective-permute-start | bytes 73736 | tf_op jit(solution)/shard_map/ppermute | solution.py:304
  50.0 4.2 %collective-permute-start.7 = (bf16[4,16,384]{2,1,0:T(8,128)(2,1)S(1)}, bf16[4,16,384]{2,1,0:T(8,128)(2,1)S(1)}, u32[]{:S(2)}, u32[]{:S(2)}) collective-permute-start(bf16[4,16,384]{2,1,0:T(8,128)(2,1)S(1)} %pad_maximum_fusion.1), channel_id=1, source_target_pairs={{0,2},{1,5},{2,0},{3,7},{4,6},{5,1},{6,4},{7,3},{8,10},{9,13},{10,... | collective-permute-start | bytes 147464 | tf_op jit(solution)/shard_map/ppermute | solution.py:304
  54.1 1.4 %collective-permute-start.8 = (bf16[8,16,384]{2,1,0:T(8,128)(2,1)S(1)}, bf16[8,16,384]{2,1,0:T(8,128)(2,1)S(1)}, u32[]{:S(2)}, u32[]{:S(2)}) collective-permute-start(bf16[8,16,384]{2,1,0:T(8,128)(2,1)S(1)} %pad_maximum_fusion), channel_id=1, source_target_pairs={{0,1},{1,0},{2,3},{3,2},{4,5},{5,4},{6,7},{7,6},{8,9},{9,8},{10,11... | collective-permute-start | bytes 294920 | tf_op jit(solution)/shard_map/ppermute | solution.py:304

commit v4 on v3

--- a/solution.py
+++ b/solution.py
@@ -69,85 +69,110 @@
     return moment[:half, half:], mixed, sums, tail
 
 
-def sums_kernel(
-    bits, group, owners, features, node_ids, labels, kept, sent, listed, rows, ids, marks, row_sems, id_sem, mark_sem
+def packed_shape(size, blocks):
+    return pltpu.VMEM((blocks, size + 2 * CLASSES + 8, size // 2), jnp.float32)
+
+
+def fill(out, section, listed, rows, ids, marks, segment):
+    blocks = out.shape[0]
+    size = rows.shape[1]
+    half = size // 2
+
+    def step(q, carry):
+        node = listed[section * blocks + q]
+        here = pl.ds(pl.multiple_of(node * segment, segment), segment)
+        alive = ids[here].reshape(1, segment) == node
+        cross, mixed, sums, tail = packed_sums(rows[here, :], alive, marks[here].reshape(1, segment))
+        out[q, 0:half] = cross
+        out[q, half:size] = mixed
+        out[q, size : size + CLASSES] = sums[:, :half]
+        out[q, size + CLASSES : size + 2 * CLASSES] = sums[:, half:]
+        out[q, size + 2 * CLASSES :] = tail
+        return carry
+
+    lax.fori_loop(0, blocks, step, 0)
+
+
+def first_sums_kernel(
+    bits, owners, features, node_ids, labels, sent, listed, rows, ids, marks, owner_list, row_sems, list_sem, id_sem, mark_sem
 ):
+    nodes = owners.shape[0]
+    segment = rows.shape[0] // nodes
+    quarter = nodes // 4
+    copies = [
+        pltpu.make_async_copy(owners, owner_list, list_sem),
+        pltpu.make_async_copy(node_ids, ids, id_sem),
+        pltpu.make_async_copy(labels, marks, mark_sem),
+    ]
+    for copy in copies:
+        copy.start()
+    for node in range(nodes):
+        part = pl.ds(node * segment, segment)
+        copies.append(pltpu.make_async_copy(features.at[part], rows.at[part], row_sems.at[node]))
+        copies[-1].start()
+    copies[0].wait()
     me = lax.axis_index("rows")
-    nodes = owners.shape[0]
-    count, segment, size = rows.shape
-    half = size // 2
-    copy_ids = pltpu.make_async_copy(node_ids, ids, id_sem)
-    copy_marks = pltpu.make_async_copy(labels, marks, mark_sem)
-    copy_ids.start()
-    copy_marks.start()
-
-    def segment_of(node):
-        return pl.ds(pl.multiple_of(node * segment, segment), segment)
-
-    def fetch(q, node):
-        return pltpu.make_async_copy(features.at[segment_of(node)], rows.at[q], row_sems.at[q])
-
     for node in range(nodes):
-        apart = owners[node] ^ me
-        place = place_of(apart, owners[node], bits)
-        slot = (place & (count // 2 - 1)) + (apart & 1) * (count // 2)
-
-        @pl.when((place >> (bits - 2)) == group)
-        def _(slot=slot, node=node):
-            listed[slot] = node
-            fetch(slot, node).start()
-
-    copy_ids.wait()
-    copy_marks.wait()
-
-    def fill(out, base):
-        def step(q, carry):
-            node = listed[base + q]
-            fetch(base + q, node).wait()
-            here = segment_of(node)
-            alive = ids[here].reshape(1, segment) == node
-            cross, mixed, sums, tail = packed_sums(rows[base + q], alive, marks[here].reshape(1, segment))
-            out[q, 0:half] = cross
-            out[q, half : 2 * half] = mixed
-            out[q, 2 * half : 2 * half + CLASSES] = sums[:, :half]
-            out[q, 2 * half + CLASSES : 2 * half + 2 * CLASSES] = sums[:, half:]
-            out[q, 2 * half + 2 * CLASSES :] = tail
-            return carry
-
-        lax.fori_loop(0, count // 2, step, 0)
-
-    fill(sent, count // 2)
-    fill(kept, 0)
-
-
-def local_sums(features, node_ids, labels, owners, bits, group):
+        owner = owner_list[node]
+        apart = owner ^ me
+        place = place_of(apart, owner, bits)
+        section = 3 - 2 * (place >> (bits - 2)) - (apart & 1)
+        listed[section * quarter + (place & (quarter - 1))] = node
+    for copy in copies[1:]:
+        copy.wait()
+    fill(sent, 0, listed, rows, ids, marks, segment)
+
+
+def first_sums(features, node_ids, labels, owners, bits):
     row_count, size = features.shape
     nodes = owners.shape[0]
-    segment = row_count // nodes
-    count = nodes // 2
-    out = pltpu.VMEM((count // 2, size + 2 * CLASSES + 8, size // 2), jnp.float32)
     far = pl.BlockSpec(memory_space=pltpu.HBM)
     near = pl.BlockSpec(memory_space=pltpu.VMEM)
+    words = pl.BlockSpec(memory_space=pltpu.SMEM)
     return pl.pallas_call(
-        functools.partial(sums_kernel, bits, group),
-        out_shape=(out, out),
-        in_specs=[pl.BlockSpec(memory_space=pltpu.SMEM), far, far, far],
-        out_specs=(near, near),
-        scratch_shapes=[
-            pltpu.SMEM((count,), jnp.int32),
-            pltpu.VMEM((count, segment, size), jnp.bfloat16),
+        functools.partial(first_sums_kernel, bits),
+        out_shape=(
+            packed_shape(size, nodes // 4),
+            pltpu.SMEM((nodes,), jnp.int32),
+            pltpu.VMEM((row_count, size), jnp.bfloat16),
             pltpu.VMEM((row_count,), jnp.int32),
             pltpu.VMEM((row_count,), jnp.int32),
-            pltpu.SemaphoreType.DMA((count,)),
+        ),
+        in_specs=[far] * 4,
+        out_specs=(near, words, near, near, near),
+        scratch_shapes=[
+            pltpu.SMEM((nodes,), jnp.int32),
+            pltpu.SemaphoreType.DMA((nodes,)),
+            pltpu.SemaphoreType.DMA,
             pltpu.SemaphoreType.DMA,
             pltpu.SemaphoreType.DMA,
         ],
         compiler_params=pltpu.CompilerParams(vmem_limit_bytes=32 << 20),
+        name="first_sums",
+    )(*(pltpu.with_memory_space_constraint(a, pltpu.HBM) for a in (owners, features, node_ids, labels)))
+
+
+def more_sums_kernel(sections, listed, rows, ids, marks, *outs):
+    segment = rows.shape[0] // listed.shape[0]
+    for section, out in zip(sections, outs):
+        fill(out, section, listed, rows, ids, marks, segment)
+
+
+def more_sums(sections, listed, rows, ids, marks):
+    row_count, size = rows.shape
+    nodes = listed.shape[0]
+    near = pl.BlockSpec(memory_space=pltpu.VMEM)
+    return pl.pallas_call(
+        functools.partial(more_sums_kernel, sections),
+        out_shape=tuple(packed_shape(size, nodes // 4) for _ in sections),
+        in_specs=[pl.BlockSpec(memory_space=pltpu.SMEM), near, near, near],
+        out_specs=tuple(near for _ in sections),
+        compiler_params=pltpu.CompilerParams(vmem_limit_bytes=32 << 20),
         cost_estimate=pl.CostEstimate(
-            flops=row_count * size * size, bytes_accessed=row_count * size, transcendentals=0
+            flops=row_count * size * size * len(sections) // 2, bytes_accessed=row_count * size, transcendentals=0
         ),
-        name="local_sums",
-    )(*(pltpu.with_memory_space_constraint(a, pltpu.HBM) for a in (owners, features, node_ids, labels)))
+        name="more_sums",
+    )(listed, rows, ids, marks)
 
 
 def sweep(matrix, size):
@@ -306,11 +331,13 @@
     def halving(x, step):
         return swap(x, [1 << order[step] for order in orders])
 
-    kept, sent = local_sums(features, node_ids, labels, owners, bits, 1)
-    sent = kept + swap(sent, (1, 1))
-    sent, later_owners = lax.optimization_barrier((sent, owners))
+    sent, listed, rows, ids, marks = first_sums(features, node_ids, labels, owners, bits)
+    came = swap(sent, (1, 1))
+    (kept,) = more_sums((1,), listed, rows, ids, marks)
+    sent = kept + came
+    sent, later_list = lax.optimization_barrier((sent, listed))
     came = halving(sent, 0)
-    kept, sent = local_sums(features, node_ids, labels, later_owners, bits, 0)
+    sent, kept = more_sums((2, 3), later_list, rows, ids, marks)
     kept = (kept, swap(sent, (1, 1)))
     for step in range(1, bits - 1):
         middle = came.shape[0] // 2
@@ -322,7 +349,7 @@
     for step in reversed(range(bits - 1)):
         held = jnp.concatenate([held, halving(held, step)], axis=0)
     held = jnp.concatenate([held, swap(held, (1, 1))], axis=0)
-    return planes, all_scores(features, node_ids, owners, held, bits)
+    return planes, all_scores(rows, ids, owners, held, bits)
 
 
 def solution(mesh):

time: 58.5 us -> 57.2 us (0.978)
  Pallas kernels: 18.6 us -> 16.6 us
  waiting for transfers between devices: 26.3 us -> 27.3 us
    pallas_call x2 -> x3, Pallas kernels: 8.83 us -> 6.87 us  [the longest x1 3.46 us: first_sums(): pl.pallas_call(functools.partial(first_sums_kernel, bits), out_shape=(pac...]
    ppermute x9, waiting for transfers between devices: 26.3 us -> 27.3 us  [swap(): lax.ppermute(x, 'rows', [(r, r ^ distances[r & 1]) for r in range(ranks)])]
  transfers between devices with their start and end apart: 9 -> 9, of which waited for: 8 -> 8; matrix products, arithmetic and copies ran while one was open for 0% -> 0% of each run, Pallas kernels for 8% -> 6%
where the time goes in v4:
time: 57.2 us; the launch traced here: 57.1 us
  waiting for transfers between devices  27.3 us (48%)
  Pallas kernels  16.6 us (29%)
  starting transfers between devices  12.2 us (21%)
  between operations  0.72 us (1%)
    ppermute x9, waiting for transfers between devices, swap(): lax.ppermute(x, 'rows', [(r, r ^ distances[r & 1]) for r in range(ranks)])  27.3 us
    ppermute x9, starting transfers between devices, swap(): lax.ppermute(x, 'rows', [(r, r ^ distances[r & 1]) for r in range(ranks)])  12.2 us
    pallas_call x1, Pallas kernels, solve(): pl.pallas_call(solve_kernel, out_shape=(jax.ShapeDtypeStruct((1, CLASSES,...  7.14 us
    pallas_call x1, Pallas kernels, first_sums(): pl.pallas_call(functools.partial(first_sums_kernel, bits), out_shape=(pac...  3.46 us
    pallas_call x2, Pallas kernels, more_sums(): pl.pallas_call(functools.partial(more_sums_kernel, sections), out_shape=t...  3.41 us
    pallas_call x1, Pallas kernels, all_scores(): pl.pallas_call(functools.partial(scores_kernel, bits, group), out_shape=j...  2.61 us
  transfers between devices with their start and end apart: 9, of which 8 were waited for; matrix products, arithmetic and copies ran while one was open for 0% of the time, Pallas kernels for 6%

profile of v4, /device:TPU:0, one launch (start us, length us, event | category | flops | bytes accessed | tf_op | source)
XLA Modules:
  0.0 57.1 jit_solution(16831798912671876175)
XLA Ops:
  0.6 3.5 %first_sums.1 = (f32[4,296,128]{2,1,0:T(8,128)S(1)}, s32[16]{0:T(128)S(4)}, bf16[8192,256]{1,0:T(8,128)(2,1)S(1)}, s32[8192]{0:T(1024)S(1)}, s32[8192]{0:T(1024)S(1)}) custom-call(s32[16]{0:T(128)} %owners.3, bf16[8192,256]{1,0:T(8,128)(2,1)} %features.1, s32[8192]{0:T(1024)} %node_ids.1, s32[8192]{0:T(1024)} %labels.1), custom_call_target="tpu_custom_call" | custom-call | tf_op jit(solution)/shard_map/first_sums/pallas_call | solution.py:132
  4.1 0.5 collective-permute-start
  4.6 1.1 %more_sums.2 = f32[4,296,128]{2,1,0:T(8,128)S(1)} custom-call(s32[16]{0:T(128)S(4)} %get-tuple-element.18.listed, bf16[8192,256]{1,0:T(8,128)(2,1)S(1)} %get-tuple-element.14.rows.features, s32[8192]{0:T(1024)S(1)} %get-tuple-element.15.ids.node_ids, s32[8192]{0:T(1024)S(1)} %get-tuple-element.16.marks), custom_call_target="tpu_custom_call" | custom-call | flops 268435456 | bytes 2097152 | tf_op jit(solution)/shard_map/more_sums/pallas_call | solution.py:165
  5.8 0.5 collective-permute-done
  6.3 0.1 add.21
  6.3 0.0 copy-start
  6.4 3.0 %collective-permute-start.2 = (f32[4,296,128]{2,1,0:T(8,128)S(1)}, f32[4,296,128]{2,1,0:T(8,128)S(1)}, u32[]{:S(2)}, u32[]{:S(2)}) collective-permute-start(f32[4,296,128]{2,1,0:T(8,128)S(1)} %add.21), channel_id=1, source_target_pairs={{0,2},{1,5},{2,0},{3,7},{4,6},{5,1},{6,4},{7,3},{8,10},{9,13},{10,... | collective-permute-start | bytes 1818632 | tf_op jit(solution)/shard_map/ppermute | solution.py:329
  9.3 2.3 %more_sums.3 = (f32[4,296,128]{2,1,0:T(8,128)S(1)}, f32[4,296,128]{2,1,0:T(8,128)S(1)}) custom-call(s32[16]{0:T(128)S(4)} %get-tuple-element.18.listed, bf16[8192,256]{1,0:T(8,128)(2,1)S(1)} %get-tuple-element.14.rows.features, s32[8192]{0:T(1024)S(1)} %get-tuple-element.15.ids.node_ids, s32[8192]{0:T(1024)S(1)} %get-tuple-element.16.marks), custom_call_target="tpu_custom_call" | custom-call | flops 536870912 | bytes 2097152 | tf_op jit(solution)/shard_map/more_sums/pallas_call | solution.py:165
  11.6 0.1 collective-permute-start.1
  11.7 5.7 %collective-permute-done.2 = f32[4,296,128]{2,1,0:T(8,128)S(1)} collective-permute-done((f32[4,296,128]{2,1,0:T(8,128)S(1)}, f32[4,296,128]{2,1,0:T(8,128)S(1)}, u32[]{:S(2)}, u32[]{:S(2)}) %collective-permute-start.2) | collective-permute-done | bytes 606240 | tf_op jit(solution)/shard_map/ppermute | solution.py:329
  17.3 0.0 collective-permute-done.1
  17.3 0.1 slice_add_fusion.2
  17.4 2.1 %collective-permute-start.3 = (f32[2,296,128]{2,1,0:T(8,128)S(1)}, f32[2,296,128]{2,1,0:T(8,128)S(1)}, u32[]{:S(2)}, u32[]{:S(2)}) collective-permute-start(f32[2,296,128]{2,1,0:T(8,128)S(1)} %get-tuple-element.25), channel_id=1, source_target_pairs={{0,4},{1,3},{2,6},{3,1},{4,0},{5,7},{6,2},{7,5},{8,12},{9,11},{10,... | collective-permute-start | bytes 909320 | tf_op jit(solution)/shard_map/ppermute | solution.py:329
  19.6 4.8 %collective-permute-done.3 = f32[2,296,128]{2,1,0:T(8,128)S(1)} collective-permute-done((f32[2,296,128]{2,1,0:T(8,128)S(1)}, f32[2,296,128]{2,1,0:T(8,128)S(1)}, u32[]{:S(2)}, u32[]{:S(2)}) %collective-permute-start.3) | collective-permute-done | bytes 303136 | tf_op jit(solution)/shard_map/ppermute | solution.py:329
  24.4 3.1 %collective-permute-start.4 = (f32[1,296,128]{2,1,0:T(8,128)S(1)}, f32[1,296,128]{2,1,0:T(8,128)S(1)}, u32[]{:S(2)}, u32[]{:S(2)}) collective-permute-start(f32[1,296,128]{2,1,0:T(8,128)S(1)} %get-tuple-element.26), channel_id=1, source_target_pairs={{0,8},{1,9},{2,10},{3,11},{4,12},{5,13},{6,14},{7,15},{8,0},{9,1},... | collective-permute-start | bytes 454664 | tf_op jit(solution)/shard_map/ppermute | solution.py:329
  27.5 5.8 %collective-permute-done.4.came = f32[1,296,128]{2,1,0:T(8,128)S(1)} collective-permute-done((f32[1,296,128]{2,1,0:T(8,128)S(1)}, f32[1,296,128]{2,1,0:T(8,128)S(1)}, u32[]{:S(2)}, u32[]{:S(2)}) %collective-permute-start.4) | collective-permute-done | bytes 151584 | tf_op jit(solution)/shard_map/ppermute | solution.py:329
  33.3 7.1 %solve.1 = (f32[1,16,256]{2,1,0:T(8,128)}, bf16[1,16,384]{2,1,0:T(8,128)(2,1)S(1)}) custom-call(f32[1,296,128]{2,1,0:T(8,128)S(1)} %get-tuple-element.27.kept, f32[1,296,128]{2,1,0:T(8,128)S(1)} %collective-permute-done.4.came), custom_call_target="tpu_custom_call" | custom-call | tf_op jit(solution)/shard_map/solve/pallas_call | solution.py:277
  40.4 0.4 collective-permute-start.5
  40.8 4.2 %collective-permute-done.5 = bf16[1,16,384]{2,1,0:T(8,128)(2,1)S(1)} collective-permute-done((bf16[1,16,384]{2,1,0:T(8,128)(2,1)S(1)}, bf16[1,16,384]{2,1,0:T(8,128)(2,1)S(1)}, u32[]{:S(2)}, u32[]{:S(2)}) %collective-permute-start.5) | collective-permute-done | bytes 12320 | tf_op jit(solution)/shard_map/ppermute | solution.py:329
  45.0 1.2 %collective-permute-start.6 = (bf16[2,16,384]{2,1,0:T(8,128)(2,1)S(1)}, bf16[2,16,384]{2,1,0:T(8,128)(2,1)S(1)}, u32[]{:S(2)}, u32[]{:S(2)}) collective-permute-start(bf16[2,16,384]{2,1,0:T(8,128)(2,1)S(1)} %pad_maximum_fusion.2), channel_id=1, source_target_pairs={{0,4},{1,3},{2,6},{3,1},{4,0},{5,7},{6,2},{7,5},{8,12},{9,11},{10,... | collective-permute-start | bytes 73736 | tf_op jit(solution)/shard_map/ppermute | solution.py:329
  46.2 2.7 %collective-permute-done.6 = bf16[2,16,384]{2,1,0:T(8,128)(2,1)S(1)} collective-permute-done((bf16[2,16,384]{2,1,0:T(8,128)(2,1)S(1)}, bf16[2,16,384]{2,1,0:T(8,128)(2,1)S(1)}, u32[]{:S(2)}, u32[]{:S(2)}) %collective-permute-start.6) | collective-permute-done | bytes 24608 | tf_op jit(solution)/shard_map/ppermute | solution.py:329
  48.9 1.7 %collective-permute-start.7 = (bf16[4,16,384]{2,1,0:T(8,128)(2,1)S(1)}, bf16[4,16,384]{2,1,0:T(8,128)(2,1)S(1)}, u32[]{:S(2)}, u32[]{:S(2)}) collective-permute-start(bf16[4,16,384]{2,1,0:T(8,128)(2,1)S(1)} %pad_maximum_fusion.1), channel_id=1, source_target_pairs={{0,2},{1,5},{2,0},{3,7},{4,6},{5,1},{6,4},{7,3},{8,10},{9,13},{10,... | collective-permute-start | bytes 147464 | tf_op jit(solution)/shard_map/ppermute | solution.py:329
  50.6 2.4 %collective-permute-done.7 = bf16[4,16,384]{2,1,0:T(8,128)(2,1)S(1)} collective-permute-done((bf16[4,16,384]{2,1,0:T(8,128)(2,1)S(1)}, bf16[4,16,384]{2,1,0:T(8,128)(2,1)S(1)}, u32[]{:S(2)}, u32[]{:S(2)}) %collective-permute-start.7) | collective-permute-done | bytes 49184 | tf_op jit(solution)/shard_map/ppermute | solution.py:329
  53.1 0.1 collective-permute-start.8
  53.1 1.3 %collective-permute-done.8 = bf16[8,16,384]{2,1,0:T(8,128)(2,1)S(1)} collective-permute-done((bf16[8,16,384]{2,1,0:T(8,128)(2,1)S(1)}, bf16[8,16,384]{2,1,0:T(8,128)(2,1)S(1)}, u32[]{:S(2)}, u32[]{:S(2)}) %collective-permute-start.8) | collective-permute-done | bytes 98336 | tf_op jit(solution)/shard_map/ppermute | solution.py:329
  54.4 0.0 copy-done
  54.4 2.6 %all_scores.1 = f32[16,8192]{1,0:T(8,128)} custom-call(s32[16]{0:T(128)S(1)} %copy-done, bf16[8192,256]{1,0:T(8,128)(2,1)S(1)} %get-tuple-element.14.rows.features, s32[8192]{0:T(1024)S(1)} %get-tuple-element.15.ids.node_ids, bf16[16,16,384]{2,1,0:T(8,128)(2,1)S(1)} %constant_dynamic-update-slice_fusion.messages), custom_call_target="tpu_custom_call" | custom-call | tf_op jit(solution)/shard_map/all_scores/pallas_call | solution.py:312
  (9 shorter events, 0.1 us)
Async XLA Ops:
  4.1 2.2 %collective-permute-start = (f32[4,296,128]{2,1,0:T(8,128)S(1)}, f32[4,296,128]{2,1,0:T(8,128)S(1)}, u32[]{:S(2)}, u32[]{:S(2)}) collective-permute-start(f32[4,296,128]{2,1,0:T(8,128)S(1)} %get-tuple-element.17), channel_id=1, source_target_pairs={{0,1},{1,0},{2,3},{3,2},{4,5},{5,4},{6,7},{7,6},{8,9},{9,8},{10,11... | collective-permute-start | bytes 1818632 | tf_op jit(solution)/shard_map/ppermute | solution.py:329
  6.3 48.1 %copy-start = (s32[16]{0:T(128)S(1)}, s32[16]{0:T(128)}, u32[]{:S(2)}) copy-start(s32[16]{0:T(128)} %owners.3) | copy-start | bytes 196
  6.4 11.0 %collective-permute-start.2 = (f32[4,296,128]{2,1,0:T(8,128)S(1)}, f32[4,296,128]{2,1,0:T(8,128)S(1)}, u32[]{:S(2)}, u32[]{:S(2)}) collective-permute-start(f32[4,296,128]{2,1,0:T(8,128)S(1)} %add.21), channel_id=1, source_target_pairs={{0,2},{1,5},{2,0},{3,7},{4,6},{5,1},{6,4},{7,3},{8,10},{9,13},{10,... | collective-permute-start | bytes 1818632 | tf_op jit(solution)/shard_map/ppermute | solution.py:329
  11.6 5.8 %collective-permute-start.1 = (f32[4,296,128]{2,1,0:T(8,128)S(1)}, f32[4,296,128]{2,1,0:T(8,128)S(1)}, u32[]{:S(2)}, u32[]{:S(2)}) collective-permute-start(f32[4,296,128]{2,1,0:T(8,128)S(1)} %get-tuple-element.20), channel_id=1, source_target_pairs={{0,1},{1,0},{2,3},{3,2},{4,5},{5,4},{6,7},{7,6},{8,9},{9,8},{10,11... | collective-permute-start | bytes 1818632 | tf_op jit(solution)/shard_map/ppermute | solution.py:329
  17.4 6.9 %collective-permute-start.3 = (f32[2,296,128]{2,1,0:T(8,128)S(1)}, f32[2,296,128]{2,1,0:T(8,128)S(1)}, u32[]{:S(2)}, u32[]{:S(2)}) collective-permute-start(f32[2,296,128]{2,1,0:T(8,128)S(1)} %get-tuple-element.25), channel_id=1, source_target_pairs={{0,4},{1,3},{2,6},{3,1},{4,0},{5,7},{6,2},{7,5},{8,12},{9,11},{10,... | collective-permute-start | bytes 909320 | tf_op jit(solution)/shard_map/ppermute | solution.py:329
  24.4 8.9 %collective-permute-start.4 = (f32[1,296,128]{2,1,0:T(8,128)S(1)}, f32[1,296,128]{2,1,0:T(8,128)S(1)}, u32[]{:S(2)}, u32[]{:S(2)}) collective-permute-start(f32[1,296,128]{2,1,0:T(8,128)S(1)} %get-tuple-element.26), channel_id=1, source_target_pairs={{0,8},{1,9},{2,10},{3,11},{4,12},{5,13},{6,14},{7,15},{8,0},{9,1},... | collective-permute-start | bytes 454664 | tf_op jit(solution)/shard_map/ppermute | solution.py:329
  40.4 4.6 %collective-permute-start.5 = (bf16[1,16,384]{2,1,0:T(8,128)(2,1)S(1)}, bf16[1,16,384]{2,1,0:T(8,128)(2,1)S(1)}, u32[]{:S(2)}, u32[]{:S(2)}) collective-permute-start(bf16[1,16,384]{2,1,0:T(8,128)(2,1)S(1)} %get-tuple-element.23), channel_id=1, source_target_pairs={{0,8},{1,9},{2,10},{3,11},{4,12},{5,13},{6,14},{7,15},{8,0},{9,1},... | collective-permute-start | bytes 36872 | tf_op jit(solution)/shard_map/ppermute | solution.py:329
  45.0 3.8 %collective-permute-start.6 = (bf16[2,16,384]{2,1,0:T(8,128)(2,1)S(1)}, bf16[2,16,384]{2,1,0:T(8,128)(2,1)S(1)}, u32[]{:S(2)}, u32[]{:S(2)}) collective-permute-start(bf16[2,16,384]{2,1,0:T(8,128)(2,1)S(1)} %pad_maximum_fusion.2), channel_id=1, source_target_pairs={{0,4},{1,3},{2,6},{3,1},{4,0},{5,7},{6,2},{7,5},{8,12},{9,11},{10,... | collective-permute-start | bytes 73736 | tf_op jit(solution)/shard_map/ppermute | solution.py:329
  48.9 4.2 %collective-permute-start.7 = (bf16[4,16,384]{2,1,0:T(8,128)(2,1)S(1)}, bf16[4,16,384]{2,1,0:T(8,128)(2,1)S(1)}, u32[]{:S(2)}, u32[]{:S(2)}) collective-permute-start(bf16[4,16,384]{2,1,0:T(8,128)(2,1)S(1)} %pad_maximum_fusion.1), channel_id=1, source_target_pairs={{0,2},{1,5},{2,0},{3,7},{4,6},{5,1},{6,4},{7,3},{8,10},{9,13},{10,... | collective-permute-start | bytes 147464 | tf_op jit(solution)/shard_map/ppermute | solution.py:329
  53.1 1.4 %collective-permute-start.8 = (bf16[8,16,384]{2,1,0:T(8,128)(2,1)S(1)}, bf16[8,16,384]{2,1,0:T(8,128)(2,1)S(1)}, u32[]{:S(2)}, u32[]{:S(2)}) collective-permute-start(bf16[8,16,384]{2,1,0:T(8,128)(2,1)S(1)} %pad_maximum_fusion), channel_id=1, source_target_pairs={{0,1},{1,0},{2,3},{3,2},{4,5},{5,4},{6,7},{7,6},{8,9},{9,8},{10,11... | collective-permute-start | bytes 294920 | tf_op jit(solution)/shard_map/ppermute | solution.py:329

commit v5 on v4

--- a/solution.py
+++ b/solution.py
@@ -73,16 +73,18 @@
     return pltpu.VMEM((blocks, size + 2 * CLASSES + 8, size // 2), jnp.float32)
 
 
-def fill(out, section, listed, rows, ids, marks, segment):
-    blocks = out.shape[0]
-    size = rows.shape[1]
+def fill(out, first, row_first, listed, rows, ids, marks, ready=None):
+    size = rows.shape[2]
+    segment = rows.shape[1]
     half = size // 2
 
     def step(q, carry):
-        node = listed[section * blocks + q]
+        node = listed[first + q]
+        if ready is not None:
+            ready(first + q)
         here = pl.ds(pl.multiple_of(node * segment, segment), segment)
         alive = ids[here].reshape(1, segment) == node
-        cross, mixed, sums, tail = packed_sums(rows[here, :], alive, marks[here].reshape(1, segment))
+        cross, mixed, sums, tail = packed_sums(rows[row_first + q], alive, marks[here].reshape(1, segment))
         out[q, 0:half] = cross
         out[q, half:size] = mixed
         out[q, size : size + CLASSES] = sums[:, :half]
@@ -90,15 +92,21 @@
         out[q, size + 2 * CLASSES :] = tail
         return carry
 
-    lax.fori_loop(0, blocks, step, 0)
+    lax.fori_loop(0, out.shape[0], step, 0)
+
+
+def row_copy(features, rows, sems, listed, first, position):
+    segment = rows.shape[1]
+    start = pl.multiple_of(listed[position] * segment, segment)
+    slot = position - first
+    return pltpu.make_async_copy(features.at[pl.ds(start, segment)], rows.at[slot], sems.at[slot])
 
 
 def first_sums_kernel(
     bits, owners, features, node_ids, labels, sent, listed, rows, ids, marks, owner_list, row_sems, list_sem, id_sem, mark_sem
 ):
     nodes = owners.shape[0]
-    segment = rows.shape[0] // nodes
-    quarter = nodes // 4
+    blocks = sent.shape[0]
     copies = [
         pltpu.make_async_copy(owners, owner_list, list_sem),
         pltpu.make_async_copy(node_ids, ids, id_sem),
@@ -106,21 +114,34 @@
     ]
     for copy in copies:
         copy.start()
-    for node in range(nodes):
-        part = pl.ds(node * segment, segment)
-        copies.append(pltpu.make_async_copy(features.at[part], rows.at[part], row_sems.at[node]))
-        copies[-1].start()
     copies[0].wait()
     me = lax.axis_index("rows")
     for node in range(nodes):
         owner = owner_list[node]
         apart = owner ^ me
         place = place_of(apart, owner, bits)
-        section = 3 - 2 * (place >> (bits - 2)) - (apart & 1)
-        listed[section * quarter + (place & (quarter - 1))] = node
+        chunk = 7 - 2 * (place >> (bits - 3)) - (apart & 1)
+        listed[chunk * blocks + (place & (blocks - 1))] = node
+    for position in range(nodes // 2):
+        row_copy(features, rows, row_sems, listed, 0, position).start()
     for copy in copies[1:]:
         copy.wait()
-    fill(sent, 0, listed, rows, ids, marks, segment)
+
+    def ready(position):
+        row_copy(features, rows, row_sems, listed, 0, position).wait()
+
+    fill(sent, 0, 0, listed, rows, ids, marks, ready)
+    for position in range(blocks, nodes // 2):
+        ready(position)
+
+
+def hbm(x):
+    return pltpu.with_memory_space_constraint(x, pltpu.HBM)
+
+
+def half_rows(features, nodes):
+    row_count, size = features.shape
+    return pltpu.VMEM((nodes // 2, row_count // nodes, size), features.dtype)
 
 
 def first_sums(features, node_ids, labels, owners, bits):
@@ -132,9 +153,9 @@
     return pl.pallas_call(
         functools.partial(first_sums_kernel, bits),
         out_shape=(
-            packed_shape(size, nodes // 4),
+            packed_shape(size, nodes // 8),
             pltpu.SMEM((nodes,), jnp.int32),
-            pltpu.VMEM((row_count, size), jnp.bfloat16),
+            half_rows(features, nodes),
             pltpu.VMEM((row_count,), jnp.int32),
             pltpu.VMEM((row_count,), jnp.int32),
         ),
@@ -142,35 +163,72 @@
         out_specs=(near, words, near, near, near),
         scratch_shapes=[
             pltpu.SMEM((nodes,), jnp.int32),
-            pltpu.SemaphoreType.DMA((nodes,)),
+            pltpu.SemaphoreType.DMA((nodes // 2,)),
             pltpu.SemaphoreType.DMA,
             pltpu.SemaphoreType.DMA,
             pltpu.SemaphoreType.DMA,
         ],
         compiler_params=pltpu.CompilerParams(vmem_limit_bytes=32 << 20),
         name="first_sums",
-    )(*(pltpu.with_memory_space_constraint(a, pltpu.HBM) for a in (owners, features, node_ids, labels)))
-
-
-def more_sums_kernel(sections, listed, rows, ids, marks, *outs):
-    segment = rows.shape[0] // listed.shape[0]
-    for section, out in zip(sections, outs):
-        fill(out, section, listed, rows, ids, marks, segment)
-
-
-def more_sums(sections, listed, rows, ids, marks):
-    row_count, size = rows.shape
+    )(hbm(owners), hbm(features), hbm(node_ids), hbm(labels))
+
+
+def loading_sums_kernel(listed, features, rows, ids, marks, early, late, later_rows, row_sems):
+    nodes = listed.shape[0]
+    blocks = early.shape[0]
+    middle = nodes // 2
+    for position in range(middle, nodes):
+        row_copy(features, later_rows, row_sems, listed, middle, position).start()
+    fill(early, 3 * blocks, 3 * blocks, listed, rows, ids, marks)
+
+    def ready(position):
+        row_copy(features, later_rows, row_sems, listed, middle, position).wait()
+
+    fill(late, 4 * blocks, 0, listed, later_rows, ids, marks, ready)
+    for position in range(middle + blocks, nodes):
+        ready(position)
+
+
+def loading_sums(features, listed, rows, ids, marks):
+    size = features.shape[1]
     nodes = listed.shape[0]
     near = pl.BlockSpec(memory_space=pltpu.VMEM)
     return pl.pallas_call(
-        functools.partial(more_sums_kernel, sections),
-        out_shape=tuple(packed_shape(size, nodes // 4) for _ in sections),
+        loading_sums_kernel,
+        out_shape=(packed_shape(size, nodes // 8),) * 2 + (half_rows(features, nodes),),
+        in_specs=[pl.BlockSpec(memory_space=pltpu.SMEM), pl.BlockSpec(memory_space=pltpu.HBM), near, near, near],
+        out_specs=(near, near, near),
+        scratch_shapes=[pltpu.SemaphoreType.DMA((nodes // 2,))],
+        compiler_params=pltpu.CompilerParams(vmem_limit_bytes=32 << 20),
+        cost_estimate=sums_cost(features.shape, 2),
+        name="loading_sums",
+    )(listed, hbm(features), rows, ids, marks)
+
+
+def sums_cost(shape, chunks):
+    row_count, size = shape
+    return pl.CostEstimate(
+        flops=row_count * size * size * chunks // 4, bytes_accessed=row_count * size * chunks // 4, transcendentals=0
+    )
+
+
+def more_sums_kernel(chunks, listed, rows, ids, marks, *outs):
+    for chunk, out in zip(chunks, outs):
+        blocks = out.shape[0]
+        fill(out, chunk * blocks, chunk * blocks % rows.shape[0], listed, rows, ids, marks)
+
+
+def more_sums(chunks, listed, rows, ids, marks):
+    size = rows.shape[2]
+    nodes = listed.shape[0]
+    near = pl.BlockSpec(memory_space=pltpu.VMEM)
+    return pl.pallas_call(
+        functools.partial(more_sums_kernel, chunks),
+        out_shape=(packed_shape(size, nodes // 8),) * len(chunks),
         in_specs=[pl.BlockSpec(memory_space=pltpu.SMEM), near, near, near],
-        out_specs=tuple(near for _ in sections),
+        out_specs=(near,) * len(chunks),
         compiler_params=pltpu.CompilerParams(vmem_limit_bytes=32 << 20),
-        cost_estimate=pl.CostEstimate(
-            flops=row_count * size * size * len(sections) // 2, bytes_accessed=row_count * size, transcendentals=0
-        ),
+        cost_estimate=sums_cost((ids.shape[0], size), len(chunks)),
         name="more_sums",
     )(listed, rows, ids, marks)
 
@@ -331,15 +389,23 @@
     def halving(x, step):
         return swap(x, [1 << order[step] for order in orders])
 
-    sent, listed, rows, ids, marks = first_sums(features, node_ids, labels, owners, bits)
-    came = swap(sent, (1, 1))
-    (kept,) = more_sums((1,), listed, rows, ids, marks)
-    sent = kept + came
-    sent, later_list = lax.optimization_barrier((sent, listed))
-    came = halving(sent, 0)
-    sent, kept = more_sums((2, 3), later_list, rows, ids, marks)
-    kept = (kept, swap(sent, (1, 1)))
-    for step in range(1, bits - 1):
+    sent_a, listed, rows, ids, marks = first_sums(features, node_ids, labels, owners, bits)
+    came_a = swap(sent_a, (1, 1))
+    kept_a, sent_b = more_sums((1, 2), listed, rows, ids, marks)
+    came_b = swap(sent_b, (1, 1))
+    sent_a, listed = lax.optimization_barrier((kept_a + came_a, listed))
+    came_a = halving(sent_a, 0)
+    kept_b, next_a, rows_later = loading_sums(features, listed, rows, ids, marks)
+    next_a = swap(next_a, (1, 1))
+    sent_b, listed = lax.optimization_barrier((kept_b + came_b, listed))
+    came_b = halving(sent_b, 0)
+    (kept_a,) = more_sums((5,), listed, rows_later, ids, marks)
+    sent_a, listed = lax.optimization_barrier((kept_a + next_a + came_a, listed))
+    came = halving(sent_a, 1)
+    next_b, kept_b = more_sums((6, 7), listed, rows_later, ids, marks)
+    next_b = swap(next_b, (1, 1))
+    kept = (kept_b, next_b, came_b)
+    for step in range(2, bits - 1):
         middle = came.shape[0] // 2
         sent = sum(k[middle:] for k in kept) + came[middle:]
         next_came = halving(sent, step)
@@ -349,7 +415,7 @@
     for step in reversed(range(bits - 1)):
         held = jnp.concatenate([held, halving(held, step)], axis=0)
     held = jnp.concatenate([held, swap(held, (1, 1))], axis=0)
-    return planes, all_scores(rows, ids, owners, held, bits)
+    return planes, all_scores(features, ids, owners, held, bits)
 
 
 def solution(mesh):

time: 57.2 us -> 55.2 us (0.965)
  waiting for transfers between devices: 27.3 us -> 24 us
  starting transfers between devices: 12.2 us -> 13.2 us
    ppermute x9 -> x12, waiting for transfers between devices: 27.3 us -> 24 us  [swap(): lax.ppermute(x, 'rows', [(r, r ^ distances[r & 1]) for r in range(ranks)])]
    pallas_call x1, Pallas kernels: 3.46 us -> 2.44 us  [first_sums(): pl.pallas_call(functools.partial(first_sums_kernel, bits), out_shape=(pac...]
    pallas_call x2 -> x4, Pallas kernels: 3.41 us -> 4.43 us  [the longest x3 2.84 us: more_sums(): pl.pallas_call(functools.partial(more_sums_kernel, chunks), out_shape=(pa...]
    ppermute x9 -> x12, starting transfers between devices: 12.2 us -> 13.2 us  [swap(): lax.ppermute(x, 'rows', [(r, r ^ distances[r & 1]) for r in range(ranks)])]
  transfers between devices with their start and end apart: 9 -> 12, of which waited for: 8 -> 8; matrix products, arithmetic and copies ran while one was open for 0% -> 0% of each run, Pallas kernels for 6% -> 8%
where the time goes in v5:
time: 55.2 us; the launch traced here: 55 us
  waiting for transfers between devices  24 us (43%)
  Pallas kernels  16.6 us (30%)
  starting transfers between devices  13.2 us (24%)
  between operations  0.77 us (1%)
    ppermute x12, waiting for transfers between devices, swap(): lax.ppermute(x, 'rows', [(r, r ^ distances[r & 1]) for r in range(ranks)])  24 us
    ppermute x12, starting transfers between devices, swap(): lax.ppermute(x, 'rows', [(r, r ^ distances[r & 1]) for r in range(ranks)])  13.2 us
    pallas_call x1, Pallas kernels, solve(): pl.pallas_call(solve_kernel, out_shape=(jax.ShapeDtypeStruct((1, CLASSES,...  7.14 us
    pallas_call x3, Pallas kernels, more_sums(): pl.pallas_call(functools.partial(more_sums_kernel, chunks), out_shape=(pa...  2.84 us
    pallas_call x1, Pallas kernels, all_scores(): pl.pallas_call(functools.partial(scores_kernel, bits, group), out_shape=j...  2.61 us
    pallas_call x1, Pallas kernels, first_sums(): pl.pallas_call(functools.partial(first_sums_kernel, bits), out_shape=(pac...  2.44 us
    pallas_call x1, Pallas kernels, loading_sums(): pl.pallas_call(loading_sums_kernel, out_shape=(packed_shape(size, nodes /...  1.6 us
  transfers between devices with their start and end apart: 12, of which 8 were waited for; matrix products, arithmetic and copies ran while one was open for 0% of the time, Pallas kernels for 8%

profile of v5, /device:TPU:0, one launch (start us, length us, event | category | flops | bytes accessed | tf_op | source)
XLA Modules:
  0.0 55.0 jit_solution(2466889982651752377)
XLA Ops:
  0.6 2.4 %first_sums.1 = (f32[2,296,128]{2,1,0:T(8,128)S(1)}, s32[16]{0:T(128)S(4)}, bf16[8,512,256]{2,1,0:T(8,128)(2,1)S(1)}, s32[8192]{0:T(1024)S(1)}, s32[8192]{0:T(1024)S(1)}) custom-call(s32[16]{0:T(128)} %owners.3, bf16[8192,256]{1,0:T(8,128)(2,1)} %features.5, s32[8192]{0:T(1024)} %node_ids.1, s32[8192]{0:T(1024)} %labels.1), custom_call_target="tpu_custom_call" | custom-call | tf_op jit(solution)/shard_map/first_sums/pallas_call | solution.py:153
  3.1 0.5 collective-permute-start
  3.6 1.1 %more_sums.3 = (f32[2,296,128]{2,1,0:T(8,128)S(1)}, f32[2,296,128]{2,1,0:T(8,128)S(1)}) custom-call(s32[16]{0:T(128)S(4)} %get-tuple-element.35.listed, bf16[8,512,256]{2,1,0:T(8,128)(2,1)S(1)} %get-tuple-element.23.rows, s32[8192]{0:T(1024)S(1)} %get-tuple-element.24.ids.node_ids, s32[8192]{0:T(1024)S(1)} %get-tuple-element.25.marks), custom_call_target="tpu_custom_call" | custom-call | flops 268435456 | bytes 1048576 | tf_op jit(solution)/shard_map/more_sums/pallas_call | solution.py:225
  4.7 0.1 collective-permute-start.1
  4.9 0.0 collective-permute-done
  4.9 3.0 %collective-permute-start.3 = (f32[2,296,128]{2,1,0:T(8,128)S(1)}, f32[2,296,128]{2,1,0:T(8,128)S(1)}, u32[]{:S(2)}, u32[]{:S(2)}) collective-permute-start(f32[2,296,128]{2,1,0:T(8,128)S(1)} %add.30), channel_id=1, source_target_pairs={{0,2},{1,5},{2,0},{3,7},{4,6},{5,1},{6,4},{7,3},{8,10},{9,13},{10,... | collective-permute-start | bytes 909320 | tf_op jit(solution)/shard_map/ppermute | solution.py:387
  7.9 1.6 %loading_sums.1 = (f32[2,296,128]{2,1,0:T(8,128)S(1)}, f32[2,296,128]{2,1,0:T(8,128)S(1)}, bf16[8,512,256]{2,1,0:T(8,128)(2,1)S(1)}) custom-call(s32[16]{0:T(128)S(4)} %get-tuple-element.35.listed, bf16[8192,256]{1,0:T(8,128)(2,1)} %features.5, bf16[8,512,256]{2,1,0:T(8,128)(2,1)S(1)} %get-tuple-element.23.rows, s32[8192]{0:T(1024)S(1)} %get-tuple-element.24.ids.node_ids, ...), custom_call_target="tpu_custom_call" | custom-call | flops 268435456 | bytes 1048576 | tf_op jit(solution)/shard_map/loading_sums/pallas_call | solution.py:196
  9.5 0.1 collective-permute-start.2
  9.6 0.0 collective-permute-done.1
  9.7 1.4 %collective-permute-start.5 = (f32[2,296,128]{2,1,0:T(8,128)S(1)}, f32[2,296,128]{2,1,0:T(8,128)S(1)}, u32[]{:S(2)}, u32[]{:S(2)}) collective-permute-start(f32[2,296,128]{2,1,0:T(8,128)S(1)} %add.31), channel_id=1, source_target_pairs={{0,2},{1,5},{2,0},{3,7},{4,6},{5,1},{6,4},{7,3},{8,10},{9,13},{10,... | collective-permute-start | bytes 909320 | tf_op jit(solution)/shard_map/ppermute | solution.py:387
  11.0 0.6 %more_sums.4 = f32[2,296,128]{2,1,0:T(8,128)S(1)} custom-call(s32[16]{0:T(128)S(4)} %get-tuple-element.35.listed, bf16[8,512,256]{2,1,0:T(8,128)(2,1)S(1)} %get-tuple-element.32.rows, s32[8192]{0:T(1024)S(1)} %get-tuple-element.24.ids.node_ids, s32[8192]{0:T(1024)S(1)} %get-tuple-element.25.marks), custom_call_target="tpu_custom_call" | custom-call | flops 134217728 | bytes 524288 | tf_op jit(solution)/shard_map/more_sums/pallas_call | solution.py:225
  11.6 1.1 %collective-permute-done.3 = f32[2,296,128]{2,1,0:T(8,128)S(1)} collective-permute-done((f32[2,296,128]{2,1,0:T(8,128)S(1)}, f32[2,296,128]{2,1,0:T(8,128)S(1)}, u32[]{:S(2)}, u32[]{:S(2)}) %collective-permute-start.3) | collective-permute-done | bytes 303136 | tf_op jit(solution)/shard_map/ppermute | solution.py:387
  12.7 0.0 collective-permute-done.2
  12.7 0.1 add_add_fusion
  12.8 0.0 copy-start
  12.8 0.0 copy-start.1
  12.8 1.1 %more_sums.5 = (f32[2,296,128]{2,1,0:T(8,128)S(1)}, f32[2,296,128]{2,1,0:T(8,128)S(1)}) custom-call(s32[16]{0:T(128)S(4)} %get-tuple-element.35.listed, bf16[8,512,256]{2,1,0:T(8,128)(2,1)S(1)} %get-tuple-element.32.rows, s32[8192]{0:T(1024)S(1)} %get-tuple-element.24.ids.node_ids, s32[8192]{0:T(1024)S(1)} %get-tuple-element.25.marks), custom_call_target="tpu_custom_call" | custom-call | flops 268435456 | bytes 1048576 | tf_op jit(solution)/shard_map/more_sums/pallas_call | solution.py:225
  14.0 0.1 collective-permute-start.4
  14.0 2.1 %collective-permute-start.6 = (f32[2,296,128]{2,1,0:T(8,128)S(1)}, f32[2,296,128]{2,1,0:T(8,128)S(1)}, u32[]{:S(2)}, u32[]{:S(2)}) collective-permute-start(f32[2,296,128]{2,1,0:T(8,128)S(1)} %add_add_fusion), channel_id=1, source_target_pairs={{0,4},{1,3},{2,6},{3,1},{4,0},{5,7},{6,2},{7,5},{8,12},{9,11},{10,... | collective-permute-start | bytes 909320 | tf_op jit(solution)/shard_map/ppermute | solution.py:387
  16.2 0.4 collective-permute-done.5
  16.5 0.0 collective-permute-done.4
  16.5 4.4 %collective-permute-done.6 = f32[2,296,128]{2,1,0:T(8,128)S(1)} collective-permute-done((f32[2,296,128]{2,1,0:T(8,128)S(1)}, f32[2,296,128]{2,1,0:T(8,128)S(1)}, u32[]{:S(2)}, u32[]{:S(2)}) %collective-permute-start.6) | collective-permute-done | bytes 303136 | tf_op jit(solution)/shard_map/ppermute | solution.py:387
  21.0 0.1 slice_add_fusion
  21.1 3.1 %collective-permute-start.7 = (f32[1,296,128]{2,1,0:T(8,128)S(1)}, f32[1,296,128]{2,1,0:T(8,128)S(1)}, u32[]{:S(2)}, u32[]{:S(2)}) collective-permute-start(f32[1,296,128]{2,1,0:T(8,128)S(1)} %get-tuple-element.42), channel_id=1, source_target_pairs={{0,8},{1,9},{2,10},{3,11},{4,12},{5,13},{6,14},{7,15},{8,0},{9,1},... | collective-permute-start | bytes 454664 | tf_op jit(solution)/shard_map/ppermute | solution.py:387
  24.2 6.9 %collective-permute-done.7.came = f32[1,296,128]{2,1,0:T(8,128)S(1)} collective-permute-done((f32[1,296,128]{2,1,0:T(8,128)S(1)}, f32[1,296,128]{2,1,0:T(8,128)S(1)}, u32[]{:S(2)}, u32[]{:S(2)}) %collective-permute-start.7) | collective-permute-done | bytes 151584 | tf_op jit(solution)/shard_map/ppermute | solution.py:387
  31.1 7.1 %solve.1 = (f32[1,16,256]{2,1,0:T(8,128)}, bf16[1,16,384]{2,1,0:T(8,128)(2,1)S(1)}) custom-call(f32[1,296,128]{2,1,0:T(8,128)S(1)} %get-tuple-element.43.kept, f32[1,296,128]{2,1,0:T(8,128)S(1)} %collective-permute-done.7.came), custom_call_target="tpu_custom_call" | custom-call | tf_op jit(solution)/shard_map/solve/pallas_call | solution.py:335
  38.2 0.0 collective-permute-start.8
  38.3 4.7 %collective-permute-done.8 = bf16[1,16,384]{2,1,0:T(8,128)(2,1)S(1)} collective-permute-done((bf16[1,16,384]{2,1,0:T(8,128)(2,1)S(1)}, bf16[1,16,384]{2,1,0:T(8,128)(2,1)S(1)}, u32[]{:S(2)}, u32[]{:S(2)}) %collective-permute-start.8) | collective-permute-done | bytes 12320 | tf_op jit(solution)/shard_map/ppermute | solution.py:387
  42.9 1.1 %collective-permute-start.9 = (bf16[2,16,384]{2,1,0:T(8,128)(2,1)S(1)}, bf16[2,16,384]{2,1,0:T(8,128)(2,1)S(1)}, u32[]{:S(2)}, u32[]{:S(2)}) collective-permute-start(bf16[2,16,384]{2,1,0:T(8,128)(2,1)S(1)} %pad_maximum_fusion.2), channel_id=1, source_target_pairs={{0,4},{1,3},{2,6},{3,1},{4,0},{5,7},{6,2},{7,5},{8,12},{9,11},{10,... | collective-permute-start | bytes 73736 | tf_op jit(solution)/shard_map/ppermute | solution.py:387
  44.0 2.7 %collective-permute-done.9 = bf16[2,16,384]{2,1,0:T(8,128)(2,1)S(1)} collective-permute-done((bf16[2,16,384]{2,1,0:T(8,128)(2,1)S(1)}, bf16[2,16,384]{2,1,0:T(8,128)(2,1)S(1)}, u32[]{:S(2)}, u32[]{:S(2)}) %collective-permute-start.9) | collective-permute-done | bytes 24608 | tf_op jit(solution)/shard_map/ppermute | solution.py:387
  46.8 1.6 %collective-permute-start.10 = (bf16[4,16,384]{2,1,0:T(8,128)(2,1)S(1)}, bf16[4,16,384]{2,1,0:T(8,128)(2,1)S(1)}, u32[]{:S(2)}, u32[]{:S(2)}) collective-permute-start(bf16[4,16,384]{2,1,0:T(8,128)(2,1)S(1)} %pad_maximum_fusion.1), channel_id=1, source_target_pairs={{0,2},{1,5},{2,0},{3,7},{4,6},{5,1},{6,4},{7,3},{8,10},{9,13},{10,... | collective-permute-start | bytes 147464 | tf_op jit(solution)/shard_map/ppermute | solution.py:387
  48.4 2.6 %collective-permute-done.10 = bf16[4,16,384]{2,1,0:T(8,128)(2,1)S(1)} collective-permute-done((bf16[4,16,384]{2,1,0:T(8,128)(2,1)S(1)}, bf16[4,16,384]{2,1,0:T(8,128)(2,1)S(1)}, u32[]{:S(2)}, u32[]{:S(2)}) %collective-permute-start.10) | collective-permute-done | bytes 49184 | tf_op jit(solution)/shard_map/ppermute | solution.py:387
  50.9 0.1 collective-permute-start.11
  51.0 1.3 %collective-permute-done.11 = bf16[8,16,384]{2,1,0:T(8,128)(2,1)S(1)} collective-permute-done((bf16[8,16,384]{2,1,0:T(8,128)(2,1)S(1)}, bf16[8,16,384]{2,1,0:T(8,128)(2,1)S(1)}, u32[]{:S(2)}, u32[]{:S(2)}) %collective-permute-start.11) | collective-permute-done | bytes 98336 | tf_op jit(solution)/shard_map/ppermute | solution.py:387
  52.3 0.0 copy-done
  52.3 0.0 copy-done.1
  52.3 2.6 %all_scores.1 = f32[16,8192]{1,0:T(8,128)} custom-call(s32[16]{0:T(128)S(1)} %copy-done.1, bf16[8192,256]{1,0:T(8,128)(2,1)S(1)} %copy-done, s32[8192]{0:T(1024)S(1)} %get-tuple-element.24.ids.node_ids, bf16[16,16,384]{2,1,0:T(8,128)(2,1)S(1)} %constant_dynamic-update-slice_fusion.messages), custom_call_target="tpu_custom_call" | custom-call | tf_op jit(solution)/shard_map/all_scores/pallas_call | solution.py:370
  (10 shorter events, 0.1 us)
Async XLA Ops:
  3.1 1.8 %collective-permute-start = (f32[2,296,128]{2,1,0:T(8,128)S(1)}, f32[2,296,128]{2,1,0:T(8,128)S(1)}, u32[]{:S(2)}, u32[]{:S(2)}) collective-permute-start(f32[2,296,128]{2,1,0:T(8,128)S(1)} %get-tuple-element.27), channel_id=1, source_target_pairs={{0,1},{1,0},{2,3},{3,2},{4,5},{5,4},{6,7},{7,6},{8,9},{9,8},{10,11... | collective-permute-start | bytes 909320 | tf_op jit(solution)/shard_map/ppermute | solution.py:387
  4.7 4.9 %collective-permute-start.1 = (f32[2,296,128]{2,1,0:T(8,128)S(1)}, f32[2,296,128]{2,1,0:T(8,128)S(1)}, u32[]{:S(2)}, u32[]{:S(2)}) collective-permute-start(f32[2,296,128]{2,1,0:T(8,128)S(1)} %get-tuple-element.30), channel_id=1, source_target_pairs={{0,1},{1,0},{2,3},{3,2},{4,5},{5,4},{6,7},{7,6},{8,9},{9,8},{10,11... | collective-permute-start | bytes 909320 | tf_op jit(solution)/shard_map/ppermute | solution.py:387
  4.9 7.8 %collective-permute-start.3 = (f32[2,296,128]{2,1,0:T(8,128)S(1)}, f32[2,296,128]{2,1,0:T(8,128)S(1)}, u32[]{:S(2)}, u32[]{:S(2)}) collective-permute-start(f32[2,296,128]{2,1,0:T(8,128)S(1)} %add.30), channel_id=1, source_target_pairs={{0,2},{1,5},{2,0},{3,7},{4,6},{5,1},{6,4},{7,3},{8,10},{9,13},{10,... | collective-permute-start | bytes 909320 | tf_op jit(solution)/shard_map/ppermute | solution.py:387
  9.5 3.2 %collective-permute-start.2 = (f32[2,296,128]{2,1,0:T(8,128)S(1)}, f32[2,296,128]{2,1,0:T(8,128)S(1)}, u32[]{:S(2)}, u32[]{:S(2)}) collective-permute-start(f32[2,296,128]{2,1,0:T(8,128)S(1)} %get-tuple-element.33), channel_id=1, source_target_pairs={{0,1},{1,0},{2,3},{3,2},{4,5},{5,4},{6,7},{7,6},{8,9},{9,8},{10,11... | collective-permute-start | bytes 909320 | tf_op jit(solution)/shard_map/ppermute | solution.py:387
  9.7 6.9 %collective-permute-start.5 = (f32[2,296,128]{2,1,0:T(8,128)S(1)}, f32[2,296,128]{2,1,0:T(8,128)S(1)}, u32[]{:S(2)}, u32[]{:S(2)}) collective-permute-start(f32[2,296,128]{2,1,0:T(8,128)S(1)} %add.31), channel_id=1, source_target_pairs={{0,2},{1,5},{2,0},{3,7},{4,6},{5,1},{6,4},{7,3},{8,10},{9,13},{10,... | collective-permute-start | bytes 909320 | tf_op jit(solution)/shard_map/ppermute | solution.py:387
  12.8 39.5 %copy-start = (bf16[8192,256]{1,0:T(8,128)(2,1)S(1)}, bf16[8192,256]{1,0:T(8,128)(2,1)}, u32[]{:S(2)}) copy-start(bf16[8192,256]{1,0:T(8,128)(2,1)} %features.5) | copy-start | bytes 12582916
  12.8 39.5 %copy-start.1 = (s32[16]{0:T(128)S(1)}, s32[16]{0:T(128)}, u32[]{:S(2)}) copy-start(s32[16]{0:T(128)} %owners.3) | copy-start | bytes 196
  14.0 2.6 %collective-permute-start.4 = (f32[2,296,128]{2,1,0:T(8,128)S(1)}, f32[2,296,128]{2,1,0:T(8,128)S(1)}, u32[]{:S(2)}, u32[]{:S(2)}) collective-permute-start(f32[2,296,128]{2,1,0:T(8,128)S(1)} %get-tuple-element.37), channel_id=1, source_target_pairs={{0,1},{1,0},{2,3},{3,2},{4,5},{5,4},{6,7},{7,6},{8,9},{9,8},{10,11... | collective-permute-start | bytes 909320 | tf_op jit(solution)/shard_map/ppermute | solution.py:387
  14.0 6.9 %collective-permute-start.6 = (f32[2,296,128]{2,1,0:T(8,128)S(1)}, f32[2,296,128]{2,1,0:T(8,128)S(1)}, u32[]{:S(2)}, u32[]{:S(2)}) collective-permute-start(f32[2,296,128]{2,1,0:T(8,128)S(1)} %add_add_fusion), channel_id=1, source_target_pairs={{0,4},{1,3},{2,6},{3,1},{4,0},{5,7},{6,2},{7,5},{8,12},{9,11},{10,... | collective-permute-start | bytes 909320 | tf_op jit(solution)/shard_map/ppermute | solution.py:387
  21.1 10.0 %collective-permute-start.7 = (f32[1,296,128]{2,1,0:T(8,128)S(1)}, f32[1,296,128]{2,1,0:T(8,128)S(1)}, u32[]{:S(2)}, u32[]{:S(2)}) collective-permute-start(f32[1,296,128]{2,1,0:T(8,128)S(1)} %get-tuple-element.42), channel_id=1, source_target_pairs={{0,8},{1,9},{2,10},{3,11},{4,12},{5,13},{6,14},{7,15},{8,0},{9,1},... | collective-permute-start | bytes 454664 | tf_op jit(solution)/shard_map/ppermute | solution.py:387
  38.2 4.7 %collective-permute-start.8 = (bf16[1,16,384]{2,1,0:T(8,128)(2,1)S(1)}, bf16[1,16,384]{2,1,0:T(8,128)(2,1)S(1)}, u32[]{:S(2)}, u32[]{:S(2)}) collective-permute-start(bf16[1,16,384]{2,1,0:T(8,128)(2,1)S(1)} %get-tuple-element.41), channel_id=1, source_target_pairs={{0,8},{1,9},{2,10},{3,11},{4,12},{5,13},{6,14},{7,15},{8,0},{9,1},... | collective-permute-start | bytes 36872 | tf_op jit(solution)/shard_map/ppermute | solution.py:387
  42.9 3.8 %collective-permute-start.9 = (bf16[2,16,384]{2,1,0:T(8,128)(2,1)S(1)}, bf16[2,16,384]{2,1,0:T(8,128)(2,1)S(1)}, u32[]{:S(2)}, u32[]{:S(2)}) collective-permute-start(bf16[2,16,384]{2,1,0:T(8,128)(2,1)S(1)} %pad_maximum_fusion.2), channel_id=1, source_target_pairs={{0,4},{1,3},{2,6},{3,1},{4,0},{5,7},{6,2},{7,5},{8,12},{9,11},{10,... | collective-permute-start | bytes 73736 | tf_op jit(solution)/shard_map/ppermute | solution.py:387
  46.8 4.2 %collective-permute-start.10 = (bf16[4,16,384]{2,1,0:T(8,128)(2,1)S(1)}, bf16[4,16,384]{2,1,0:T(8,128)(2,1)S(1)}, u32[]{:S(2)}, u32[]{:S(2)}) collective-permute-start(bf16[4,16,384]{2,1,0:T(8,128)(2,1)S(1)} %pad_maximum_fusion.1), channel_id=1, source_target_pairs={{0,2},{1,5},{2,0},{3,7},{4,6},{5,1},{6,4},{7,3},{8,10},{9,13},{10,... | collective-permute-start | bytes 147464 | tf_op jit(solution)/shard_map/ppermute | solution.py:387
  50.9 1.4 %collective-permute-start.11 = (bf16[8,16,384]{2,1,0:T(8,128)(2,1)S(1)}, bf16[8,16,384]{2,1,0:T(8,128)(2,1)S(1)}, u32[]{:S(2)}, u32[]{:S(2)}) collective-permute-start(bf16[8,16,384]{2,1,0:T(8,128)(2,1)S(1)} %pad_maximum_fusion), channel_id=1, source_target_pairs={{0,1},{1,0},{2,3},{3,2},{4,5},{5,4},{6,7},{7,6},{8,9},{9,8},{10,11... | collective-permute-start | bytes 294920 | tf_op jit(solution)/shard_map/ppermute | solution.py:387

commit v6 on v5

--- a/solution.py
+++ b/solution.py
@@ -73,18 +73,17 @@
     return pltpu.VMEM((blocks, size + 2 * CLASSES + 8, size // 2), jnp.float32)
 
 
-def fill(out, first, row_first, listed, rows, ids, marks, ready=None):
-    size = rows.shape[2]
-    segment = rows.shape[1]
+def fill(out, first, listed, rows, ids, marks, ready=None):
+    _, segment, size = rows.shape
     half = size // 2
 
     def step(q, carry):
         node = listed[first + q]
         if ready is not None:
-            ready(first + q)
+            ready(node)
         here = pl.ds(pl.multiple_of(node * segment, segment), segment)
         alive = ids[here].reshape(1, segment) == node
-        cross, mixed, sums, tail = packed_sums(rows[row_first + q], alive, marks[here].reshape(1, segment))
+        cross, mixed, sums, tail = packed_sums(rows[node], alive, marks[here].reshape(1, segment))
         out[q, 0:half] = cross
         out[q, half:size] = mixed
         out[q, size : size + CLASSES] = sums[:, :half]
@@ -95,18 +94,12 @@
     lax.fori_loop(0, out.shape[0], step, 0)
 
 
-def row_copy(features, rows, sems, listed, first, position):
-    segment = rows.shape[1]
-    start = pl.multiple_of(listed[position] * segment, segment)
-    slot = position - first
-    return pltpu.make_async_copy(features.at[pl.ds(start, segment)], rows.at[slot], sems.at[slot])
-
-
 def first_sums_kernel(
     bits, owners, features, node_ids, labels, sent, listed, rows, ids, marks, owner_list, row_sems, list_sem, id_sem, mark_sem
 ):
     nodes = owners.shape[0]
     blocks = sent.shape[0]
+    segment = rows.shape[1]
     copies = [
         pltpu.make_async_copy(owners, owner_list, list_sem),
         pltpu.make_async_copy(node_ids, ids, id_sem),
@@ -114,6 +107,13 @@
     ]
     for copy in copies:
         copy.start()
+
+    def row_copy(node):
+        start = pl.multiple_of(node * segment, segment)
+        return pltpu.make_async_copy(features.at[pl.ds(start, segment)], rows.at[node], row_sems.at[node])
+
+    for node in range(nodes):
+        row_copy(node).start()
     copies[0].wait()
     me = lax.axis_index("rows")
     for node in range(nodes):
@@ -122,26 +122,15 @@
         place = place_of(apart, owner, bits)
         chunk = 7 - 2 * (place >> (bits - 3)) - (apart & 1)
         listed[chunk * blocks + (place & (blocks - 1))] = node
-    for position in range(nodes // 2):
-        row_copy(features, rows, row_sems, listed, 0, position).start()
     for copy in copies[1:]:
         copy.wait()
-
-    def ready(position):
-        row_copy(features, rows, row_sems, listed, 0, position).wait()
-
-    fill(sent, 0, 0, listed, rows, ids, marks, ready)
-    for position in range(blocks, nodes // 2):
-        ready(position)
+    fill(sent, 0, listed, rows, ids, marks, lambda node: row_copy(node).wait())
+    for position in range(blocks, nodes):
+        row_copy(listed[position]).wait()
 
 
 def hbm(x):
     return pltpu.with_memory_space_constraint(x, pltpu.HBM)
-
-
-def half_rows(features, nodes):
-    row_count, size = features.shape
-    return pltpu.VMEM((nodes // 2, row_count // nodes, size), features.dtype)
 
 
 def first_sums(features, node_ids, labels, owners, bits):
@@ -155,7 +144,7 @@
         out_shape=(
             packed_shape(size, nodes // 8),
             pltpu.SMEM((nodes,), jnp.int32),
-            half_rows(features, nodes),
+            pltpu.VMEM((nodes, row_count // nodes, size), features.dtype),
             pltpu.VMEM((row_count,), jnp.int32),
             pltpu.VMEM((row_count,), jnp.int32),
         ),
@@ -163,7 +152,7 @@
         out_specs=(near, words, near, near, near),
         scratch_shapes=[
             pltpu.SMEM((nodes,), jnp.int32),
-            pltpu.SemaphoreType.DMA((nodes // 2,)),
+            pltpu.SemaphoreType.DMA((nodes,)),
             pltpu.SemaphoreType.DMA,
             pltpu.SemaphoreType.DMA,
             pltpu.SemaphoreType.DMA,
@@ -173,38 +162,6 @@
     )(hbm(owners), hbm(features), hbm(node_ids), hbm(labels))
 
 
-def loading_sums_kernel(listed, features, rows, ids, marks, early, late, later_rows, row_sems):
-    nodes = listed.shape[0]
-    blocks = early.shape[0]
-    middle = nodes // 2
-    for position in range(middle, nodes):
-        row_copy(features, later_rows, row_sems, listed, middle, position).start()
-    fill(early, 3 * blocks, 3 * blocks, listed, rows, ids, marks)
-
-    def ready(position):
-        row_copy(features, later_rows, row_sems, listed, middle, position).wait()
-
-    fill(late, 4 * blocks, 0, listed, later_rows, ids, marks, ready)
-    for position in range(middle + blocks, nodes):
-        ready(position)
-
-
-def loading_sums(features, listed, rows, ids, marks):
-    size = features.shape[1]
-    nodes = listed.shape[0]
-    near = pl.BlockSpec(memory_space=pltpu.VMEM)
-    return pl.pallas_call(
-        loading_sums_kernel,
-        out_shape=(packed_shape(size, nodes // 8),) * 2 + (half_rows(features, nodes),),
-        in_specs=[pl.BlockSpec(memory_space=pltpu.SMEM), pl.BlockSpec(memory_space=pltpu.HBM), near, near, near],
-        out_specs=(near, near, near),
-        scratch_shapes=[pltpu.SemaphoreType.DMA((nodes // 2,))],
-        compiler_params=pltpu.CompilerParams(vmem_limit_bytes=32 << 20),
-        cost_estimate=sums_cost(features.shape, 2),
-        name="loading_sums",
-    )(listed, hbm(features), rows, ids, marks)
-
-
 def sums_cost(shape, chunks):
     row_count, size = shape
     return pl.CostEstimate(
@@ -215,7 +172,7 @@
 def more_sums_kernel(chunks, listed, rows, ids, marks, *outs):
     for chunk, out in zip(chunks, outs):
         blocks = out.shape[0]
-        fill(out, chunk * blocks, chunk * blocks % rows.shape[0], listed, rows, ids, marks)
+        fill(out, chunk * blocks, listed, rows, ids, marks)
 
 
 def more_sums(chunks, listed, rows, ids, marks):
@@ -344,38 +301,48 @@
     )(kept, came)
 
 
-def scores_kernel(bits, group, owners, features, node_ids, messages, scores):
-    size = features.shape[1]
-    segment = scores.shape[1] // group
-    for g in range(group):
-        node = pl.program_id(0) * group + g
-        here = pl.ds(pl.multiple_of(node * segment, segment), segment)
-        alive = node_ids[here].reshape(1, segment) == node
-        owner = owners[node]
-        apart = owner ^ lax.axis_index("rows")
-        message = messages[place_of(apart, owner, bits) + ((apart & 1) << (bits - 1))]
-        offsets = jnp.sum(message[:, size:].astype(jnp.float32), axis=1, keepdims=True)
-        result = lax.dot_general(
-            message[:, :size], features[here, :], (((1,), (1,)), ((), ())), preferred_element_type=jnp.float32
-        )
-        scores[:, g * segment : (g + 1) * segment] = jnp.where(alive, result + offsets, 0.0)
-
-
-def all_scores(features, node_ids, owners, messages, bits):
-    row_count, size = features.shape
-    nodes = owners.shape[0]
-    segment = row_count // nodes
-    group = nodes // 2
+def scores_kernel(parity, listed, rows, ids, messages, *refs):
+    scores, scratch, sems = refs[-3:]
+    nodes, segment, size = rows.shape
+    blocks = nodes // 8
+    copies = []
+    for chunk in range(1 - parity, 8, 2):
+        for q in range(blocks):
+            node = listed[chunk * blocks + q]
+            start = pl.multiple_of(node * segment, segment)
+            alive = ids[pl.ds(start, segment)].reshape(1, segment) == node
+            message = messages[(7 - chunk) // 2 * blocks + q]
+            offsets = jnp.sum(message[:, size:].astype(jnp.float32), axis=1, keepdims=True)
+            result = lax.dot_general(
+                message[:, :size], rows[node], (((1,), (1,)), ((), ())), preferred_element_type=jnp.float32
+            )
+            slot = len(copies)
+            scratch[slot] = jnp.where(alive, result + offsets, 0.0)
+            copies.append(
+                pltpu.make_async_copy(scratch.at[slot], scores.at[:, pl.ds(start, segment)], sems.at[slot])
+            )
+            copies[-1].start()
+    for copy in copies:
+        copy.wait()
+
+
+def half_scores(parity, listed, rows, ids, messages, *earlier):
+    nodes, segment, _ = rows.shape
     near = pl.BlockSpec(memory_space=pltpu.VMEM)
+    far = pl.BlockSpec(memory_space=pltpu.HBM)
     return pl.pallas_call(
-        functools.partial(scores_kernel, bits, group),
-        out_shape=jax.ShapeDtypeStruct((CLASSES, row_count), jnp.float32),
-        grid=(nodes // group,),
-        in_specs=[pl.BlockSpec(memory_space=pltpu.SMEM), near, near, near],
-        out_specs=pl.BlockSpec((CLASSES, segment * group), lambda n: (0, n)),
+        functools.partial(scores_kernel, parity),
+        out_shape=pltpu.HBM((CLASSES, nodes * segment), jnp.float32),
+        in_specs=[pl.BlockSpec(memory_space=pltpu.SMEM), near, near, near] + [far] * len(earlier),
+        out_specs=far,
+        scratch_shapes=[
+            pltpu.VMEM((nodes // 2, CLASSES, segment), jnp.float32),
+            pltpu.SemaphoreType.DMA((nodes // 2,)),
+        ],
+        input_output_aliases={4: 0} if earlier else {},
         compiler_params=pltpu.CompilerParams(vmem_limit_bytes=32 << 20),
-        name="all_scores",
-    )(owners, features, node_ids, messages)
+        name="half_scores",
+    )(listed, rows, ids, messages, *(hbm(e) for e in earlier))
 
 
 def on_device(ranks, features, node_ids, labels, owners):
@@ -395,14 +362,14 @@
     came_b = swap(sent_b, (1, 1))
     sent_a, listed = lax.optimization_barrier((kept_a + came_a, listed))
     came_a = halving(sent_a, 0)
-    kept_b, next_a, rows_later = loading_sums(features, listed, rows, ids, marks)
+    kept_b, next_a = more_sums((3, 4), listed, rows, ids, marks)
     next_a = swap(next_a, (1, 1))
     sent_b, listed = lax.optimization_barrier((kept_b + came_b, listed))
     came_b = halving(sent_b, 0)
-    (kept_a,) = more_sums((5,), listed, rows_later, ids, marks)
+    (kept_a,) = more_sums((5,), listed, rows, ids, marks)
     sent_a, listed = lax.optimization_barrier((kept_a + next_a + came_a, listed))
     came = halving(sent_a, 1)
-    next_b, kept_b = more_sums((6, 7), listed, rows_later, ids, marks)
+    next_b, kept_b = more_sums((6, 7), listed, rows, ids, marks)
     next_b = swap(next_b, (1, 1))
     kept = (kept_b, next_b, came_b)
     for step in range(2, bits - 1):
@@ -414,8 +381,9 @@
     planes, held = solve(kept[0], came, size)
     for step in reversed(range(bits - 1)):
         held = jnp.concatenate([held, halving(held, step)], axis=0)
-    held = jnp.concatenate([held, swap(held, (1, 1))], axis=0)
-    return planes, all_scores(features, ids, owners, held, bits)
+    others = swap(held, (1, 1))
+    scores = half_scores(0, listed, rows, ids, held)
+    return planes, half_scores(1, listed, rows, ids, others, scores)
 
 
 def solution(mesh):

time: 55.2 us -> 53.1 us (0.962)
  waiting for transfers between devices: 24 us -> 22.1 us
    ppermute x12, waiting for transfers between devices: 24 us -> 22.1 us  [swap(): lax.ppermute(x, 'rows', [(r, r ^ distances[r & 1]) for r in range(ranks)])]
    pallas_call x2, Pallas kernels: 4.21 us -> 2.71 us  [half_scores(): pl.pallas_call(functools.partial(scores_kernel, parity), out_shape=pltpu....]
    pallas_call x3 -> x4, Pallas kernels: 2.84 us -> 3.97 us  [more_sums(): pl.pallas_call(functools.partial(more_sums_kernel, chunks), out_shape=(pa...]
  transfers between devices with their start and end apart: 12 -> 12, of which waited for: 8 -> 7; matrix products, arithmetic and copies ran while one was open for 0% -> 0% of each run, Pallas kernels for 8% -> 10%
where the time goes in v6:
time: 53.1 us; the launch traced here: 52.9 us
  waiting for transfers between devices  22.1 us (42%)
  Pallas kernels  16.7 us (31%)
  starting transfers between devices  13.1 us (25%)
  between operations  0.74 us (1%)
    ppermute x12, waiting for transfers between devices, swap(): lax.ppermute(x, 'rows', [(r, r ^ distances[r & 1]) for r in range(ranks)])  22.1 us
    ppermute x12, starting transfers between devices, swap(): lax.ppermute(x, 'rows', [(r, r ^ distances[r & 1]) for r in range(ranks)])  13.1 us
    pallas_call x1, Pallas kernels, solve(): pl.pallas_call(solve_kernel, out_shape=(jax.ShapeDtypeStruct((1, CLASSES,...  7.14 us
    pallas_call x4, Pallas kernels, more_sums(): pl.pallas_call(functools.partial(more_sums_kernel, chunks), out_shape=(pa...  3.97 us
    pallas_call x1, Pallas kernels, first_sums(): pl.pallas_call(functools.partial(first_sums_kernel, bits), out_shape=(pac...  2.85 us
    pallas_call x2, Pallas kernels, half_scores(): pl.pallas_call(functools.partial(scores_kernel, parity), out_shape=pltpu....  2.71 us
  transfers between devices with their start and end apart: 12, of which 7 were waited for; matrix products, arithmetic and copies ran while one was open for 0% of the time, Pallas kernels for 10%

profile of v6, /device:TPU:0, one launch (start us, length us, event | category | flops | bytes accessed | tf_op | source)
XLA Modules:
  0.0 52.9 jit_solution(16433630621294196570)
XLA Ops:
  0.6 2.8 %first_sums.1 = (f32[2,296,128]{2,1,0:T(8,128)S(1)}, s32[16]{0:T(128)S(4)}, bf16[16,512,256]{2,1,0:T(8,128)(2,1)S(1)}, s32[8192]{0:T(1024)S(1)}, s32[8192]{0:T(1024)S(1)}) custom-call(s32[16]{0:T(128)} %owners.1, bf16[8192,256]{1,0:T(8,128)(2,1)} %features.1, s32[8192]{0:T(1024)} %node_ids.1, s32[8192]{0:T(1024)} %labels.1), custom_call_target="tpu_custom_call" | custom-call | tf_op jit(solution)/shard_map/first_sums/pallas_call | solution.py:142
  3.5 0.5 collective-permute-start
  4.0 1.1 %more_sums.4 = (f32[2,296,128]{2,1,0:T(8,128)S(1)}, f32[2,296,128]{2,1,0:T(8,128)S(1)}) custom-call(s32[16]{0:T(128)S(4)} %get-tuple-element.33.listed, bf16[16,512,256]{2,1,0:T(8,128)(2,1)S(1)} %get-tuple-element.22.rows, s32[8192]{0:T(1024)S(1)} %get-tuple-element.23.ids, s32[8192]{0:T(1024)S(1)} %get-tuple-element.24.marks), custom_call_target="tpu_custom_call" | custom-call | flops 268435456 | bytes 1048576 | tf_op jit(solution)/shard_map/more_sums/pallas_call | solution.py:182
  5.1 0.2 collective-permute-start.1
  5.3 0.0 collective-permute-done
  5.3 3.0 %collective-permute-start.3 = (f32[2,296,128]{2,1,0:T(8,128)S(1)}, f32[2,296,128]{2,1,0:T(8,128)S(1)}, u32[]{:S(2)}, u32[]{:S(2)}) collective-permute-start(f32[2,296,128]{2,1,0:T(8,128)S(1)} %add.30), channel_id=1, source_target_pairs={{0,2},{1,5},{2,0},{3,7},{4,6},{5,1},{6,4},{7,3},{8,10},{9,13},{10,... | collective-permute-start | bytes 909320 | tf_op jit(solution)/shard_map/ppermute | solution.py:354
  8.3 1.1 %more_sums.5 = (f32[2,296,128]{2,1,0:T(8,128)S(1)}, f32[2,296,128]{2,1,0:T(8,128)S(1)}) custom-call(s32[16]{0:T(128)S(4)} %get-tuple-element.33.listed, bf16[16,512,256]{2,1,0:T(8,128)(2,1)S(1)} %get-tuple-element.22.rows, s32[8192]{0:T(1024)S(1)} %get-tuple-element.23.ids, s32[8192]{0:T(1024)S(1)} %get-tuple-element.24.marks), custom_call_target="tpu_custom_call" | custom-call | flops 268435456 | bytes 1048576 | tf_op jit(solution)/shard_map/more_sums/pallas_call | solution.py:182
  9.4 0.1 collective-permute-start.2
  9.5 0.0 collective-permute-done.1
  9.6 1.4 %collective-permute-start.5 = (f32[2,296,128]{2,1,0:T(8,128)S(1)}, f32[2,296,128]{2,1,0:T(8,128)S(1)}, u32[]{:S(2)}, u32[]{:S(2)}) collective-permute-start(f32[2,296,128]{2,1,0:T(8,128)S(1)} %add.31), channel_id=1, source_target_pairs={{0,2},{1,5},{2,0},{3,7},{4,6},{5,1},{6,4},{7,3},{8,10},{9,13},{10,... | collective-permute-start | bytes 909320 | tf_op jit(solution)/shard_map/ppermute | solution.py:354
  10.9 0.6 %more_sums.6 = f32[2,296,128]{2,1,0:T(8,128)S(1)} custom-call(s32[16]{0:T(128)S(4)} %get-tuple-element.33.listed, bf16[16,512,256]{2,1,0:T(8,128)(2,1)S(1)} %get-tuple-element.22.rows, s32[8192]{0:T(1024)S(1)} %get-tuple-element.23.ids, s32[8192]{0:T(1024)S(1)} %get-tuple-element.24.marks), custom_call_target="tpu_custom_call" | custom-call | flops 134217728 | bytes 524288 | tf_op jit(solution)/shard_map/more_sums/pallas_call | solution.py:182
  11.5 1.6 %collective-permute-done.3 = f32[2,296,128]{2,1,0:T(8,128)S(1)} collective-permute-done((f32[2,296,128]{2,1,0:T(8,128)S(1)}, f32[2,296,128]{2,1,0:T(8,128)S(1)}, u32[]{:S(2)}, u32[]{:S(2)}) %collective-permute-start.3) | collective-permute-done | bytes 303136 | tf_op jit(solution)/shard_map/ppermute | solution.py:354
  13.1 0.0 collective-permute-done.2
  13.1 0.1 add_add_fusion
  13.2 2.1 %collective-permute-start.6 = (f32[2,296,128]{2,1,0:T(8,128)S(1)}, f32[2,296,128]{2,1,0:T(8,128)S(1)}, u32[]{:S(2)}, u32[]{:S(2)}) collective-permute-start(f32[2,296,128]{2,1,0:T(8,128)S(1)} %add_add_fusion), channel_id=1, source_target_pairs={{0,4},{1,3},{2,6},{3,1},{4,0},{5,7},{6,2},{7,5},{8,12},{9,11},{10,... | collective-permute-start | bytes 909320 | tf_op jit(solution)/shard_map/ppermute | solution.py:354
  15.3 1.1 %more_sums.7 = (f32[2,296,128]{2,1,0:T(8,128)S(1)}, f32[2,296,128]{2,1,0:T(8,128)S(1)}) custom-call(s32[16]{0:T(128)S(4)} %get-tuple-element.33.listed, bf16[16,512,256]{2,1,0:T(8,128)(2,1)S(1)} %get-tuple-element.22.rows, s32[8192]{0:T(1024)S(1)} %get-tuple-element.23.ids, s32[8192]{0:T(1024)S(1)} %get-tuple-element.24.marks), custom_call_target="tpu_custom_call" | custom-call | flops 268435456 | bytes 1048576 | tf_op jit(solution)/shard_map/more_sums/pallas_call | solution.py:182
  16.4 0.1 collective-permute-start.4
  16.5 1.0 %collective-permute-done.5 = f32[2,296,128]{2,1,0:T(8,128)S(1)} collective-permute-done((f32[2,296,128]{2,1,0:T(8,128)S(1)}, f32[2,296,128]{2,1,0:T(8,128)S(1)}, u32[]{:S(2)}, u32[]{:S(2)}) %collective-permute-start.5) | collective-permute-done | bytes 303136 | tf_op jit(solution)/shard_map/ppermute | solution.py:354
  17.5 2.6 %collective-permute-done.6 = f32[2,296,128]{2,1,0:T(8,128)S(1)} collective-permute-done((f32[2,296,128]{2,1,0:T(8,128)S(1)}, f32[2,296,128]{2,1,0:T(8,128)S(1)}, u32[]{:S(2)}, u32[]{:S(2)}) %collective-permute-start.6) | collective-permute-done | bytes 303136 | tf_op jit(solution)/shard_map/ppermute | solution.py:354
  20.1 0.0 collective-permute-done.4
  20.1 0.1 slice_add_fusion
  20.2 3.1 %collective-permute-start.7 = (f32[1,296,128]{2,1,0:T(8,128)S(1)}, f32[1,296,128]{2,1,0:T(8,128)S(1)}, u32[]{:S(2)}, u32[]{:S(2)}) collective-permute-start(f32[1,296,128]{2,1,0:T(8,128)S(1)} %get-tuple-element.40), channel_id=1, source_target_pairs={{0,8},{1,9},{2,10},{3,11},{4,12},{5,13},{6,14},{7,15},{8,0},{9,1},... | collective-permute-start | bytes 454664 | tf_op jit(solution)/shard_map/ppermute | solution.py:354
  23.3 7.0 %collective-permute-done.7.came = f32[1,296,128]{2,1,0:T(8,128)S(1)} collective-permute-done((f32[1,296,128]{2,1,0:T(8,128)S(1)}, f32[1,296,128]{2,1,0:T(8,128)S(1)}, u32[]{:S(2)}, u32[]{:S(2)}) %collective-permute-start.7) | collective-permute-done | bytes 151584 | tf_op jit(solution)/shard_map/ppermute | solution.py:354
  30.3 7.1 %solve.1 = (f32[1,16,256]{2,1,0:T(8,128)}, bf16[1,16,384]{2,1,0:T(8,128)(2,1)S(1)}) custom-call(f32[1,296,128]{2,1,0:T(8,128)S(1)} %get-tuple-element.41.kept, f32[1,296,128]{2,1,0:T(8,128)S(1)} %collective-permute-done.7.came), custom_call_target="tpu_custom_call" | custom-call | tf_op jit(solution)/shard_map/solve/pallas_call | solution.py:292
  37.4 0.0 collective-permute-start.8
  37.4 4.7 %collective-permute-done.8 = bf16[1,16,384]{2,1,0:T(8,128)(2,1)S(1)} collective-permute-done((bf16[1,16,384]{2,1,0:T(8,128)(2,1)S(1)}, bf16[1,16,384]{2,1,0:T(8,128)(2,1)S(1)}, u32[]{:S(2)}, u32[]{:S(2)}) %collective-permute-start.8) | collective-permute-done | bytes 12320 | tf_op jit(solution)/shard_map/ppermute | solution.py:354
  42.1 1.1 %collective-permute-start.9 = (bf16[2,16,384]{2,1,0:T(8,128)(2,1)S(1)}, bf16[2,16,384]{2,1,0:T(8,128)(2,1)S(1)}, u32[]{:S(2)}, u32[]{:S(2)}) collective-permute-start(bf16[2,16,384]{2,1,0:T(8,128)(2,1)S(1)} %pad_maximum_fusion.1), channel_id=1, source_target_pairs={{0,4},{1,3},{2,6},{3,1},{4,0},{5,7},{6,2},{7,5},{8,12},{9,11},{10,... | collective-permute-start | bytes 73736 | tf_op jit(solution)/shard_map/ppermute | solution.py:354
  43.2 2.7 %collective-permute-done.9 = bf16[2,16,384]{2,1,0:T(8,128)(2,1)S(1)} collective-permute-done((bf16[2,16,384]{2,1,0:T(8,128)(2,1)S(1)}, bf16[2,16,384]{2,1,0:T(8,128)(2,1)S(1)}, u32[]{:S(2)}, u32[]{:S(2)}) %collective-permute-start.9) | collective-permute-done | bytes 24608 | tf_op jit(solution)/shard_map/ppermute | solution.py:354
  46.0 1.6 %collective-permute-start.10 = (bf16[4,16,384]{2,1,0:T(8,128)(2,1)S(1)}, bf16[4,16,384]{2,1,0:T(8,128)(2,1)S(1)}, u32[]{:S(2)}, u32[]{:S(2)}) collective-permute-start(bf16[4,16,384]{2,1,0:T(8,128)(2,1)S(1)} %pad_maximum_fusion), channel_id=1, source_target_pairs={{0,2},{1,5},{2,0},{3,7},{4,6},{5,1},{6,4},{7,3},{8,10},{9,13},{10,... | collective-permute-start | bytes 147464 | tf_op jit(solution)/shard_map/ppermute | solution.py:354
  47.6 2.6 %collective-permute-done.10 = bf16[4,16,384]{2,1,0:T(8,128)(2,1)S(1)} collective-permute-done((bf16[4,16,384]{2,1,0:T(8,128)(2,1)S(1)}, bf16[4,16,384]{2,1,0:T(8,128)(2,1)S(1)}, u32[]{:S(2)}, u32[]{:S(2)}) %collective-permute-start.10) | collective-permute-done | bytes 49184 | tf_op jit(solution)/shard_map/ppermute | solution.py:354
  50.1 0.1 collective-permute-start.11
  50.2 1.4 %half_scores.2.refs_0_ = f32[16,8192]{1,0:T(8,128)} custom-call(s32[16]{0:T(128)S(4)} %get-tuple-element.33.listed, bf16[16,512,256]{2,1,0:T(8,128)(2,1)S(1)} %get-tuple-element.22.rows, s32[8192]{0:T(1024)S(1)} %get-tuple-element.23.ids, bf16[8,16,384]{2,1,0:T(8,128)(2,1)S(1)} %constant_dynamic-update-slice_fusion.messages), custom_call_target="tpu_custom_call" | custom-call | tf_op jit(solution)/shard_map/half_scores/pallas_call | solution.py:333
  51.6 0.0 collective-permute-done.11.messages
  51.6 1.4 %half_scores.3 = f32[16,8192]{1,0:T(8,128)} custom-call(s32[16]{0:T(128)S(4)} %get-tuple-element.33.listed, bf16[16,512,256]{2,1,0:T(8,128)(2,1)S(1)} %get-tuple-element.22.rows, s32[8192]{0:T(1024)S(1)} %get-tuple-element.23.ids, bf16[8,16,384]{2,1,0:T(8,128)(2,1)S(1)} %collective-permute-done.11.messages, ...), custom_call_target="tpu_custom_call", output_to_operand_aliasing={{}: (4, {})} | custom-call | tf_op jit(solution)/shard_map/half_scores/pallas_call | solution.py:333
  (8 shorter events, 0.1 us)
Async XLA Ops:
  3.5 1.8 %collective-permute-start = (f32[2,296,128]{2,1,0:T(8,128)S(1)}, f32[2,296,128]{2,1,0:T(8,128)S(1)}, u32[]{:S(2)}, u32[]{:S(2)}) collective-permute-start(f32[2,296,128]{2,1,0:T(8,128)S(1)} %get-tuple-element.26), channel_id=1, source_target_pairs={{0,1},{1,0},{2,3},{3,2},{4,5},{5,4},{6,7},{7,6},{8,9},{9,8},{10,11... | collective-permute-start | bytes 909320 | tf_op jit(solution)/shard_map/ppermute | solution.py:354
  5.1 4.4 %collective-permute-start.1 = (f32[2,296,128]{2,1,0:T(8,128)S(1)}, f32[2,296,128]{2,1,0:T(8,128)S(1)}, u32[]{:S(2)}, u32[]{:S(2)}) collective-permute-start(f32[2,296,128]{2,1,0:T(8,128)S(1)} %get-tuple-element.29), channel_id=1, source_target_pairs={{0,1},{1,0},{2,3},{3,2},{4,5},{5,4},{6,7},{7,6},{8,9},{9,8},{10,11... | collective-permute-start | bytes 909320 | tf_op jit(solution)/shard_map/ppermute | solution.py:354
  5.3 7.8 %collective-permute-start.3 = (f32[2,296,128]{2,1,0:T(8,128)S(1)}, f32[2,296,128]{2,1,0:T(8,128)S(1)}, u32[]{:S(2)}, u32[]{:S(2)}) collective-permute-start(f32[2,296,128]{2,1,0:T(8,128)S(1)} %add.30), channel_id=1, source_target_pairs={{0,2},{1,5},{2,0},{3,7},{4,6},{5,1},{6,4},{7,3},{8,10},{9,13},{10,... | collective-permute-start | bytes 909320 | tf_op jit(solution)/shard_map/ppermute | solution.py:354
  9.4 3.7 %collective-permute-start.2 = (f32[2,296,128]{2,1,0:T(8,128)S(1)}, f32[2,296,128]{2,1,0:T(8,128)S(1)}, u32[]{:S(2)}, u32[]{:S(2)}) collective-permute-start(f32[2,296,128]{2,1,0:T(8,128)S(1)} %get-tuple-element.31), channel_id=1, source_target_pairs={{0,1},{1,0},{2,3},{3,2},{4,5},{5,4},{6,7},{7,6},{8,9},{9,8},{10,11... | collective-permute-start | bytes 909320 | tf_op jit(solution)/shard_map/ppermute | solution.py:354
  9.6 7.9 %collective-permute-start.5 = (f32[2,296,128]{2,1,0:T(8,128)S(1)}, f32[2,296,128]{2,1,0:T(8,128)S(1)}, u32[]{:S(2)}, u32[]{:S(2)}) collective-permute-start(f32[2,296,128]{2,1,0:T(8,128)S(1)} %add.31), channel_id=1, source_target_pairs={{0,2},{1,5},{2,0},{3,7},{4,6},{5,1},{6,4},{7,3},{8,10},{9,13},{10,... | collective-permute-start | bytes 909320 | tf_op jit(solution)/shard_map/ppermute | solution.py:354
  13.2 6.9 %collective-permute-start.6 = (f32[2,296,128]{2,1,0:T(8,128)S(1)}, f32[2,296,128]{2,1,0:T(8,128)S(1)}, u32[]{:S(2)}, u32[]{:S(2)}) collective-permute-start(f32[2,296,128]{2,1,0:T(8,128)S(1)} %add_add_fusion), channel_id=1, source_target_pairs={{0,4},{1,3},{2,6},{3,1},{4,0},{5,7},{6,2},{7,5},{8,12},{9,11},{10,... | collective-permute-start | bytes 909320 | tf_op jit(solution)/shard_map/ppermute | solution.py:354
  16.4 3.7 %collective-permute-start.4 = (f32[2,296,128]{2,1,0:T(8,128)S(1)}, f32[2,296,128]{2,1,0:T(8,128)S(1)}, u32[]{:S(2)}, u32[]{:S(2)}) collective-permute-start(f32[2,296,128]{2,1,0:T(8,128)S(1)} %get-tuple-element.35), channel_id=1, source_target_pairs={{0,1},{1,0},{2,3},{3,2},{4,5},{5,4},{6,7},{7,6},{8,9},{9,8},{10,11... | collective-permute-start | bytes 909320 | tf_op jit(solution)/shard_map/ppermute | solution.py:354
  20.2 10.1 %collective-permute-start.7 = (f32[1,296,128]{2,1,0:T(8,128)S(1)}, f32[1,296,128]{2,1,0:T(8,128)S(1)}, u32[]{:S(2)}, u32[]{:S(2)}) collective-permute-start(f32[1,296,128]{2,1,0:T(8,128)S(1)} %get-tuple-element.40), channel_id=1, source_target_pairs={{0,8},{1,9},{2,10},{3,11},{4,12},{5,13},{6,14},{7,15},{8,0},{9,1},... | collective-permute-start | bytes 454664 | tf_op jit(solution)/shard_map/ppermute | solution.py:354
  37.4 4.7 %collective-permute-start.8 = (bf16[1,16,384]{2,1,0:T(8,128)(2,1)S(1)}, bf16[1,16,384]{2,1,0:T(8,128)(2,1)S(1)}, u32[]{:S(2)}, u32[]{:S(2)}) collective-permute-start(bf16[1,16,384]{2,1,0:T(8,128)(2,1)S(1)} %get-tuple-element.39), channel_id=1, source_target_pairs={{0,8},{1,9},{2,10},{3,11},{4,12},{5,13},{6,14},{7,15},{8,0},{9,1},... | collective-permute-start | bytes 36872 | tf_op jit(solution)/shard_map/ppermute | solution.py:354
  42.1 3.8 %collective-permute-start.9 = (bf16[2,16,384]{2,1,0:T(8,128)(2,1)S(1)}, bf16[2,16,384]{2,1,0:T(8,128)(2,1)S(1)}, u32[]{:S(2)}, u32[]{:S(2)}) collective-permute-start(bf16[2,16,384]{2,1,0:T(8,128)(2,1)S(1)} %pad_maximum_fusion.1), channel_id=1, source_target_pairs={{0,4},{1,3},{2,6},{3,1},{4,0},{5,7},{6,2},{7,5},{8,12},{9,11},{10,... | collective-permute-start | bytes 73736 | tf_op jit(solution)/shard_map/ppermute | solution.py:354
  46.0 4.2 %collective-permute-start.10 = (bf16[4,16,384]{2,1,0:T(8,128)(2,1)S(1)}, bf16[4,16,384]{2,1,0:T(8,128)(2,1)S(1)}, u32[]{:S(2)}, u32[]{:S(2)}) collective-permute-start(bf16[4,16,384]{2,1,0:T(8,128)(2,1)S(1)} %pad_maximum_fusion), channel_id=1, source_target_pairs={{0,2},{1,5},{2,0},{3,7},{4,6},{5,1},{6,4},{7,3},{8,10},{9,13},{10,... | collective-permute-start | bytes 147464 | tf_op jit(solution)/shard_map/ppermute | solution.py:354
  50.1 1.4 %collective-permute-start.11 = (bf16[8,16,384]{2,1,0:T(8,128)(2,1)S(1)}, bf16[8,16,384]{2,1,0:T(8,128)(2,1)S(1)}, u32[]{:S(2)}, u32[]{:S(2)}) collective-permute-start(bf16[8,16,384]{2,1,0:T(8,128)(2,1)S(1)} %constant_dynamic-update-slice_fusion.messages), channel_id=1, source_target_pairs={{0,1},{1,0},{2,3},{3,2},{4,5},{5,4},{6,7},{7,6},{8,9},{9,8},{10,11... | collective-permute-start | bytes 294920 | tf_op jit(solution)/shard_map/ppermute | solution.py:354

commit v7 on v6

--- a/solution.py
+++ b/solution.py
@@ -190,7 +190,7 @@
     )(listed, rows, ids, marks)
 
 
-def sweep(matrix, size):
+def sweep(matrix, size, columns, works):
     across = size // LANES
     lanes = lax.broadcasted_iota(jnp.int32, (1, size), 1)
     rows = lax.broadcasted_iota(jnp.int32, (PANEL, 1), 0)
@@ -219,6 +219,15 @@
         cross = own
         for k in range(0, PANEL, 2):
             c0, c1 = column[k], column[k + 1]
+            group, turn = k // 8 * 8, k // 2 % 2
+            for c in range(k + 2, PANEL):
+                columns[turn, c, 0:8] = column[c][group : group + 8, :]
+            works[turn, 0:8] = work[group : group + 8, :]
+
+            def repeated(ref, at, group=group):
+                rows8 = ref[pl.ds(at - group, 8, stride=0), :]
+                return jnp.concatenate([rows8] * (PANEL // 8), axis=0)
+
             b00 = jnp.broadcast_to(c0[k : k + 1, :], (PANEL, LANES))
             b10 = jnp.broadcast_to(c0[k + 1 : k + 2, :], (PANEL, LANES))
             b11 = jnp.broadcast_to(c1[k + 1 : k + 2, :], (PANEL, LANES))
@@ -230,8 +239,10 @@
             own = jnp.where(rows == k, n00, jnp.where(rows == k + 1, n11, own))
             cross = jnp.where(pair, n10, cross)
             for c in range(k + 2, PANEL):
-                column[c] = column[c] - f0 * column[c][k : k + 1, :] - f1 * column[c][k + 1 : k + 2, :]
-            work = work - wide(f0) * work[k : k + 1, :] - wide(f1) * work[k + 1 : k + 2, :]
+                row0, row1 = (repeated(columns.at[turn, c], k + t) for t in range(2))
+                column[c] = column[c] - f0 * row0 - f1 * row1
+            row0, row1 = (repeated(works.at[turn], k + t) for t in range(2))
+            work = work - wide(f0) * row0 - wide(f1) * row1
         other = jnp.where(odd, pltpu.roll(work, 1, 0), pltpu.roll(work, PANEL - 1, 0))
         work = work * wide(own) + other * wide(cross)
         if last < size:
@@ -249,7 +260,7 @@
         matrix[first:last, :] = work
 
 
-def solve_kernel(kept, came, planes, message, matrix):
+def solve_kernel(kept, came, planes, message, matrix, columns, works):
     size = matrix.shape[0]
     half = size // 2
     packed = kept[0] + came[0]
@@ -276,7 +287,7 @@
     matrix[:half, half:] = (cross - between[:half, half:]) / total
     matrix[half:, :half] = (cross.T - between[half:, :half]) / total
     matrix[half:, half:] = (end - between[half:, half:]) / total + ridge
-    sweep(matrix, size)
+    sweep(matrix, size, columns, works)
     result = -jnp.dot(shifts, matrix[...], precision=HIGH, preferred_element_type=jnp.float32)
     planes[0] = result
     offsets = -jnp.sum(result * centers, axis=1, keepdims=True)
@@ -295,7 +306,11 @@
             jax.ShapeDtypeStruct((1, CLASSES, size), jnp.float32),
             jax.ShapeDtypeStruct((1, CLASSES, size + LANES), jnp.bfloat16),
         ),
-        scratch_shapes=[pltpu.VMEM((size, size), jnp.float32)],
+        scratch_shapes=[
+            pltpu.VMEM((size, size), jnp.float32),
+            pltpu.VMEM((2, PANEL, 16, LANES), jnp.float32),
+            pltpu.VMEM((2, 16, size), jnp.float32),
+        ],
         compiler_params=pltpu.CompilerParams(vmem_limit_bytes=32 << 20),
         name="solve",
     )(kept, came)

time: 53.1 us -> 52.9 us (level)
  no operation moved by 1% of the time
where the time goes in v7:
time: 52.9 us; the launch traced here: 52.7 us
  waiting for transfers between devices  22 us (42%)
  Pallas kernels  16.4 us (31%)
  starting transfers between devices  13.2 us (25%)
  between operations  0.74 us (1%)
    ppermute x12, waiting for transfers between devices, swap(): lax.ppermute(x, 'rows', [(r, r ^ distances[r & 1]) for r in range(ranks)])  22 us
    ppermute x12, starting transfers between devices, swap(): lax.ppermute(x, 'rows', [(r, r ^ distances[r & 1]) for r in range(ranks)])  13.2 us
    pallas_call x1, Pallas kernels, solve(): pl.pallas_call(solve_kernel, out_shape=(jax.ShapeDtypeStruct((1, CLASSES,...  6.92 us
    pallas_call x4, Pallas kernels, more_sums(): pl.pallas_call(functools.partial(more_sums_kernel, chunks), out_shape=(pa...  3.97 us
    pallas_call x1, Pallas kernels, first_sums(): pl.pallas_call(functools.partial(first_sums_kernel, bits), out_shape=(pac...  2.8 us
    pallas_call x2, Pallas kernels, half_scores(): pl.pallas_call(functools.partial(scores_kernel, parity), out_shape=pltpu....  2.71 us
  transfers between devices with their start and end apart: 12, of which 7 were waited for; matrix products, arithmetic and copies ran while one was open for 0% of the time, Pallas kernels for 10%

profile of v7, /device:TPU:0, one launch (start us, length us, event | category | flops | bytes accessed | tf_op | source)
XLA Modules:
  0.0 52.7 jit_solution(9263418655976026609)
XLA Ops:
  0.6 2.8 %first_sums.1 = (f32[2,296,128]{2,1,0:T(8,128)S(1)}, s32[16]{0:T(128)S(4)}, bf16[16,512,256]{2,1,0:T(8,128)(2,1)S(1)}, s32[8192]{0:T(1024)S(1)}, s32[8192]{0:T(1024)S(1)}) custom-call(s32[16]{0:T(128)} %owners.1, bf16[8192,256]{1,0:T(8,128)(2,1)} %features.1, s32[8192]{0:T(1024)} %node_ids.1, s32[8192]{0:T(1024)} %labels.1), custom_call_target="tpu_custom_call" | custom-call | tf_op jit(solution)/shard_map/first_sums/pallas_call | solution.py:142
  3.4 0.5 collective-permute-start
  4.0 1.1 %more_sums.4 = (f32[2,296,128]{2,1,0:T(8,128)S(1)}, f32[2,296,128]{2,1,0:T(8,128)S(1)}) custom-call(s32[16]{0:T(128)S(4)} %get-tuple-element.33.listed, bf16[16,512,256]{2,1,0:T(8,128)(2,1)S(1)} %get-tuple-element.22.rows, s32[8192]{0:T(1024)S(1)} %get-tuple-element.23.ids, s32[8192]{0:T(1024)S(1)} %get-tuple-element.24.marks), custom_call_target="tpu_custom_call" | custom-call | flops 268435456 | bytes 1048576 | tf_op jit(solution)/shard_map/more_sums/pallas_call | solution.py:182
  5.1 0.1 collective-permute-start.1
  5.2 0.0 collective-permute-done
  5.3 3.0 %collective-permute-start.3 = (f32[2,296,128]{2,1,0:T(8,128)S(1)}, f32[2,296,128]{2,1,0:T(8,128)S(1)}, u32[]{:S(2)}, u32[]{:S(2)}) collective-permute-start(f32[2,296,128]{2,1,0:T(8,128)S(1)} %add.30), channel_id=1, source_target_pairs={{0,2},{1,5},{2,0},{3,7},{4,6},{5,1},{6,4},{7,3},{8,10},{9,13},{10,... | collective-permute-start | bytes 909320 | tf_op jit(solution)/shard_map/ppermute | solution.py:369
  8.3 1.1 %more_sums.5 = (f32[2,296,128]{2,1,0:T(8,128)S(1)}, f32[2,296,128]{2,1,0:T(8,128)S(1)}) custom-call(s32[16]{0:T(128)S(4)} %get-tuple-element.33.listed, bf16[16,512,256]{2,1,0:T(8,128)(2,1)S(1)} %get-tuple-element.22.rows, s32[8192]{0:T(1024)S(1)} %get-tuple-element.23.ids, s32[8192]{0:T(1024)S(1)} %get-tuple-element.24.marks), custom_call_target="tpu_custom_call" | custom-call | flops 268435456 | bytes 1048576 | tf_op jit(solution)/shard_map/more_sums/pallas_call | solution.py:182
  9.4 0.1 collective-permute-start.2
  9.5 0.0 collective-permute-done.1
  9.6 1.4 %collective-permute-start.5 = (f32[2,296,128]{2,1,0:T(8,128)S(1)}, f32[2,296,128]{2,1,0:T(8,128)S(1)}, u32[]{:S(2)}, u32[]{:S(2)}) collective-permute-start(f32[2,296,128]{2,1,0:T(8,128)S(1)} %add.31), channel_id=1, source_target_pairs={{0,2},{1,5},{2,0},{3,7},{4,6},{5,1},{6,4},{7,3},{8,10},{9,13},{10,... | collective-permute-start | bytes 909320 | tf_op jit(solution)/shard_map/ppermute | solution.py:369
  10.9 0.6 %more_sums.6 = f32[2,296,128]{2,1,0:T(8,128)S(1)} custom-call(s32[16]{0:T(128)S(4)} %get-tuple-element.33.listed, bf16[16,512,256]{2,1,0:T(8,128)(2,1)S(1)} %get-tuple-element.22.rows, s32[8192]{0:T(1024)S(1)} %get-tuple-element.23.ids, s32[8192]{0:T(1024)S(1)} %get-tuple-element.24.marks), custom_call_target="tpu_custom_call" | custom-call | flops 134217728 | bytes 524288 | tf_op jit(solution)/shard_map/more_sums/pallas_call | solution.py:182
  11.5 1.6 %collective-permute-done.3 = f32[2,296,128]{2,1,0:T(8,128)S(1)} collective-permute-done((f32[2,296,128]{2,1,0:T(8,128)S(1)}, f32[2,296,128]{2,1,0:T(8,128)S(1)}, u32[]{:S(2)}, u32[]{:S(2)}) %collective-permute-start.3) | collective-permute-done | bytes 303136 | tf_op jit(solution)/shard_map/ppermute | solution.py:369
  13.1 0.0 collective-permute-done.2
  13.1 0.1 add_add_fusion
  13.2 2.1 %collective-permute-start.6 = (f32[2,296,128]{2,1,0:T(8,128)S(1)}, f32[2,296,128]{2,1,0:T(8,128)S(1)}, u32[]{:S(2)}, u32[]{:S(2)}) collective-permute-start(f32[2,296,128]{2,1,0:T(8,128)S(1)} %add_add_fusion), channel_id=1, source_target_pairs={{0,4},{1,3},{2,6},{3,1},{4,0},{5,7},{6,2},{7,5},{8,12},{9,11},{10,... | collective-permute-start | bytes 909320 | tf_op jit(solution)/shard_map/ppermute | solution.py:369
  15.3 1.1 %more_sums.7 = (f32[2,296,128]{2,1,0:T(8,128)S(1)}, f32[2,296,128]{2,1,0:T(8,128)S(1)}) custom-call(s32[16]{0:T(128)S(4)} %get-tuple-element.33.listed, bf16[16,512,256]{2,1,0:T(8,128)(2,1)S(1)} %get-tuple-element.22.rows, s32[8192]{0:T(1024)S(1)} %get-tuple-element.23.ids, s32[8192]{0:T(1024)S(1)} %get-tuple-element.24.marks), custom_call_target="tpu_custom_call" | custom-call | flops 268435456 | bytes 1048576 | tf_op jit(solution)/shard_map/more_sums/pallas_call | solution.py:182
  16.4 0.1 collective-permute-start.4
  16.5 1.0 %collective-permute-done.5 = f32[2,296,128]{2,1,0:T(8,128)S(1)} collective-permute-done((f32[2,296,128]{2,1,0:T(8,128)S(1)}, f32[2,296,128]{2,1,0:T(8,128)S(1)}, u32[]{:S(2)}, u32[]{:S(2)}) %collective-permute-start.5) | collective-permute-done | bytes 303136 | tf_op jit(solution)/shard_map/ppermute | solution.py:369
  17.5 2.6 %collective-permute-done.6 = f32[2,296,128]{2,1,0:T(8,128)S(1)} collective-permute-done((f32[2,296,128]{2,1,0:T(8,128)S(1)}, f32[2,296,128]{2,1,0:T(8,128)S(1)}, u32[]{:S(2)}, u32[]{:S(2)}) %collective-permute-start.6) | collective-permute-done | bytes 303136 | tf_op jit(solution)/shard_map/ppermute | solution.py:369
  20.1 0.0 collective-permute-done.4
  20.1 0.1 slice_add_fusion
  20.2 3.1 %collective-permute-start.7 = (f32[1,296,128]{2,1,0:T(8,128)S(1)}, f32[1,296,128]{2,1,0:T(8,128)S(1)}, u32[]{:S(2)}, u32[]{:S(2)}) collective-permute-start(f32[1,296,128]{2,1,0:T(8,128)S(1)} %get-tuple-element.40), channel_id=1, source_target_pairs={{0,8},{1,9},{2,10},{3,11},{4,12},{5,13},{6,14},{7,15},{8,0},{9,1},... | collective-permute-start | bytes 454664 | tf_op jit(solution)/shard_map/ppermute | solution.py:369
  23.3 7.0 %collective-permute-done.7.came = f32[1,296,128]{2,1,0:T(8,128)S(1)} collective-permute-done((f32[1,296,128]{2,1,0:T(8,128)S(1)}, f32[1,296,128]{2,1,0:T(8,128)S(1)}, u32[]{:S(2)}, u32[]{:S(2)}) %collective-permute-start.7) | collective-permute-done | bytes 151584 | tf_op jit(solution)/shard_map/ppermute | solution.py:369
  30.3 6.9 %solve.1 = (f32[1,16,256]{2,1,0:T(8,128)}, bf16[1,16,384]{2,1,0:T(8,128)(2,1)S(1)}) custom-call(f32[1,296,128]{2,1,0:T(8,128)S(1)} %get-tuple-element.41.kept, f32[1,296,128]{2,1,0:T(8,128)S(1)} %collective-permute-done.7.came), custom_call_target="tpu_custom_call" | custom-call | tf_op jit(solution)/shard_map/solve/pallas_call | solution.py:303
  37.2 0.0 collective-permute-start.8
  37.2 4.7 %collective-permute-done.8 = bf16[1,16,384]{2,1,0:T(8,128)(2,1)S(1)} collective-permute-done((bf16[1,16,384]{2,1,0:T(8,128)(2,1)S(1)}, bf16[1,16,384]{2,1,0:T(8,128)(2,1)S(1)}, u32[]{:S(2)}, u32[]{:S(2)}) %collective-permute-start.8) | collective-permute-done | bytes 12320 | tf_op jit(solution)/shard_map/ppermute | solution.py:369
  41.9 1.1 %collective-permute-start.9 = (bf16[2,16,384]{2,1,0:T(8,128)(2,1)S(1)}, bf16[2,16,384]{2,1,0:T(8,128)(2,1)S(1)}, u32[]{:S(2)}, u32[]{:S(2)}) collective-permute-start(bf16[2,16,384]{2,1,0:T(8,128)(2,1)S(1)} %pad_maximum_fusion.1), channel_id=1, source_target_pairs={{0,4},{1,3},{2,6},{3,1},{4,0},{5,7},{6,2},{7,5},{8,12},{9,11},{10,... | collective-permute-start | bytes 73736 | tf_op jit(solution)/shard_map/ppermute | solution.py:369
  43.0 2.7 %collective-permute-done.9 = bf16[2,16,384]{2,1,0:T(8,128)(2,1)S(1)} collective-permute-done((bf16[2,16,384]{2,1,0:T(8,128)(2,1)S(1)}, bf16[2,16,384]{2,1,0:T(8,128)(2,1)S(1)}, u32[]{:S(2)}, u32[]{:S(2)}) %collective-permute-start.9) | collective-permute-done | bytes 24608 | tf_op jit(solution)/shard_map/ppermute | solution.py:369
  45.7 1.6 %collective-permute-start.10 = (bf16[4,16,384]{2,1,0:T(8,128)(2,1)S(1)}, bf16[4,16,384]{2,1,0:T(8,128)(2,1)S(1)}, u32[]{:S(2)}, u32[]{:S(2)}) collective-permute-start(bf16[4,16,384]{2,1,0:T(8,128)(2,1)S(1)} %pad_maximum_fusion), channel_id=1, source_target_pairs={{0,2},{1,5},{2,0},{3,7},{4,6},{5,1},{6,4},{7,3},{8,10},{9,13},{10,... | collective-permute-start | bytes 147464 | tf_op jit(solution)/shard_map/ppermute | solution.py:369
  47.4 2.5 %collective-permute-done.10 = bf16[4,16,384]{2,1,0:T(8,128)(2,1)S(1)} collective-permute-done((bf16[4,16,384]{2,1,0:T(8,128)(2,1)S(1)}, bf16[4,16,384]{2,1,0:T(8,128)(2,1)S(1)}, u32[]{:S(2)}, u32[]{:S(2)}) %collective-permute-start.10) | collective-permute-done | bytes 49184 | tf_op jit(solution)/shard_map/ppermute | solution.py:369
  49.9 0.1 collective-permute-start.11
  50.0 1.4 %half_scores.2.refs_0_ = f32[16,8192]{1,0:T(8,128)} custom-call(s32[16]{0:T(128)S(4)} %get-tuple-element.33.listed, bf16[16,512,256]{2,1,0:T(8,128)(2,1)S(1)} %get-tuple-element.22.rows, s32[8192]{0:T(1024)S(1)} %get-tuple-element.23.ids, bf16[8,16,384]{2,1,0:T(8,128)(2,1)S(1)} %constant_dynamic-update-slice_fusion.messages), custom_call_target="tpu_custom_call" | custom-call | tf_op jit(solution)/shard_map/half_scores/pallas_call | solution.py:348
  51.3 0.0 collective-permute-done.11.messages
  51.4 1.4 %half_scores.3 = f32[16,8192]{1,0:T(8,128)} custom-call(s32[16]{0:T(128)S(4)} %get-tuple-element.33.listed, bf16[16,512,256]{2,1,0:T(8,128)(2,1)S(1)} %get-tuple-element.22.rows, s32[8192]{0:T(1024)S(1)} %get-tuple-element.23.ids, bf16[8,16,384]{2,1,0:T(8,128)(2,1)S(1)} %collective-permute-done.11.messages, ...), custom_call_target="tpu_custom_call", output_to_operand_aliasing={{}: (4, {})} | custom-call | tf_op jit(solution)/shard_map/half_scores/pallas_call | solution.py:348
  (8 shorter events, 0.1 us)
Async XLA Ops:
  3.4 1.8 %collective-permute-start = (f32[2,296,128]{2,1,0:T(8,128)S(1)}, f32[2,296,128]{2,1,0:T(8,128)S(1)}, u32[]{:S(2)}, u32[]{:S(2)}) collective-permute-start(f32[2,296,128]{2,1,0:T(8,128)S(1)} %get-tuple-element.26), channel_id=1, source_target_pairs={{0,1},{1,0},{2,3},{3,2},{4,5},{5,4},{6,7},{7,6},{8,9},{9,8},{10,11... | collective-permute-start | bytes 909320 | tf_op jit(solution)/shard_map/ppermute | solution.py:369
  5.1 4.4 %collective-permute-start.1 = (f32[2,296,128]{2,1,0:T(8,128)S(1)}, f32[2,296,128]{2,1,0:T(8,128)S(1)}, u32[]{:S(2)}, u32[]{:S(2)}) collective-permute-start(f32[2,296,128]{2,1,0:T(8,128)S(1)} %get-tuple-element.29), channel_id=1, source_target_pairs={{0,1},{1,0},{2,3},{3,2},{4,5},{5,4},{6,7},{7,6},{8,9},{9,8},{10,11... | collective-permute-start | bytes 909320 | tf_op jit(solution)/shard_map/ppermute | solution.py:369
  5.3 7.8 %collective-permute-start.3 = (f32[2,296,128]{2,1,0:T(8,128)S(1)}, f32[2,296,128]{2,1,0:T(8,128)S(1)}, u32[]{:S(2)}, u32[]{:S(2)}) collective-permute-start(f32[2,296,128]{2,1,0:T(8,128)S(1)} %add.30), channel_id=1, source_target_pairs={{0,2},{1,5},{2,0},{3,7},{4,6},{5,1},{6,4},{7,3},{8,10},{9,13},{10,... | collective-permute-start | bytes 909320 | tf_op jit(solution)/shard_map/ppermute | solution.py:369
  9.4 3.7 %collective-permute-start.2 = (f32[2,296,128]{2,1,0:T(8,128)S(1)}, f32[2,296,128]{2,1,0:T(8,128)S(1)}, u32[]{:S(2)}, u32[]{:S(2)}) collective-permute-start(f32[2,296,128]{2,1,0:T(8,128)S(1)} %get-tuple-element.31), channel_id=1, source_target_pairs={{0,1},{1,0},{2,3},{3,2},{4,5},{5,4},{6,7},{7,6},{8,9},{9,8},{10,11... | collective-permute-start | bytes 909320 | tf_op jit(solution)/shard_map/ppermute | solution.py:369
  9.6 7.9 %collective-permute-start.5 = (f32[2,296,128]{2,1,0:T(8,128)S(1)}, f32[2,296,128]{2,1,0:T(8,128)S(1)}, u32[]{:S(2)}, u32[]{:S(2)}) collective-permute-start(f32[2,296,128]{2,1,0:T(8,128)S(1)} %add.31), channel_id=1, source_target_pairs={{0,2},{1,5},{2,0},{3,7},{4,6},{5,1},{6,4},{7,3},{8,10},{9,13},{10,... | collective-permute-start | bytes 909320 | tf_op jit(solution)/shard_map/ppermute | solution.py:369
  13.2 6.9 %collective-permute-start.6 = (f32[2,296,128]{2,1,0:T(8,128)S(1)}, f32[2,296,128]{2,1,0:T(8,128)S(1)}, u32[]{:S(2)}, u32[]{:S(2)}) collective-permute-start(f32[2,296,128]{2,1,0:T(8,128)S(1)} %add_add_fusion), channel_id=1, source_target_pairs={{0,4},{1,3},{2,6},{3,1},{4,0},{5,7},{6,2},{7,5},{8,12},{9,11},{10,... | collective-permute-start | bytes 909320 | tf_op jit(solution)/shard_map/ppermute | solution.py:369
  16.4 3.6 %collective-permute-start.4 = (f32[2,296,128]{2,1,0:T(8,128)S(1)}, f32[2,296,128]{2,1,0:T(8,128)S(1)}, u32[]{:S(2)}, u32[]{:S(2)}) collective-permute-start(f32[2,296,128]{2,1,0:T(8,128)S(1)} %get-tuple-element.35), channel_id=1, source_target_pairs={{0,1},{1,0},{2,3},{3,2},{4,5},{5,4},{6,7},{7,6},{8,9},{9,8},{10,11... | collective-permute-start | bytes 909320 | tf_op jit(solution)/shard_map/ppermute | solution.py:369
  20.2 10.1 %collective-permute-start.7 = (f32[1,296,128]{2,1,0:T(8,128)S(1)}, f32[1,296,128]{2,1,0:T(8,128)S(1)}, u32[]{:S(2)}, u32[]{:S(2)}) collective-permute-start(f32[1,296,128]{2,1,0:T(8,128)S(1)} %get-tuple-element.40), channel_id=1, source_target_pairs={{0,8},{1,9},{2,10},{3,11},{4,12},{5,13},{6,14},{7,15},{8,0},{9,1},... | collective-permute-start | bytes 454664 | tf_op jit(solution)/shard_map/ppermute | solution.py:369
  37.2 4.7 %collective-permute-start.8 = (bf16[1,16,384]{2,1,0:T(8,128)(2,1)S(1)}, bf16[1,16,384]{2,1,0:T(8,128)(2,1)S(1)}, u32[]{:S(2)}, u32[]{:S(2)}) collective-permute-start(bf16[1,16,384]{2,1,0:T(8,128)(2,1)S(1)} %get-tuple-element.39), channel_id=1, source_target_pairs={{0,8},{1,9},{2,10},{3,11},{4,12},{5,13},{6,14},{7,15},{8,0},{9,1},... | collective-permute-start | bytes 36872 | tf_op jit(solution)/shard_map/ppermute | solution.py:369
  41.9 3.8 %collective-permute-start.9 = (bf16[2,16,384]{2,1,0:T(8,128)(2,1)S(1)}, bf16[2,16,384]{2,1,0:T(8,128)(2,1)S(1)}, u32[]{:S(2)}, u32[]{:S(2)}) collective-permute-start(bf16[2,16,384]{2,1,0:T(8,128)(2,1)S(1)} %pad_maximum_fusion.1), channel_id=1, source_target_pairs={{0,4},{1,3},{2,6},{3,1},{4,0},{5,7},{6,2},{7,5},{8,12},{9,11},{10,... | collective-permute-start | bytes 73736 | tf_op jit(solution)/shard_map/ppermute | solution.py:369
  45.7 4.2 %collective-permute-start.10 = (bf16[4,16,384]{2,1,0:T(8,128)(2,1)S(1)}, bf16[4,16,384]{2,1,0:T(8,128)(2,1)S(1)}, u32[]{:S(2)}, u32[]{:S(2)}) collective-permute-start(bf16[4,16,384]{2,1,0:T(8,128)(2,1)S(1)} %pad_maximum_fusion), channel_id=1, source_target_pairs={{0,2},{1,5},{2,0},{3,7},{4,6},{5,1},{6,4},{7,3},{8,10},{9,13},{10,... | collective-permute-start | bytes 147464 | tf_op jit(solution)/shard_map/ppermute | solution.py:369
  49.9 1.4 %collective-permute-start.11 = (bf16[8,16,384]{2,1,0:T(8,128)(2,1)S(1)}, bf16[8,16,384]{2,1,0:T(8,128)(2,1)S(1)}, u32[]{:S(2)}, u32[]{:S(2)}) collective-permute-start(bf16[8,16,384]{2,1,0:T(8,128)(2,1)S(1)} %constant_dynamic-update-slice_fusion.messages), channel_id=1, source_target_pairs={{0,1},{1,0},{2,3},{3,2},{4,5},{5,4},{6,7},{7,6},{8,9},{9,8},{10,11... | collective-permute-start | bytes 294920 | tf_op jit(solution)/shard_map/ppermute | solution.py:369

commit v8 on v7

--- a/solution.py
+++ b/solution.py
@@ -220,7 +220,7 @@
         for k in range(0, PANEL, 2):
             c0, c1 = column[k], column[k + 1]
             group, turn = k // 8 * 8, k // 2 % 2
-            for c in range(k + 2, PANEL):
+            for c in range(k, PANEL):
                 columns[turn, c, 0:8] = column[c][group : group + 8, :]
             works[turn, 0:8] = work[group : group + 8, :]
 
@@ -228,9 +228,8 @@
                 rows8 = ref[pl.ds(at - group, 8, stride=0), :]
                 return jnp.concatenate([rows8] * (PANEL // 8), axis=0)
 
-            b00 = jnp.broadcast_to(c0[k : k + 1, :], (PANEL, LANES))
-            b10 = jnp.broadcast_to(c0[k + 1 : k + 2, :], (PANEL, LANES))
-            b11 = jnp.broadcast_to(c1[k + 1 : k + 2, :], (PANEL, LANES))
+            b00, b10 = (repeated(columns.at[turn, k], k + t) for t in range(2))
+            b11 = repeated(columns.at[turn, k + 1], k + 1)
             inverse = 1.0 / (b00 * b11 - b10 * b10)
             n00, n10, n11 = b11 * inverse, -b10 * inverse, b00 * inverse
             pair = (rows == k) | (rows == k + 1)
@@ -256,7 +255,11 @@
         needed = last + PANEL if last + PANEL < size else 0
         for base in sorted(starts, key=lambda t: not t <= needed < t + LANES):
             part = over_rows(left[:, base : base + LANES], right)
-            matrix[base : base + LANES, :] = jnp.where(inside, 0.0, matrix[base : base + LANES, :]) - part
+            for lane in starts:
+                block = matrix[base : base + LANES, lane : lane + LANES]
+                if lane <= first < lane + LANES:
+                    block = jnp.where(inside[:, lane : lane + LANES], 0.0, block)
+                matrix[base : base + LANES, lane : lane + LANES] = block - part[:, lane : lane + LANES]
         matrix[first:last, :] = work
 
 

time: 52.9 us -> 52.8 us (level)
  no operation moved by 1% of the time
where the time goes in v8:
time: 52.8 us; the launch traced here: 52.6 us
  waiting for transfers between devices  22.2 us (42%)
  Pallas kernels  16.3 us (31%)
  starting transfers between devices  13.2 us (25%)
  between operations  0.74 us (1%)
    ppermute x12, waiting for transfers between devices, swap(): lax.ppermute(x, 'rows', [(r, r ^ distances[r & 1]) for r in range(ranks)])  22.2 us
    ppermute x12, starting transfers between devices, swap(): lax.ppermute(x, 'rows', [(r, r ^ distances[r & 1]) for r in range(ranks)])  13.2 us
    pallas_call x1, Pallas kernels, solve(): pl.pallas_call(solve_kernel, out_shape=(jax.ShapeDtypeStruct((1, CLASSES,...  6.78 us
    pallas_call x4, Pallas kernels, more_sums(): pl.pallas_call(functools.partial(more_sums_kernel, chunks), out_shape=(pa...  3.97 us
    pallas_call x1, Pallas kernels, first_sums(): pl.pallas_call(functools.partial(first_sums_kernel, bits), out_shape=(pac...  2.8 us
    pallas_call x2, Pallas kernels, half_scores(): pl.pallas_call(functools.partial(scores_kernel, parity), out_shape=pltpu....  2.71 us
  transfers between devices with their start and end apart: 12, of which 7 were waited for; matrix products, arithmetic and copies ran while one was open for 0% of the time, Pallas kernels for 10%

profile of v8, /device:TPU:0, one launch (start us, length us, event | category | flops | bytes accessed | tf_op | source)
XLA Modules:
  0.0 52.6 jit_solution(11681214647799924638)
XLA Ops:
  0.6 2.8 %first_sums.1 = (f32[2,296,128]{2,1,0:T(8,128)S(1)}, s32[16]{0:T(128)S(4)}, bf16[16,512,256]{2,1,0:T(8,128)(2,1)S(1)}, s32[8192]{0:T(1024)S(1)}, s32[8192]{0:T(1024)S(1)}) custom-call(s32[16]{0:T(128)} %owners.1, bf16[8192,256]{1,0:T(8,128)(2,1)} %features.1, s32[8192]{0:T(1024)} %node_ids.1, s32[8192]{0:T(1024)} %labels.1), custom_call_target="tpu_custom_call" | custom-call | tf_op jit(solution)/shard_map/first_sums/pallas_call | solution.py:142
  3.4 0.5 collective-permute-start
  4.0 1.1 %more_sums.4 = (f32[2,296,128]{2,1,0:T(8,128)S(1)}, f32[2,296,128]{2,1,0:T(8,128)S(1)}) custom-call(s32[16]{0:T(128)S(4)} %get-tuple-element.33.listed, bf16[16,512,256]{2,1,0:T(8,128)(2,1)S(1)} %get-tuple-element.22.rows, s32[8192]{0:T(1024)S(1)} %get-tuple-element.23.ids, s32[8192]{0:T(1024)S(1)} %get-tuple-element.24.marks), custom_call_target="tpu_custom_call" | custom-call | flops 268435456 | bytes 1048576 | tf_op jit(solution)/shard_map/more_sums/pallas_call | solution.py:182
  5.1 0.1 collective-permute-start.1
  5.2 0.0 collective-permute-done
  5.3 3.0 %collective-permute-start.3 = (f32[2,296,128]{2,1,0:T(8,128)S(1)}, f32[2,296,128]{2,1,0:T(8,128)S(1)}, u32[]{:S(2)}, u32[]{:S(2)}) collective-permute-start(f32[2,296,128]{2,1,0:T(8,128)S(1)} %add.30), channel_id=1, source_target_pairs={{0,2},{1,5},{2,0},{3,7},{4,6},{5,1},{6,4},{7,3},{8,10},{9,13},{10,... | collective-permute-start | bytes 909320 | tf_op jit(solution)/shard_map/ppermute | solution.py:372
  8.3 1.1 %more_sums.5 = (f32[2,296,128]{2,1,0:T(8,128)S(1)}, f32[2,296,128]{2,1,0:T(8,128)S(1)}) custom-call(s32[16]{0:T(128)S(4)} %get-tuple-element.33.listed, bf16[16,512,256]{2,1,0:T(8,128)(2,1)S(1)} %get-tuple-element.22.rows, s32[8192]{0:T(1024)S(1)} %get-tuple-element.23.ids, s32[8192]{0:T(1024)S(1)} %get-tuple-element.24.marks), custom_call_target="tpu_custom_call" | custom-call | flops 268435456 | bytes 1048576 | tf_op jit(solution)/shard_map/more_sums/pallas_call | solution.py:182
  9.4 0.1 collective-permute-start.2
  9.5 0.0 collective-permute-done.1
  9.6 1.4 %collective-permute-start.5 = (f32[2,296,128]{2,1,0:T(8,128)S(1)}, f32[2,296,128]{2,1,0:T(8,128)S(1)}, u32[]{:S(2)}, u32[]{:S(2)}) collective-permute-start(f32[2,296,128]{2,1,0:T(8,128)S(1)} %add.31), channel_id=1, source_target_pairs={{0,2},{1,5},{2,0},{3,7},{4,6},{5,1},{6,4},{7,3},{8,10},{9,13},{10,... | collective-permute-start | bytes 909320 | tf_op jit(solution)/shard_map/ppermute | solution.py:372
  10.9 0.6 %more_sums.6 = f32[2,296,128]{2,1,0:T(8,128)S(1)} custom-call(s32[16]{0:T(128)S(4)} %get-tuple-element.33.listed, bf16[16,512,256]{2,1,0:T(8,128)(2,1)S(1)} %get-tuple-element.22.rows, s32[8192]{0:T(1024)S(1)} %get-tuple-element.23.ids, s32[8192]{0:T(1024)S(1)} %get-tuple-element.24.marks), custom_call_target="tpu_custom_call" | custom-call | flops 134217728 | bytes 524288 | tf_op jit(solution)/shard_map/more_sums/pallas_call | solution.py:182
  11.5 1.6 %collective-permute-done.3 = f32[2,296,128]{2,1,0:T(8,128)S(1)} collective-permute-done((f32[2,296,128]{2,1,0:T(8,128)S(1)}, f32[2,296,128]{2,1,0:T(8,128)S(1)}, u32[]{:S(2)}, u32[]{:S(2)}) %collective-permute-start.3) | collective-permute-done | bytes 303136 | tf_op jit(solution)/shard_map/ppermute | solution.py:372
  13.1 0.0 collective-permute-done.2
  13.1 0.1 add_add_fusion
  13.2 2.1 %collective-permute-start.6 = (f32[2,296,128]{2,1,0:T(8,128)S(1)}, f32[2,296,128]{2,1,0:T(8,128)S(1)}, u32[]{:S(2)}, u32[]{:S(2)}) collective-permute-start(f32[2,296,128]{2,1,0:T(8,128)S(1)} %add_add_fusion), channel_id=1, source_target_pairs={{0,4},{1,3},{2,6},{3,1},{4,0},{5,7},{6,2},{7,5},{8,12},{9,11},{10,... | collective-permute-start | bytes 909320 | tf_op jit(solution)/shard_map/ppermute | solution.py:372
  15.3 1.1 %more_sums.7 = (f32[2,296,128]{2,1,0:T(8,128)S(1)}, f32[2,296,128]{2,1,0:T(8,128)S(1)}) custom-call(s32[16]{0:T(128)S(4)} %get-tuple-element.33.listed, bf16[16,512,256]{2,1,0:T(8,128)(2,1)S(1)} %get-tuple-element.22.rows, s32[8192]{0:T(1024)S(1)} %get-tuple-element.23.ids, s32[8192]{0:T(1024)S(1)} %get-tuple-element.24.marks), custom_call_target="tpu_custom_call" | custom-call | flops 268435456 | bytes 1048576 | tf_op jit(solution)/shard_map/more_sums/pallas_call | solution.py:182
  16.4 0.1 collective-permute-start.4
  16.5 1.0 %collective-permute-done.5 = f32[2,296,128]{2,1,0:T(8,128)S(1)} collective-permute-done((f32[2,296,128]{2,1,0:T(8,128)S(1)}, f32[2,296,128]{2,1,0:T(8,128)S(1)}, u32[]{:S(2)}, u32[]{:S(2)}) %collective-permute-start.5) | collective-permute-done | bytes 303136 | tf_op jit(solution)/shard_map/ppermute | solution.py:372
  17.5 2.6 %collective-permute-done.6 = f32[2,296,128]{2,1,0:T(8,128)S(1)} collective-permute-done((f32[2,296,128]{2,1,0:T(8,128)S(1)}, f32[2,296,128]{2,1,0:T(8,128)S(1)}, u32[]{:S(2)}, u32[]{:S(2)}) %collective-permute-start.6) | collective-permute-done | bytes 303136 | tf_op jit(solution)/shard_map/ppermute | solution.py:372
  20.1 0.0 collective-permute-done.4
  20.1 0.1 slice_add_fusion
  20.2 3.1 %collective-permute-start.7 = (f32[1,296,128]{2,1,0:T(8,128)S(1)}, f32[1,296,128]{2,1,0:T(8,128)S(1)}, u32[]{:S(2)}, u32[]{:S(2)}) collective-permute-start(f32[1,296,128]{2,1,0:T(8,128)S(1)} %get-tuple-element.40), channel_id=1, source_target_pairs={{0,8},{1,9},{2,10},{3,11},{4,12},{5,13},{6,14},{7,15},{8,0},{9,1},... | collective-permute-start | bytes 454664 | tf_op jit(solution)/shard_map/ppermute | solution.py:372
  23.3 7.0 %collective-permute-done.7.came = f32[1,296,128]{2,1,0:T(8,128)S(1)} collective-permute-done((f32[1,296,128]{2,1,0:T(8,128)S(1)}, f32[1,296,128]{2,1,0:T(8,128)S(1)}, u32[]{:S(2)}, u32[]{:S(2)}) %collective-permute-start.7) | collective-permute-done | bytes 151584 | tf_op jit(solution)/shard_map/ppermute | solution.py:372
  30.4 6.8 %solve.1 = (f32[1,16,256]{2,1,0:T(8,128)}, bf16[1,16,384]{2,1,0:T(8,128)(2,1)S(1)}) custom-call(f32[1,296,128]{2,1,0:T(8,128)S(1)} %get-tuple-element.41.kept, f32[1,296,128]{2,1,0:T(8,128)S(1)} %collective-permute-done.7.came), custom_call_target="tpu_custom_call" | custom-call | tf_op jit(solution)/shard_map/solve/pallas_call | solution.py:306
  37.1 0.0 collective-permute-start.8
  37.1 4.7 %collective-permute-done.8 = bf16[1,16,384]{2,1,0:T(8,128)(2,1)S(1)} collective-permute-done((bf16[1,16,384]{2,1,0:T(8,128)(2,1)S(1)}, bf16[1,16,384]{2,1,0:T(8,128)(2,1)S(1)}, u32[]{:S(2)}, u32[]{:S(2)}) %collective-permute-start.8) | collective-permute-done | bytes 12320 | tf_op jit(solution)/shard_map/ppermute | solution.py:372
  41.8 1.1 %collective-permute-start.9 = (bf16[2,16,384]{2,1,0:T(8,128)(2,1)S(1)}, bf16[2,16,384]{2,1,0:T(8,128)(2,1)S(1)}, u32[]{:S(2)}, u32[]{:S(2)}) collective-permute-start(bf16[2,16,384]{2,1,0:T(8,128)(2,1)S(1)} %pad_maximum_fusion.1), channel_id=1, source_target_pairs={{0,4},{1,3},{2,6},{3,1},{4,0},{5,7},{6,2},{7,5},{8,12},{9,11},{10,... | collective-permute-start | bytes 73736 | tf_op jit(solution)/shard_map/ppermute | solution.py:372
  42.9 2.7 %collective-permute-done.9 = bf16[2,16,384]{2,1,0:T(8,128)(2,1)S(1)} collective-permute-done((bf16[2,16,384]{2,1,0:T(8,128)(2,1)S(1)}, bf16[2,16,384]{2,1,0:T(8,128)(2,1)S(1)}, u32[]{:S(2)}, u32[]{:S(2)}) %collective-permute-start.9) | collective-permute-done | bytes 24608 | tf_op jit(solution)/shard_map/ppermute | solution.py:372
  45.7 1.5 %collective-permute-start.10 = (bf16[4,16,384]{2,1,0:T(8,128)(2,1)S(1)}, bf16[4,16,384]{2,1,0:T(8,128)(2,1)S(1)}, u32[]{:S(2)}, u32[]{:S(2)}) collective-permute-start(bf16[4,16,384]{2,1,0:T(8,128)(2,1)S(1)} %pad_maximum_fusion), channel_id=1, source_target_pairs={{0,2},{1,5},{2,0},{3,7},{4,6},{5,1},{6,4},{7,3},{8,10},{9,13},{10,... | collective-permute-start | bytes 147464 | tf_op jit(solution)/shard_map/ppermute | solution.py:372
  47.2 2.6 %collective-permute-done.10 = bf16[4,16,384]{2,1,0:T(8,128)(2,1)S(1)} collective-permute-done((bf16[4,16,384]{2,1,0:T(8,128)(2,1)S(1)}, bf16[4,16,384]{2,1,0:T(8,128)(2,1)S(1)}, u32[]{:S(2)}, u32[]{:S(2)}) %collective-permute-start.10) | collective-permute-done | bytes 49184 | tf_op jit(solution)/shard_map/ppermute | solution.py:372
  49.8 0.1 collective-permute-start.11
  49.9 1.4 %half_scores.2.refs_0_ = f32[16,8192]{1,0:T(8,128)} custom-call(s32[16]{0:T(128)S(4)} %get-tuple-element.33.listed, bf16[16,512,256]{2,1,0:T(8,128)(2,1)S(1)} %get-tuple-element.22.rows, s32[8192]{0:T(1024)S(1)} %get-tuple-element.23.ids, bf16[8,16,384]{2,1,0:T(8,128)(2,1)S(1)} %constant_dynamic-update-slice_fusion.messages), custom_call_target="tpu_custom_call" | custom-call | tf_op jit(solution)/shard_map/half_scores/pallas_call | solution.py:351
  51.3 0.0 collective-permute-done.11.messages
  51.3 1.4 %half_scores.3 = f32[16,8192]{1,0:T(8,128)} custom-call(s32[16]{0:T(128)S(4)} %get-tuple-element.33.listed, bf16[16,512,256]{2,1,0:T(8,128)(2,1)S(1)} %get-tuple-element.22.rows, s32[8192]{0:T(1024)S(1)} %get-tuple-element.23.ids, bf16[8,16,384]{2,1,0:T(8,128)(2,1)S(1)} %collective-permute-done.11.messages, ...), custom_call_target="tpu_custom_call", output_to_operand_aliasing={{}: (4, {})} | custom-call | tf_op jit(solution)/shard_map/half_scores/pallas_call | solution.py:351
  (8 shorter events, 0.1 us)
Async XLA Ops:
  3.4 1.8 %collective-permute-start = (f32[2,296,128]{2,1,0:T(8,128)S(1)}, f32[2,296,128]{2,1,0:T(8,128)S(1)}, u32[]{:S(2)}, u32[]{:S(2)}) collective-permute-start(f32[2,296,128]{2,1,0:T(8,128)S(1)} %get-tuple-element.26), channel_id=1, source_target_pairs={{0,1},{1,0},{2,3},{3,2},{4,5},{5,4},{6,7},{7,6},{8,9},{9,8},{10,11... | collective-permute-start | bytes 909320 | tf_op jit(solution)/shard_map/ppermute | solution.py:372
  5.1 4.4 %collective-permute-start.1 = (f32[2,296,128]{2,1,0:T(8,128)S(1)}, f32[2,296,128]{2,1,0:T(8,128)S(1)}, u32[]{:S(2)}, u32[]{:S(2)}) collective-permute-start(f32[2,296,128]{2,1,0:T(8,128)S(1)} %get-tuple-element.29), channel_id=1, source_target_pairs={{0,1},{1,0},{2,3},{3,2},{4,5},{5,4},{6,7},{7,6},{8,9},{9,8},{10,11... | collective-permute-start | bytes 909320 | tf_op jit(solution)/shard_map/ppermute | solution.py:372
  5.3 7.8 %collective-permute-start.3 = (f32[2,296,128]{2,1,0:T(8,128)S(1)}, f32[2,296,128]{2,1,0:T(8,128)S(1)}, u32[]{:S(2)}, u32[]{:S(2)}) collective-permute-start(f32[2,296,128]{2,1,0:T(8,128)S(1)} %add.30), channel_id=1, source_target_pairs={{0,2},{1,5},{2,0},{3,7},{4,6},{5,1},{6,4},{7,3},{8,10},{9,13},{10,... | collective-permute-start | bytes 909320 | tf_op jit(solution)/shard_map/ppermute | solution.py:372
  9.4 3.6 %collective-permute-start.2 = (f32[2,296,128]{2,1,0:T(8,128)S(1)}, f32[2,296,128]{2,1,0:T(8,128)S(1)}, u32[]{:S(2)}, u32[]{:S(2)}) collective-permute-start(f32[2,296,128]{2,1,0:T(8,128)S(1)} %get-tuple-element.31), channel_id=1, source_target_pairs={{0,1},{1,0},{2,3},{3,2},{4,5},{5,4},{6,7},{7,6},{8,9},{9,8},{10,11... | collective-permute-start | bytes 909320 | tf_op jit(solution)/shard_map/ppermute | solution.py:372
  9.6 7.9 %collective-permute-start.5 = (f32[2,296,128]{2,1,0:T(8,128)S(1)}, f32[2,296,128]{2,1,0:T(8,128)S(1)}, u32[]{:S(2)}, u32[]{:S(2)}) collective-permute-start(f32[2,296,128]{2,1,0:T(8,128)S(1)} %add.31), channel_id=1, source_target_pairs={{0,2},{1,5},{2,0},{3,7},{4,6},{5,1},{6,4},{7,3},{8,10},{9,13},{10,... | collective-permute-start | bytes 909320 | tf_op jit(solution)/shard_map/ppermute | solution.py:372
  13.2 6.9 %collective-permute-start.6 = (f32[2,296,128]{2,1,0:T(8,128)S(1)}, f32[2,296,128]{2,1,0:T(8,128)S(1)}, u32[]{:S(2)}, u32[]{:S(2)}) collective-permute-start(f32[2,296,128]{2,1,0:T(8,128)S(1)} %add_add_fusion), channel_id=1, source_target_pairs={{0,4},{1,3},{2,6},{3,1},{4,0},{5,7},{6,2},{7,5},{8,12},{9,11},{10,... | collective-permute-start | bytes 909320 | tf_op jit(solution)/shard_map/ppermute | solution.py:372
  16.4 3.7 %collective-permute-start.4 = (f32[2,296,128]{2,1,0:T(8,128)S(1)}, f32[2,296,128]{2,1,0:T(8,128)S(1)}, u32[]{:S(2)}, u32[]{:S(2)}) collective-permute-start(f32[2,296,128]{2,1,0:T(8,128)S(1)} %get-tuple-element.35), channel_id=1, source_target_pairs={{0,1},{1,0},{2,3},{3,2},{4,5},{5,4},{6,7},{7,6},{8,9},{9,8},{10,11... | collective-permute-start | bytes 909320 | tf_op jit(solution)/shard_map/ppermute | solution.py:372
  20.2 10.2 %collective-permute-start.7 = (f32[1,296,128]{2,1,0:T(8,128)S(1)}, f32[1,296,128]{2,1,0:T(8,128)S(1)}, u32[]{:S(2)}, u32[]{:S(2)}) collective-permute-start(f32[1,296,128]{2,1,0:T(8,128)S(1)} %get-tuple-element.40), channel_id=1, source_target_pairs={{0,8},{1,9},{2,10},{3,11},{4,12},{5,13},{6,14},{7,15},{8,0},{9,1},... | collective-permute-start | bytes 454664 | tf_op jit(solution)/shard_map/ppermute | solution.py:372
  37.1 4.7 %collective-permute-start.8 = (bf16[1,16,384]{2,1,0:T(8,128)(2,1)S(1)}, bf16[1,16,384]{2,1,0:T(8,128)(2,1)S(1)}, u32[]{:S(2)}, u32[]{:S(2)}) collective-permute-start(bf16[1,16,384]{2,1,0:T(8,128)(2,1)S(1)} %get-tuple-element.39), channel_id=1, source_target_pairs={{0,8},{1,9},{2,10},{3,11},{4,12},{5,13},{6,14},{7,15},{8,0},{9,1},... | collective-permute-start | bytes 36872 | tf_op jit(solution)/shard_map/ppermute | solution.py:372
  41.8 3.8 %collective-permute-start.9 = (bf16[2,16,384]{2,1,0:T(8,128)(2,1)S(1)}, bf16[2,16,384]{2,1,0:T(8,128)(2,1)S(1)}, u32[]{:S(2)}, u32[]{:S(2)}) collective-permute-start(bf16[2,16,384]{2,1,0:T(8,128)(2,1)S(1)} %pad_maximum_fusion.1), channel_id=1, source_target_pairs={{0,4},{1,3},{2,6},{3,1},{4,0},{5,7},{6,2},{7,5},{8,12},{9,11},{10,... | collective-permute-start | bytes 73736 | tf_op jit(solution)/shard_map/ppermute | solution.py:372
  45.7 4.2 %collective-permute-start.10 = (bf16[4,16,384]{2,1,0:T(8,128)(2,1)S(1)}, bf16[4,16,384]{2,1,0:T(8,128)(2,1)S(1)}, u32[]{:S(2)}, u32[]{:S(2)}) collective-permute-start(bf16[4,16,384]{2,1,0:T(8,128)(2,1)S(1)} %pad_maximum_fusion), channel_id=1, source_target_pairs={{0,2},{1,5},{2,0},{3,7},{4,6},{5,1},{6,4},{7,3},{8,10},{9,13},{10,... | collective-permute-start | bytes 147464 | tf_op jit(solution)/shard_map/ppermute | solution.py:372
  49.8 1.4 %collective-permute-start.11 = (bf16[8,16,384]{2,1,0:T(8,128)(2,1)S(1)}, bf16[8,16,384]{2,1,0:T(8,128)(2,1)S(1)}, u32[]{:S(2)}, u32[]{:S(2)}) collective-permute-start(bf16[8,16,384]{2,1,0:T(8,128)(2,1)S(1)} %constant_dynamic-update-slice_fusion.messages), channel_id=1, source_target_pairs={{0,1},{1,0},{2,3},{3,2},{4,5},{5,4},{6,7},{7,6},{8,9},{9,8},{10,11... | collective-permute-start | bytes 294920 | tf_op jit(solution)/shard_map/ppermute | solution.py:372

commit v9 on v8

--- a/solution.py
+++ b/solution.py
@@ -113,7 +113,7 @@
         return pltpu.make_async_copy(features.at[pl.ds(start, segment)], rows.at[node], row_sems.at[node])
 
     for node in range(nodes):
-        row_copy(node).start()
+        row_copy(node).start(priority=node % 2)
     copies[0].wait()
     me = lax.axis_index("rows")
     for node in range(nodes):

time: 52.8 us -> 52.5 us (level)
  no operation moved by 1% of the time
where the time goes in v9:
time: 52.5 us; the launch traced here: 52.3 us
  waiting for transfers between devices  21.9 us (42%)
  Pallas kernels  15.8 us (30%)
  starting transfers between devices  13.6 us (26%)
  between operations  0.73 us (1%)
    ppermute x12, waiting for transfers between devices, swap(): lax.ppermute(x, 'rows', [(r, r ^ distances[r & 1]) for r in range(ranks)])  21.9 us
    ppermute x12, starting transfers between devices, swap(): lax.ppermute(x, 'rows', [(r, r ^ distances[r & 1]) for r in range(ranks)])  13.6 us
    pallas_call x1, Pallas kernels, solve(): pl.pallas_call(solve_kernel, out_shape=(jax.ShapeDtypeStruct((1, CLASSES,...  6.78 us
    pallas_call x4, Pallas kernels, more_sums(): pl.pallas_call(functools.partial(more_sums_kernel, chunks), out_shape=(pa...  3.97 us
    pallas_call x2, Pallas kernels, half_scores(): pl.pallas_call(functools.partial(scores_kernel, parity), out_shape=pltpu....  2.71 us
    pallas_call x1, Pallas kernels, first_sums(): pl.pallas_call(functools.partial(first_sums_kernel, bits), out_shape=(pac...  2.32 us
  transfers between devices with their start and end apart: 12, of which 7 were waited for; matrix products, arithmetic and copies ran while one was open for 0% of the time, Pallas kernels for 10%

profile of v9, /device:TPU:0, one launch (start us, length us, event | category | flops | bytes accessed | tf_op | source)
XLA Modules:
  0.0 52.3 jit_solution(1976432510415980847)
XLA Ops:
  0.6 2.3 %first_sums.1 = (f32[2,296,128]{2,1,0:T(8,128)S(1)}, s32[16]{0:T(128)S(4)}, bf16[16,512,256]{2,1,0:T(8,128)(2,1)S(1)}, s32[8192]{0:T(1024)S(1)}, s32[8192]{0:T(1024)S(1)}) custom-call(s32[16]{0:T(128)} %owners.1, bf16[8192,256]{1,0:T(8,128)(2,1)} %features.1, s32[8192]{0:T(1024)} %node_ids.1, s32[8192]{0:T(1024)} %labels.1), custom_call_target="tpu_custom_call" | custom-call | tf_op jit(solution)/shard_map/first_sums/pallas_call | solution.py:142
  3.0 0.5 collective-permute-start
  3.5 1.1 %more_sums.4 = (f32[2,296,128]{2,1,0:T(8,128)S(1)}, f32[2,296,128]{2,1,0:T(8,128)S(1)}) custom-call(s32[16]{0:T(128)S(4)} %get-tuple-element.33.listed, bf16[16,512,256]{2,1,0:T(8,128)(2,1)S(1)} %get-tuple-element.22.rows, s32[8192]{0:T(1024)S(1)} %get-tuple-element.23.ids, s32[8192]{0:T(1024)S(1)} %get-tuple-element.24.marks), custom_call_target="tpu_custom_call" | custom-call | flops 268435456 | bytes 1048576 | tf_op jit(solution)/shard_map/more_sums/pallas_call | solution.py:182
  4.6 0.1 collective-permute-start.1
  4.7 0.0 collective-permute-done
  4.8 3.0 %collective-permute-start.3 = (f32[2,296,128]{2,1,0:T(8,128)S(1)}, f32[2,296,128]{2,1,0:T(8,128)S(1)}, u32[]{:S(2)}, u32[]{:S(2)}) collective-permute-start(f32[2,296,128]{2,1,0:T(8,128)S(1)} %add.30), channel_id=1, source_target_pairs={{0,2},{1,5},{2,0},{3,7},{4,6},{5,1},{6,4},{7,3},{8,10},{9,13},{10,... | collective-permute-start | bytes 909320 | tf_op jit(solution)/shard_map/ppermute | solution.py:372
  7.8 1.1 %more_sums.5 = (f32[2,296,128]{2,1,0:T(8,128)S(1)}, f32[2,296,128]{2,1,0:T(8,128)S(1)}) custom-call(s32[16]{0:T(128)S(4)} %get-tuple-element.33.listed, bf16[16,512,256]{2,1,0:T(8,128)(2,1)S(1)} %get-tuple-element.22.rows, s32[8192]{0:T(1024)S(1)} %get-tuple-element.23.ids, s32[8192]{0:T(1024)S(1)} %get-tuple-element.24.marks), custom_call_target="tpu_custom_call" | custom-call | flops 268435456 | bytes 1048576 | tf_op jit(solution)/shard_map/more_sums/pallas_call | solution.py:182
  9.0 0.2 collective-permute-start.2
  9.2 0.0 collective-permute-done.1
  9.3 1.6 %collective-permute-start.5 = (f32[2,296,128]{2,1,0:T(8,128)S(1)}, f32[2,296,128]{2,1,0:T(8,128)S(1)}, u32[]{:S(2)}, u32[]{:S(2)}) collective-permute-start(f32[2,296,128]{2,1,0:T(8,128)S(1)} %add.31), channel_id=1, source_target_pairs={{0,2},{1,5},{2,0},{3,7},{4,6},{5,1},{6,4},{7,3},{8,10},{9,13},{10,... | collective-permute-start | bytes 909320 | tf_op jit(solution)/shard_map/ppermute | solution.py:372
  10.9 0.6 %more_sums.6 = f32[2,296,128]{2,1,0:T(8,128)S(1)} custom-call(s32[16]{0:T(128)S(4)} %get-tuple-element.33.listed, bf16[16,512,256]{2,1,0:T(8,128)(2,1)S(1)} %get-tuple-element.22.rows, s32[8192]{0:T(1024)S(1)} %get-tuple-element.23.ids, s32[8192]{0:T(1024)S(1)} %get-tuple-element.24.marks), custom_call_target="tpu_custom_call" | custom-call | flops 134217728 | bytes 524288 | tf_op jit(solution)/shard_map/more_sums/pallas_call | solution.py:182
  11.5 1.2 %collective-permute-done.3 = f32[2,296,128]{2,1,0:T(8,128)S(1)} collective-permute-done((f32[2,296,128]{2,1,0:T(8,128)S(1)}, f32[2,296,128]{2,1,0:T(8,128)S(1)}, u32[]{:S(2)}, u32[]{:S(2)}) %collective-permute-start.3) | collective-permute-done | bytes 303136 | tf_op jit(solution)/shard_map/ppermute | solution.py:372
  12.6 0.0 collective-permute-done.2
  12.6 0.1 add_add_fusion
  12.7 2.5 %collective-permute-start.6 = (f32[2,296,128]{2,1,0:T(8,128)S(1)}, f32[2,296,128]{2,1,0:T(8,128)S(1)}, u32[]{:S(2)}, u32[]{:S(2)}) collective-permute-start(f32[2,296,128]{2,1,0:T(8,128)S(1)} %add_add_fusion), channel_id=1, source_target_pairs={{0,4},{1,3},{2,6},{3,1},{4,0},{5,7},{6,2},{7,5},{8,12},{9,11},{10,... | collective-permute-start | bytes 909320 | tf_op jit(solution)/shard_map/ppermute | solution.py:372
  15.2 1.1 %more_sums.7 = (f32[2,296,128]{2,1,0:T(8,128)S(1)}, f32[2,296,128]{2,1,0:T(8,128)S(1)}) custom-call(s32[16]{0:T(128)S(4)} %get-tuple-element.33.listed, bf16[16,512,256]{2,1,0:T(8,128)(2,1)S(1)} %get-tuple-element.22.rows, s32[8192]{0:T(1024)S(1)} %get-tuple-element.23.ids, s32[8192]{0:T(1024)S(1)} %get-tuple-element.24.marks), custom_call_target="tpu_custom_call" | custom-call | flops 268435456 | bytes 1048576 | tf_op jit(solution)/shard_map/more_sums/pallas_call | solution.py:182
  16.3 0.1 collective-permute-start.4
  16.4 0.6 %collective-permute-done.5 = f32[2,296,128]{2,1,0:T(8,128)S(1)} collective-permute-done((f32[2,296,128]{2,1,0:T(8,128)S(1)}, f32[2,296,128]{2,1,0:T(8,128)S(1)}, u32[]{:S(2)}, u32[]{:S(2)}) %collective-permute-start.5) | collective-permute-done | bytes 303136 | tf_op jit(solution)/shard_map/ppermute | solution.py:372
  17.0 3.0 %collective-permute-done.6 = f32[2,296,128]{2,1,0:T(8,128)S(1)} collective-permute-done((f32[2,296,128]{2,1,0:T(8,128)S(1)}, f32[2,296,128]{2,1,0:T(8,128)S(1)}, u32[]{:S(2)}, u32[]{:S(2)}) %collective-permute-start.6) | collective-permute-done | bytes 303136 | tf_op jit(solution)/shard_map/ppermute | solution.py:372
  20.0 0.0 collective-permute-done.4
  20.0 0.1 slice_add_fusion
  20.1 2.9 %collective-permute-start.7 = (f32[1,296,128]{2,1,0:T(8,128)S(1)}, f32[1,296,128]{2,1,0:T(8,128)S(1)}, u32[]{:S(2)}, u32[]{:S(2)}) collective-permute-start(f32[1,296,128]{2,1,0:T(8,128)S(1)} %get-tuple-element.40), channel_id=1, source_target_pairs={{0,8},{1,9},{2,10},{3,11},{4,12},{5,13},{6,14},{7,15},{8,0},{9,1},... | collective-permute-start | bytes 454664 | tf_op jit(solution)/shard_map/ppermute | solution.py:372
  23.0 7.0 %collective-permute-done.7.came = f32[1,296,128]{2,1,0:T(8,128)S(1)} collective-permute-done((f32[1,296,128]{2,1,0:T(8,128)S(1)}, f32[1,296,128]{2,1,0:T(8,128)S(1)}, u32[]{:S(2)}, u32[]{:S(2)}) %collective-permute-start.7) | collective-permute-done | bytes 151584 | tf_op jit(solution)/shard_map/ppermute | solution.py:372
  30.1 6.8 %solve.1 = (f32[1,16,256]{2,1,0:T(8,128)}, bf16[1,16,384]{2,1,0:T(8,128)(2,1)S(1)}) custom-call(f32[1,296,128]{2,1,0:T(8,128)S(1)} %get-tuple-element.41.kept, f32[1,296,128]{2,1,0:T(8,128)S(1)} %collective-permute-done.7.came), custom_call_target="tpu_custom_call" | custom-call | tf_op jit(solution)/shard_map/solve/pallas_call | solution.py:306
  36.8 0.0 collective-permute-start.8
  36.8 4.7 %collective-permute-done.8 = bf16[1,16,384]{2,1,0:T(8,128)(2,1)S(1)} collective-permute-done((bf16[1,16,384]{2,1,0:T(8,128)(2,1)S(1)}, bf16[1,16,384]{2,1,0:T(8,128)(2,1)S(1)}, u32[]{:S(2)}, u32[]{:S(2)}) %collective-permute-start.8) | collective-permute-done | bytes 12320 | tf_op jit(solution)/shard_map/ppermute | solution.py:372
  41.5 1.1 %collective-permute-start.9 = (bf16[2,16,384]{2,1,0:T(8,128)(2,1)S(1)}, bf16[2,16,384]{2,1,0:T(8,128)(2,1)S(1)}, u32[]{:S(2)}, u32[]{:S(2)}) collective-permute-start(bf16[2,16,384]{2,1,0:T(8,128)(2,1)S(1)} %pad_maximum_fusion.1), channel_id=1, source_target_pairs={{0,4},{1,3},{2,6},{3,1},{4,0},{5,7},{6,2},{7,5},{8,12},{9,11},{10,... | collective-permute-start | bytes 73736 | tf_op jit(solution)/shard_map/ppermute | solution.py:372
  42.6 2.7 %collective-permute-done.9 = bf16[2,16,384]{2,1,0:T(8,128)(2,1)S(1)} collective-permute-done((bf16[2,16,384]{2,1,0:T(8,128)(2,1)S(1)}, bf16[2,16,384]{2,1,0:T(8,128)(2,1)S(1)}, u32[]{:S(2)}, u32[]{:S(2)}) %collective-permute-start.9) | collective-permute-done | bytes 24608 | tf_op jit(solution)/shard_map/ppermute | solution.py:372
  45.4 1.4 %collective-permute-start.10 = (bf16[4,16,384]{2,1,0:T(8,128)(2,1)S(1)}, bf16[4,16,384]{2,1,0:T(8,128)(2,1)S(1)}, u32[]{:S(2)}, u32[]{:S(2)}) collective-permute-start(bf16[4,16,384]{2,1,0:T(8,128)(2,1)S(1)} %pad_maximum_fusion), channel_id=1, source_target_pairs={{0,2},{1,5},{2,0},{3,7},{4,6},{5,1},{6,4},{7,3},{8,10},{9,13},{10,... | collective-permute-start | bytes 147464 | tf_op jit(solution)/shard_map/ppermute | solution.py:372
  46.7 2.8 %collective-permute-done.10 = bf16[4,16,384]{2,1,0:T(8,128)(2,1)S(1)} collective-permute-done((bf16[4,16,384]{2,1,0:T(8,128)(2,1)S(1)}, bf16[4,16,384]{2,1,0:T(8,128)(2,1)S(1)}, u32[]{:S(2)}, u32[]{:S(2)}) %collective-permute-start.10) | collective-permute-done | bytes 49184 | tf_op jit(solution)/shard_map/ppermute | solution.py:372
  49.5 0.1 collective-permute-start.11
  49.6 1.4 %half_scores.2.refs_0_ = f32[16,8192]{1,0:T(8,128)} custom-call(s32[16]{0:T(128)S(4)} %get-tuple-element.33.listed, bf16[16,512,256]{2,1,0:T(8,128)(2,1)S(1)} %get-tuple-element.22.rows, s32[8192]{0:T(1024)S(1)} %get-tuple-element.23.ids, bf16[8,16,384]{2,1,0:T(8,128)(2,1)S(1)} %constant_dynamic-update-slice_fusion.messages), custom_call_target="tpu_custom_call" | custom-call | tf_op jit(solution)/shard_map/half_scores/pallas_call | solution.py:351
  51.0 0.0 collective-permute-done.11.messages
  51.0 1.4 %half_scores.3 = f32[16,8192]{1,0:T(8,128)} custom-call(s32[16]{0:T(128)S(4)} %get-tuple-element.33.listed, bf16[16,512,256]{2,1,0:T(8,128)(2,1)S(1)} %get-tuple-element.22.rows, s32[8192]{0:T(1024)S(1)} %get-tuple-element.23.ids, bf16[8,16,384]{2,1,0:T(8,128)(2,1)S(1)} %collective-permute-done.11.messages, ...), custom_call_target="tpu_custom_call", output_to_operand_aliasing={{}: (4, {})} | custom-call | tf_op jit(solution)/shard_map/half_scores/pallas_call | solution.py:351
  (8 shorter events, 0.1 us)
Async XLA Ops:
  3.0 1.8 %collective-permute-start = (f32[2,296,128]{2,1,0:T(8,128)S(1)}, f32[2,296,128]{2,1,0:T(8,128)S(1)}, u32[]{:S(2)}, u32[]{:S(2)}) collective-permute-start(f32[2,296,128]{2,1,0:T(8,128)S(1)} %get-tuple-element.26), channel_id=1, source_target_pairs={{0,1},{1,0},{2,3},{3,2},{4,5},{5,4},{6,7},{7,6},{8,9},{9,8},{10,11... | collective-permute-start | bytes 909320 | tf_op jit(solution)/shard_map/ppermute | solution.py:372
  4.6 4.6 %collective-permute-start.1 = (f32[2,296,128]{2,1,0:T(8,128)S(1)}, f32[2,296,128]{2,1,0:T(8,128)S(1)}, u32[]{:S(2)}, u32[]{:S(2)}) collective-permute-start(f32[2,296,128]{2,1,0:T(8,128)S(1)} %get-tuple-element.29), channel_id=1, source_target_pairs={{0,1},{1,0},{2,3},{3,2},{4,5},{5,4},{6,7},{7,6},{8,9},{9,8},{10,11... | collective-permute-start | bytes 909320 | tf_op jit(solution)/shard_map/ppermute | solution.py:372
  4.8 7.8 %collective-permute-start.3 = (f32[2,296,128]{2,1,0:T(8,128)S(1)}, f32[2,296,128]{2,1,0:T(8,128)S(1)}, u32[]{:S(2)}, u32[]{:S(2)}) collective-permute-start(f32[2,296,128]{2,1,0:T(8,128)S(1)} %add.30), channel_id=1, source_target_pairs={{0,2},{1,5},{2,0},{3,7},{4,6},{5,1},{6,4},{7,3},{8,10},{9,13},{10,... | collective-permute-start | bytes 909320 | tf_op jit(solution)/shard_map/ppermute | solution.py:372
  9.0 3.7 %collective-permute-start.2 = (f32[2,296,128]{2,1,0:T(8,128)S(1)}, f32[2,296,128]{2,1,0:T(8,128)S(1)}, u32[]{:S(2)}, u32[]{:S(2)}) collective-permute-start(f32[2,296,128]{2,1,0:T(8,128)S(1)} %get-tuple-element.31), channel_id=1, source_target_pairs={{0,1},{1,0},{2,3},{3,2},{4,5},{5,4},{6,7},{7,6},{8,9},{9,8},{10,11... | collective-permute-start | bytes 909320 | tf_op jit(solution)/shard_map/ppermute | solution.py:372
  9.3 7.7 %collective-permute-start.5 = (f32[2,296,128]{2,1,0:T(8,128)S(1)}, f32[2,296,128]{2,1,0:T(8,128)S(1)}, u32[]{:S(2)}, u32[]{:S(2)}) collective-permute-start(f32[2,296,128]{2,1,0:T(8,128)S(1)} %add.31), channel_id=1, source_target_pairs={{0,2},{1,5},{2,0},{3,7},{4,6},{5,1},{6,4},{7,3},{8,10},{9,13},{10,... | collective-permute-start | bytes 909320 | tf_op jit(solution)/shard_map/ppermute | solution.py:372
  12.7 7.3 %collective-permute-start.6 = (f32[2,296,128]{2,1,0:T(8,128)S(1)}, f32[2,296,128]{2,1,0:T(8,128)S(1)}, u32[]{:S(2)}, u32[]{:S(2)}) collective-permute-start(f32[2,296,128]{2,1,0:T(8,128)S(1)} %add_add_fusion), channel_id=1, source_target_pairs={{0,4},{1,3},{2,6},{3,1},{4,0},{5,7},{6,2},{7,5},{8,12},{9,11},{10,... | collective-permute-start | bytes 909320 | tf_op jit(solution)/shard_map/ppermute | solution.py:372
  16.3 3.7 %collective-permute-start.4 = (f32[2,296,128]{2,1,0:T(8,128)S(1)}, f32[2,296,128]{2,1,0:T(8,128)S(1)}, u32[]{:S(2)}, u32[]{:S(2)}) collective-permute-start(f32[2,296,128]{2,1,0:T(8,128)S(1)} %get-tuple-element.35), channel_id=1, source_target_pairs={{0,1},{1,0},{2,3},{3,2},{4,5},{5,4},{6,7},{7,6},{8,9},{9,8},{10,11... | collective-permute-start | bytes 909320 | tf_op jit(solution)/shard_map/ppermute | solution.py:372
  20.1 10.0 %collective-permute-start.7 = (f32[1,296,128]{2,1,0:T(8,128)S(1)}, f32[1,296,128]{2,1,0:T(8,128)S(1)}, u32[]{:S(2)}, u32[]{:S(2)}) collective-permute-start(f32[1,296,128]{2,1,0:T(8,128)S(1)} %get-tuple-element.40), channel_id=1, source_target_pairs={{0,8},{1,9},{2,10},{3,11},{4,12},{5,13},{6,14},{7,15},{8,0},{9,1},... | collective-permute-start | bytes 454664 | tf_op jit(solution)/shard_map/ppermute | solution.py:372
  36.8 4.7 %collective-permute-start.8 = (bf16[1,16,384]{2,1,0:T(8,128)(2,1)S(1)}, bf16[1,16,384]{2,1,0:T(8,128)(2,1)S(1)}, u32[]{:S(2)}, u32[]{:S(2)}) collective-permute-start(bf16[1,16,384]{2,1,0:T(8,128)(2,1)S(1)} %get-tuple-element.39), channel_id=1, source_target_pairs={{0,8},{1,9},{2,10},{3,11},{4,12},{5,13},{6,14},{7,15},{8,0},{9,1},... | collective-permute-start | bytes 36872 | tf_op jit(solution)/shard_map/ppermute | solution.py:372
  41.5 3.8 %collective-permute-start.9 = (bf16[2,16,384]{2,1,0:T(8,128)(2,1)S(1)}, bf16[2,16,384]{2,1,0:T(8,128)(2,1)S(1)}, u32[]{:S(2)}, u32[]{:S(2)}) collective-permute-start(bf16[2,16,384]{2,1,0:T(8,128)(2,1)S(1)} %pad_maximum_fusion.1), channel_id=1, source_target_pairs={{0,4},{1,3},{2,6},{3,1},{4,0},{5,7},{6,2},{7,5},{8,12},{9,11},{10,... | collective-permute-start | bytes 73736 | tf_op jit(solution)/shard_map/ppermute | solution.py:372
  45.4 4.2 %collective-permute-start.10 = (bf16[4,16,384]{2,1,0:T(8,128)(2,1)S(1)}, bf16[4,16,384]{2,1,0:T(8,128)(2,1)S(1)}, u32[]{:S(2)}, u32[]{:S(2)}) collective-permute-start(bf16[4,16,384]{2,1,0:T(8,128)(2,1)S(1)} %pad_maximum_fusion), channel_id=1, source_target_pairs={{0,2},{1,5},{2,0},{3,7},{4,6},{5,1},{6,4},{7,3},{8,10},{9,13},{10,... | collective-permute-start | bytes 147464 | tf_op jit(solution)/shard_map/ppermute | solution.py:372
  49.5 1.4 %collective-permute-start.11 = (bf16[8,16,384]{2,1,0:T(8,128)(2,1)S(1)}, bf16[8,16,384]{2,1,0:T(8,128)(2,1)S(1)}, u32[]{:S(2)}, u32[]{:S(2)}) collective-permute-start(bf16[8,16,384]{2,1,0:T(8,128)(2,1)S(1)} %constant_dynamic-update-slice_fusion.messages), channel_id=1, source_target_pairs={{0,1},{1,0},{2,3},{3,2},{4,5},{5,4},{6,7},{7,6},{8,9},{9,8},{10,11... | collective-permute-start | bytes 294920 | tf_op jit(solution)/shard_map/ppermute | solution.py:372
